TPU v7x, 32 devices: a whole 2x2x4 slice. The times are simulated.
32 devices in a mesh: group: 2 (over x), shard: 16 (over z, y, core).
Axes of the slice: x: 2, y: 2, z: 4, core: 2. Of those that a mesh axis runs over, the one named last changes fastest.
Arguments:
- coords: float32 [2, 4096], P(None, ('group', 'shard')), may hold values from 0 to 3
- probes: float32 [256, 4096], P(None, ('group', 'shard')), may hold values from -6 to 6
- neighbours: int32 [64, 8], P(('group', 'shard')), may hold values from -1 to 62, as said below
Outputs:
- precision_probe: float32 [256, 4096], P(None, ('group', 'shard'))
- cond_logvar: float32 [64], P(('group', 'shard'))
Inputs may be any that keep to these rules, and one draw needn't show every extreme that they name: neighbours[b] lists 8 different blocks earlier than b, the first one b - 1; every listed block lies on the device of block b (device b // 2 in the order of group+shard) or on one of the 15 devices before it; -1 stands for a missing block, only where fewer earlier blocks exist in that reach.
All inputs are finite; a program needn't handle non-finite values.
Results may differ from a plain program's by a relative error of at most 0.0003.
Values sent between devices are 32-bit elements; how exact they have to be, the bound alone decides.
No kernel may reach another device: no remote copies, remote signals or barrier semaphores. Data moves between devices by JAX's collectives and lax.ppermute only.
A program may use at most 64 MiB of HBM per device.

v0:
```python
import functools

import jax
import jax.numpy as jnp
from jax import lax
from jax.experimental import pallas as pl
from jax.experimental.pallas import tpu as pltpu
from jax.sharding import PartitionSpec as P

PTS = 64
NEIGH = 8
SPAN = 16
BLK = 2
CORES = 2
WIDE = 128
SQRT_THREE = 1.7320508075688772
NUGGET = 0.25
AXES = ("group", "shard")
CHIPS_BACK = SPAN // CORES
CHIP_PTS = CORES * BLK * PTS
COND = NEIGH * PTS
STEPS = COND // WIDE
HIGHEST = lax.Precision.HIGHEST
F32 = jnp.float32


def dot(a, b, dims=((1,), (0,))):
    return lax.dot_general(a, b, (dims, ((), ())), precision=HIGHEST, preferred_element_type=F32)


def iota(shape, dim):
    return lax.broadcasted_iota(jnp.int32, shape, dim)


def eye(n):
    return (iota((n, n), 0) == iota((n, n), 1)).astype(F32)


def schedule(low, high):
    rho = (high - low) / (high + low)
    factors = []
    while rho > 3e-4:
        factors.append(2.0 / (2.0 - rho * rho))
        rho = rho * rho / (2.0 - rho * rho)
    return 2.0 / (low + high), factors


def inverses(mats):
    n = mats[0].shape[0]
    alpha, factors = schedule(0.245, n + 0.26)
    ident = eye(n)
    rs = [ident - alpha * m for m in mats]
    c = factors[0]
    xs = [(alpha * c) * (ident + r) for r in rs]
    rs = [(1.0 - c) * ident + c * dot(r, r) for r in rs]
    for c in factors[1:-1]:
        nxt = [c * (x + dot(x, r)) for x, r in zip(xs, rs)]
        rs = [(1.0 - c) * ident + c * dot(r, r) for r in rs]
        xs = nxt
    c = factors[-1]
    xs = [c * (x + dot(x, r)) for x, r in zip(xs, rs)]
    es = [ident - dot(m, x) for m, x in zip(mats, xs)]
    return [x + dot(x, e) for x, e in zip(xs, es)]


def kernel_value(dx, dy):
    s = SQRT_THREE * jnp.sqrt(dx * dx + dy * dy)
    return (1.0 + s) * jnp.exp(-s)


def factor_kernel(where_ref, nb_ref, coords_ref, g_ref, s_ref):
    me = where_ref[0]
    lane = iota((1, WIDE), 1)
    low = lane < PTS

    def half_row(dev, half, coord, to_low):
        row = coords_ref[dev, pl.ds(coord, 1), :]
        swapped = pltpu.roll(row, PTS, 1)
        take = half if to_low else 1 - half
        return jnp.where(take == 1, swapped, row)

    def column(row):
        return jnp.transpose(jnp.broadcast_to(row, (WIDE, WIDE)))

    mats = []
    for b in range(BLK):
        rows, valid = [], []
        for k in range(STEPS):
            pieces, oks = [], []
            for h in range(2):
                ident = nb_ref[b, 2 * k + h]
                ok = ident >= 0
                safe = jnp.where(ok, ident, me * BLK)
                dev, half = lax.div(safe, BLK), lax.rem(safe, BLK)
                pieces.append([half_row(dev, half, c, h == 0) for c in range(2)])
                oks.append(jnp.where(ok, 1.0, 0.0).astype(F32))
            rows.append([jnp.where(low, pieces[0][c], pieces[1][c]) for c in range(2)])
            valid.append(jnp.where(low, oks[0], oks[1]))
        own = [half_row(me, b, c, True) for c in range(2)]
        cols = [[column(r) for r in row] for row in rows]
        own_cols = [column(r)[:PTS, :PTS] for r in own]
        valid_cols = [column(v) for v in valid]
        mat = {}
        for i in range(STEPS):
            for j in range(i, STEPS):
                value = kernel_value(cols[i][0] - rows[j][0], cols[i][1] - rows[j][1])
                value = valid_cols[i] * valid[j] * value
                if i == j:
                    value = value + eye(WIDE) * (NUGGET * valid[j] + (1.0 - valid[j]))
                mat[i, j] = value
            value = kernel_value(cols[i][0][:, :PTS] - own[0][:, :PTS], cols[i][1][:, :PTS] - own[1][:, :PTS])
            mat[i, STEPS] = valid_cols[i][:, :PTS] * value
        value = kernel_value(own_cols[0] - own[0][:, :PTS], own_cols[1] - own[1][:, :PTS])
        mat[STEPS, STEPS] = value + NUGGET * eye(PTS)
        mats.append(mat)
    panels = [{} for _ in range(BLK)]
    for k in range(STEPS):
        invs = inverses([m[k, k] for m in mats])
        for j in range(k + 1, STEPS + 1):
            for b in range(BLK):
                panels[b][k, j] = dot(invs[b], mats[b][k, j])
        for i in range(k + 1, STEPS + 1):
            for j in range(i, STEPS + 1):
                for b in range(BLK):
                    mats[b][i, j] = mats[b][i, j] - dot(mats[b][k, i], panels[b][k, j], ((0,), (0,)))
    solved = [{} for _ in range(BLK)]
    for k in reversed(range(STEPS)):
        for b in range(BLK):
            total = panels[b][k, STEPS]
            for j in range(k + 1, STEPS):
                total = total - dot(panels[b][k, j], solved[b][j])
            solved[b][k] = total
    schur = [m[STEPS, STEPS] for m in mats]
    schur_inv = inverses(schur)
    for k in range(STEPS):
        g_ref[k * WIDE : (k + 1) * WIDE, :] = -jnp.concatenate([s[k] for s in solved], axis=1)
    g_ref[COND : COND + PTS, :] = jnp.concatenate(schur_inv, axis=1)
    s_ref[...] = jnp.concatenate(schur, axis=1)


def apply_kernel(where_ref, nb_ref, other_ref, g_ref, h_ref, window_ref, *rest):
    outs, dense = rest[:-1], rest[-1]
    me = where_ref[0]
    chip = lax.div(me, CORES)
    dense[...] = jnp.zeros_like(dense)
    for side, (ids, src) in enumerate(((nb_ref, g_ref), (other_ref, h_ref))):
        core = lax.rem(me, CORES)
        core = core if side == 0 else 1 - core
        for b in range(BLK):
            from_lanes = slice(b * PTS, (b + 1) * PTS)
            lanes = slice((side * BLK + b) * PTS, (side * BLK + b + 1) * PTS)
            for m in range(NEIGH):
                ident = ids[b, m]

                @pl.when(ident >= 0)
                def _():
                    dev = lax.div(ident, BLK)
                    back = chip - lax.div(dev, CORES)
                    inside = lax.rem(ident, CORES * BLK)
                    row = pl.multiple_of(back * CHIP_PTS + inside * PTS, PTS)
                    dense[pl.ds(row, PTS), lanes] = src[m * PTS : (m + 1) * PTS, from_lanes]

            row = pl.multiple_of((core * BLK + b) * PTS, PTS)
            dense[pl.ds(row, PTS), lanes] = eye(PTS)
    total = None
    for o in range(CHIPS_BACK + 1):
        part = dot(window_ref[o], dense[o * CHIP_PTS : (o + 1) * CHIP_PTS, :])
        total = part if total is None else total + part
    pieces = []
    for side, src in enumerate((g_ref, h_ref)):
        for b in range(BLK):
            q = side * BLK + b
            pieces.append(dot(total[:, q * PTS : (q + 1) * PTS], src[COND : COND + PTS, b * PTS : (b + 1) * PTS]))
    scaled = jnp.concatenate(pieces, axis=1)
    for o in range(CHIPS_BACK + 1):
        outs[o][...] = dot(scaled, dense[o * CHIP_PTS : (o + 1) * CHIP_PTS, :], ((1,), (1,)))


def logdet_kernel(s_ref, out_ref, work):
    work[...] = s_ref[...]
    rows = iota((PTS, WIDE), 0)
    lanes = iota((PTS, WIDE), 1)

    def step(k, total):
        mat = work[...]
        row = work[pl.ds(k, 1), :]
        first = jnp.sum(jnp.where(lanes == k, mat, 0.0), axis=1, keepdims=True)
        second = jnp.sum(jnp.where(lanes == k + PTS, mat, 0.0), axis=1, keepdims=True)
        col = jnp.where(lanes < PTS, first, second)
        pivot = jnp.sum(jnp.where(rows == k, col, 0.0), axis=0, keepdims=True)
        work[...] = mat - col * (row / pivot)
        return total + jnp.log(pivot)

    total = lax.fori_loop(0, PTS, step, jnp.zeros((1, WIDE), F32))
    out_ref[...] = jnp.broadcast_to(total * (1.0 / PTS), out_ref.shape)


def passed(value, by):
    size = lax.axis_size(AXES)
    return lax.ppermute(value, AXES, [(i, i + by) for i in range(size) if 0 <= i + by < size])


def swapped(value):
    size = lax.axis_size(AXES)
    return lax.ppermute(value, AXES, [(i, i ^ 1) for i in range(size)])


def shards(coords, probes, neighbours):
    count = lax.axis_size(AXES)
    half = probes.shape[0] // CORES
    device = lax.axis_index(AXES)
    core = device % CORES
    here = jnp.reshape(device, (1,)).astype(jnp.int32)
    smem = pl.BlockSpec(memory_space=pltpu.SMEM)
    vmem = pl.BlockSpec(memory_space=pltpu.VMEM)

    everywhere = lax.all_to_all(
        jnp.broadcast_to(jnp.pad(coords, ((0, 6), (0, 0)))[None], (count, 8, WIDE)), AXES, 0, 0
    )
    other_neighbours = swapped(neighbours)
    kept = lax.dynamic_slice_in_dim(probes, core * half, half, 0)
    given = swapped(lax.dynamic_slice_in_dim(probes, (1 - core) * half, half, 0))
    chip_probes = jnp.where(
        core == 0, jnp.concatenate([kept, given], axis=1), jnp.concatenate([given, kept], axis=1)
    )
    window = jnp.stack([chip_probes] + [passed(chip_probes, CORES * o) for o in range(1, CHIPS_BACK + 1)])

    g, schur = pl.pallas_call(
        factor_kernel,
        out_shape=(
            jax.ShapeDtypeStruct((COND + PTS, WIDE), F32),
            jax.ShapeDtypeStruct((PTS, WIDE), F32),
        ),
        in_specs=[smem, smem, vmem],
        out_specs=(vmem, vmem),
        compiler_params=pltpu.CompilerParams(vmem_limit_bytes=32 * 2**20),
        cost_estimate=pl.CostEstimate(flops=10**9, bytes_accessed=10**6, transcendentals=10**6),
        name="factor",
    )(here, neighbours, everywhere)
    h = swapped(g)
    tile = jax.ShapeDtypeStruct((half, CHIP_PTS), F32)
    terms = pl.pallas_call(
        apply_kernel,
        out_shape=(tile,) * (CHIPS_BACK + 1),
        in_specs=[smem, smem, smem, vmem, vmem, vmem],
        out_specs=(vmem,) * (CHIPS_BACK + 1),
        scratch_shapes=[pltpu.VMEM(((CHIPS_BACK + 1) * CHIP_PTS, CORES * BLK * PTS), F32)],
        compiler_params=pltpu.CompilerParams(vmem_limit_bytes=32 * 2**20),
        cost_estimate=pl.CostEstimate(flops=10**9, bytes_accessed=10**6, transcendentals=0),
        name="apply",
    )(here, neighbours, other_neighbours, g, h, window)
    logs = pl.pallas_call(
        logdet_kernel,
        out_shape=jax.ShapeDtypeStruct((8, WIDE), F32),
        in_specs=[vmem],
        out_specs=vmem,
        scratch_shapes=[pltpu.VMEM((PTS, WIDE), F32)],
        cost_estimate=pl.CostEstimate(flops=10**7, bytes_accessed=10**6, transcendentals=0),
        name="logdet",
    )(schur)
    total = terms[0]
    for o in range(1, CHIPS_BACK + 1):
        total = total + passed(terms[o], -CORES * o)
    width = BLK * PTS
    mine = lax.dynamic_slice_in_dim(total, core * width, width, 1)
    theirs = swapped(lax.dynamic_slice_in_dim(total, (1 - core) * width, width, 1))
    result = jnp.where(
        core == 0, jnp.concatenate([mine, theirs], axis=0), jnp.concatenate([theirs, mine], axis=0)
    )
    return result, logs[0, :: PTS]


def solution(mesh):
    return jax.shard_map(
        shards,
        mesh=mesh,
        in_specs=(P(None, AXES), P(None, AXES), P(AXES, None)),
        out_specs=(P(None, AXES), P(AXES)),
        check_vma=False,
    )
```

profile of v0, /device:TPU:3, one launch (start us, length us, event | category | flops | bytes accessed | tf_op | source)
XLA Modules:
  0.0 115.0 jit_solution(6896747791200823752)
XLA Ops:
  0.7 0.9 constant_dynamic-slice_fusion.3
  1.5 0.7 collective-permute-start.2
  2.3 0.9 collective-permute-done.2
  3.2 0.0 copy-start
  3.2 3.1 %collective-permute-start.3 = (f32[128,256]{1,0:T(8,128)S(1)}, f32[128,256]{1,0:T(8,128)S(1)}, u32[]{:S(2)}, u32[]{:S(2)}) collective-permute-start(f32[128,256]{1,0:T(8,128)S(1)} %maximum_select_fusion.1), channel_id=1, source_target_pairs={{0,2},{1,3},{2,4},{3,5},{4,6},{5,7},{6,8},{7,9},{8,10},{9,11},{10,... | collective-permute-start | bytes 393224 | tf_op jit(solution)/shard_map/ppermute | solution.py:200
  6.4 0.7 pad.4
  7.1 0.7 broadcast_in_dim.2
  7.7 5.4 %all-to-all-start = ((f32[32,8,128]{2,1,0:T(8,128)}), f32[32,8,128]{2,1,0:T(8,128)S(1)}, u32[]{:S(2)}, u32[]{:S(2)}) async-start(f32[32,8,128]{2,1,0:T(8,128)} %broadcast_in_dim.2), calls=%async_computation | async-start | bytes 262144 | tf_op jit(solution)/shard_map/all_to_all | solution.py:217
  13.2 0.4 collective-permute-start
  13.6 3.1 %collective-permute-start.4 = (f32[128,256]{1,0:T(8,128)S(1)}, f32[128,256]{1,0:T(8,128)S(1)}, u32[]{:S(2)}, u32[]{:S(2)}) collective-permute-start(f32[128,256]{1,0:T(8,128)S(1)} %maximum_select_fusion.1), channel_id=1, source_target_pairs={{0,4},{1,5},{2,6},{3,7},{4,8},{5,9},{6,10},{7,11},{8,12},{9,13},{1... | collective-permute-start | bytes 393224 | tf_op jit(solution)/shard_map/ppermute | solution.py:200
  16.7 4.0 %collective-permute-start.5 = (f32[128,256]{1,0:T(8,128)S(1)}, f32[128,256]{1,0:T(8,128)S(1)}, u32[]{:S(2)}, u32[]{:S(2)}) collective-permute-start(f32[128,256]{1,0:T(8,128)S(1)} %maximum_select_fusion.1), channel_id=1, source_target_pairs={{0,6},{1,7},{2,8},{3,9},{4,10},{5,11},{6,12},{7,13},{8,14},{9,15},... | collective-permute-start | bytes 393224 | tf_op jit(solution)/shard_map/ppermute | solution.py:200
  20.7 2.3 %collective-permute-start.6 = (f32[128,256]{1,0:T(8,128)S(1)}, f32[128,256]{1,0:T(8,128)S(1)}, u32[]{:S(2)}, u32[]{:S(2)}) collective-permute-start(f32[128,256]{1,0:T(8,128)S(1)} %maximum_select_fusion.1), channel_id=1, source_target_pairs={{0,8},{1,9},{2,10},{3,11},{4,12},{5,13},{6,14},{7,15},{8,16},{9,17... | collective-permute-start | bytes 393224 | tf_op jit(solution)/shard_map/ppermute | solution.py:200
  23.0 0.0 collective-permute-done.3
  23.0 1.9 %collective-permute-start.7 = (f32[128,256]{1,0:T(8,128)S(1)}, f32[128,256]{1,0:T(8,128)S(1)}, u32[]{:S(2)}, u32[]{:S(2)}) collective-permute-start(f32[128,256]{1,0:T(8,128)S(1)} %maximum_select_fusion.1), channel_id=1, source_target_pairs={{0,10},{1,11},{2,12},{3,13},{4,14},{5,15},{6,16},{7,17},{8,18},{9,... | collective-permute-start | bytes 393224 | tf_op jit(solution)/shard_map/ppermute | solution.py:200
  25.0 0.0 collective-permute-done.4
  25.0 1.9 %collective-permute-start.8 = (f32[128,256]{1,0:T(8,128)S(1)}, f32[128,256]{1,0:T(8,128)S(1)}, u32[]{:S(2)}, u32[]{:S(2)}) collective-permute-start(f32[128,256]{1,0:T(8,128)S(1)} %maximum_select_fusion.1), channel_id=1, source_target_pairs={{0,12},{1,13},{2,14},{3,15},{4,16},{5,17},{6,18},{7,19},{8,20},{9,... | collective-permute-start | bytes 393224 | tf_op jit(solution)/shard_map/ppermute | solution.py:200
  26.9 5.8 %collective-permute-done.5 = f32[128,256]{1,0:T(8,128)S(1)} collective-permute-done((f32[128,256]{1,0:T(8,128)S(1)}, f32[128,256]{1,0:T(8,128)S(1)}, u32[]{:S(2)}, u32[]{:S(2)}) %collective-permute-start.5) | collective-permute-done | bytes 131104 | tf_op jit(solution)/shard_map/ppermute | solution.py:200
  32.8 1.9 %collective-permute-start.9 = (f32[128,256]{1,0:T(8,128)S(1)}, f32[128,256]{1,0:T(8,128)S(1)}, u32[]{:S(2)}, u32[]{:S(2)}) collective-permute-start(f32[128,256]{1,0:T(8,128)S(1)} %maximum_select_fusion.1), channel_id=1, source_target_pairs={{0,14},{1,15},{2,16},{3,17},{4,18},{5,19},{6,20},{7,21},{8,22},{9,... | collective-permute-start | bytes 393224 | tf_op jit(solution)/shard_map/ppermute | solution.py:200
  34.7 1.1 collective-permute-done.6
  35.8 1.3 %collective-permute-start.10 = (f32[128,256]{1,0:T(8,128)S(1)}, f32[128,256]{1,0:T(8,128)S(1)}, u32[]{:S(2)}, u32[]{:S(2)}) collective-permute-start(f32[128,256]{1,0:T(8,128)S(1)} %maximum_select_fusion.1), channel_id=1, source_target_pairs={{0,16},{1,17},{2,18},{3,19},{4,20},{5,21},{6,22},{7,23},{8,24},{9,... | collective-permute-start | bytes 393224 | tf_op jit(solution)/shard_map/ppermute | solution.py:200
  37.1 0.0 collective-permute-done.7
  37.1 0.0 collective-permute-done.8
  37.1 0.0 all-to-all-done.coords_ref
  37.1 0.0 copy-done
  37.2 17.6 %factor.1 = (f32[576,128]{1,0:T(8,128)S(1)}, f32[64,128]{1,0:T(8,128)S(1)}) custom-call(s32[1]{0:T(128)} %bitcast.where_ref, s32[2,8]{1,0:T(2,128)S(1)} %copy-done, f32[32,8,128]{2,1,0:T(8,128)S(1)} %all-to-all-done.coords_ref), custom_call_target="tpu_custom_call" | custom-call | flops 1000000000 | bytes 1000000 | tf_op jit(solution)/shard_map/factor/pallas_call | solution.py:228
  54.8 0.0 copy-start.1
  54.8 0.6 copy-done.1
  55.4 2.4 %collective-permute-start.1 = (f32[576,128]{1,0:T(8,128)S(1)}, f32[576,128]{1,0:T(8,128)S(1)}, u32[]{:S(2)}, u32[]{:S(2)}) collective-permute-start(f32[576,128]{1,0:T(8,128)S(1)} %get-tuple-element.13.g_ref), channel_id=1, source_target_pairs={{0,1},{1,0},{2,3},{3,2},{4,5},{5,4},{6,7},{7,6},{8,9},{9,8},{10,11... | collective-permute-start | bytes 884744 | tf_op jit(solution)/shard_map/ppermute | solution.py:205
  57.8 0.0 collective-permute-done.9
  57.8 0.0 collective-permute-done.10
  57.8 0.0 collective-permute-done.other_ref
  57.8 1.2 %collective-permute-done.1.h_ref = f32[576,128]{1,0:T(8,128)S(1)} collective-permute-done((f32[576,128]{1,0:T(8,128)S(1)}, f32[576,128]{1,0:T(8,128)S(1)}, u32[]{:S(2)}, u32[]{:S(2)}) %collective-permute-start.1) | collective-permute-done | bytes 294944 | tf_op jit(solution)/shard_map/ppermute | solution.py:205
  59.0 6.8 %apply.1 = (f32[128,256]{1,0:T(8,128)S(1)}, f32[128,256]{1,0:T(8,128)S(1)}, f32[128,256]{1,0:T(8,128)S(1)}, f32[128,256]{1,0:T(8,128)S(1)}, f32[128,256]{1,0:T(8...) custom-call(s32[1]{0:T(128)} %bitcast.where_ref, ...), custom_call_target="tpu_custom_call" | custom-call | flops 1000000000 | bytes 1000000 | tf_op jit(solution)/shard_map/apply/pallas_call | solution.py:242
  65.8 9.8 %collective-permute-start.11 = (f32[128,256]{1,0:T(8,128)S(1)}, f32[128,256]{1,0:T(8,128)S(1)}, u32[]{:S(2)}, u32[]{:S(2)}) collective-permute-start(f32[128,256]{1,0:T(8,128)S(1)} %get-tuple-element.15), channel_id=1, source_target_pairs={{2,0},{3,1},{4,2},{5,3},{6,4},{7,5},{8,6},{9,7},{10,8},{11,9},{12,... | collective-permute-start | bytes 393224 | tf_op jit(solution)/shard_map/ppermute | solution.py:200
  75.5 1.9 %collective-permute-start.12 = (f32[128,256]{1,0:T(8,128)S(1)}, f32[128,256]{1,0:T(8,128)S(1)}, u32[]{:S(2)}, u32[]{:S(2)}) collective-permute-start(f32[128,256]{1,0:T(8,128)S(1)} %get-tuple-element.16), channel_id=1, source_target_pairs={{4,0},{5,1},{6,2},{7,3},{8,4},{9,5},{10,6},{11,7},{12,8},{13,9},{1... | collective-permute-start | bytes 393224 | tf_op jit(solution)/shard_map/ppermute | solution.py:200
  77.5 1.9 %collective-permute-start.13 = (f32[128,256]{1,0:T(8,128)S(1)}, f32[128,256]{1,0:T(8,128)S(1)}, u32[]{:S(2)}, u32[]{:S(2)}) collective-permute-start(f32[128,256]{1,0:T(8,128)S(1)} %get-tuple-element.17), channel_id=1, source_target_pairs={{6,0},{7,1},{8,2},{9,3},{10,4},{11,5},{12,6},{13,7},{14,8},{15,9},... | collective-permute-start | bytes 393224 | tf_op jit(solution)/shard_map/ppermute | solution.py:200
  79.4 1.9 %collective-permute-start.14 = (f32[128,256]{1,0:T(8,128)S(1)}, f32[128,256]{1,0:T(8,128)S(1)}, u32[]{:S(2)}, u32[]{:S(2)}) collective-permute-start(f32[128,256]{1,0:T(8,128)S(1)} %get-tuple-element.18), channel_id=1, source_target_pairs={{8,0},{9,1},{10,2},{11,3},{12,4},{13,5},{14,6},{15,7},{16,8},{17,9... | collective-permute-start | bytes 393224 | tf_op jit(solution)/shard_map/ppermute | solution.py:200
  81.3 1.9 %collective-permute-start.15 = (f32[128,256]{1,0:T(8,128)S(1)}, f32[128,256]{1,0:T(8,128)S(1)}, u32[]{:S(2)}, u32[]{:S(2)}) collective-permute-start(f32[128,256]{1,0:T(8,128)S(1)} %get-tuple-element.19), channel_id=1, source_target_pairs={{10,0},{11,1},{12,2},{13,3},{14,4},{15,5},{16,6},{17,7},{18,8},{19... | collective-permute-start | bytes 393224 | tf_op jit(solution)/shard_map/ppermute | solution.py:200
  83.3 0.0 collective-permute-done.11
  83.3 1.9 %collective-permute-start.16 = (f32[128,256]{1,0:T(8,128)S(1)}, f32[128,256]{1,0:T(8,128)S(1)}, u32[]{:S(2)}, u32[]{:S(2)}) collective-permute-start(f32[128,256]{1,0:T(8,128)S(1)} %get-tuple-element.20), channel_id=1, source_target_pairs={{12,0},{13,1},{14,2},{15,3},{16,4},{17,5},{18,6},{19,7},{20,8},{21... | collective-permute-start | bytes 393224 | tf_op jit(solution)/shard_map/ppermute | solution.py:200
  85.2 0.0 collective-permute-done.12
  85.2 1.9 %collective-permute-start.17 = (f32[128,256]{1,0:T(8,128)S(1)}, f32[128,256]{1,0:T(8,128)S(1)}, u32[]{:S(2)}, u32[]{:S(2)}) collective-permute-start(f32[128,256]{1,0:T(8,128)S(1)} %get-tuple-element.21), channel_id=1, source_target_pairs={{14,0},{15,1},{16,2},{17,3},{18,4},{19,5},{20,6},{21,7},{22,8},{23... | collective-permute-start | bytes 393224 | tf_op jit(solution)/shard_map/ppermute | solution.py:200
  87.1 0.0 collective-permute-done.13
  87.1 1.3 %collective-permute-start.18 = (f32[128,256]{1,0:T(8,128)S(1)}, f32[128,256]{1,0:T(8,128)S(1)}, u32[]{:S(2)}, u32[]{:S(2)}) collective-permute-start(f32[128,256]{1,0:T(8,128)S(1)} %get-tuple-element.22), channel_id=1, source_target_pairs={{16,0},{17,1},{18,2},{19,3},{20,4},{21,5},{22,6},{23,7},{24,8},{25... | collective-permute-start | bytes 393224 | tf_op jit(solution)/shard_map/ppermute | solution.py:200
  88.5 7.5 %collective-permute-done.14 = f32[128,256]{1,0:T(8,128)S(1)} collective-permute-done((f32[128,256]{1,0:T(8,128)S(1)}, f32[128,256]{1,0:T(8,128)S(1)}, u32[]{:S(2)}, u32[]{:S(2)}) %collective-permute-start.14) | collective-permute-done | bytes 131104 | tf_op jit(solution)/shard_map/ppermute | solution.py:200
  95.9 6.1 %collective-permute-done.15 = f32[128,256]{1,0:T(8,128)S(1)} collective-permute-done((f32[128,256]{1,0:T(8,128)S(1)}, f32[128,256]{1,0:T(8,128)S(1)}, u32[]{:S(2)}, u32[]{:S(2)}) %collective-permute-start.15) | collective-permute-done | bytes 131104 | tf_op jit(solution)/shard_map/ppermute | solution.py:200
  102.1 0.0 collective-permute-done.16
  102.1 0.0 collective-permute-done.17
  102.1 0.0 collective-permute-done.18
  102.1 0.1 add_add_fusion
  102.2 2.2 %collective-permute-start.19 = (f32[128,128]{1,0:T(8,128)S(1)}, f32[128,128]{1,0:T(8,128)S(1)}, u32[]{:S(2)}, u32[]{:S(2)}) collective-permute-start(f32[128,128]{1,0:T(8,128)S(1)} %get-tuple-element.25), channel_id=1, source_target_pairs={{0,1},{1,0},{2,3},{3,2},{4,5},{5,4},{6,7},{7,6},{8,9},{9,8},{10,11... | collective-permute-start | bytes 196616 | tf_op jit(solution)/shard_map/ppermute | solution.py:205
  104.4 8.7 %logdet.1 = f32[8,128]{1,0:T(8,128)} custom-call(f32[64,128]{1,0:T(8,128)} %copy-done.1), custom_call_target="tpu_custom_call" | custom-call | flops 10000000 | bytes 1000000 | tf_op jit(solution)/shard_map/logdet/pallas_call | solution.py:252
  113.0 1.3 %slice.3 = f32[1,2]{1,0:T(1,128)} slice(f32[8,128]{1,0:T(8,128)} %logdet.1), slice={[0:1:1], [0:128:64]} | slice | bytes 16 | tf_op jit(solution)/shard_map/slice | solution.py:270
  114.3 0.0 collective-permute-done.19
  114.3 0.7 maximum_select_fusion.2
  (11 shorter events, 0.1 us)
Async XLA Ops:
  1.5 1.6 %collective-permute-start.2 = (f32[128,128]{1,0:T(8,128)S(1)}, f32[128,128]{1,0:T(8,128)S(1)}, u32[]{:S(2)}, u32[]{:S(2)}) collective-permute-start(f32[128,128]{1,0:T(8,128)S(1)} %get-tuple-element.27), channel_id=1, source_target_pairs={{0,1},{1,0},{2,3},{3,2},{4,5},{5,4},{6,7},{7,6},{8,9},{9,8},{10,11... | collective-permute-start | bytes 196616 | tf_op jit(solution)/shard_map/ppermute | solution.py:205
  3.2 33.9 %copy-start = (s32[2,8]{1,0:T(2,128)S(1)}, s32[2,8]{1,0:T(2,128)}, u32[]{:S(2)}) copy-start(s32[2,8]{1,0:T(2,128)} %nb_ref.3) | copy-start | bytes 196
  3.2 19.8 %collective-permute-start.3 = (f32[128,256]{1,0:T(8,128)S(1)}, f32[128,256]{1,0:T(8,128)S(1)}, u32[]{:S(2)}, u32[]{:S(2)}) collective-permute-start(f32[128,256]{1,0:T(8,128)S(1)} %maximum_select_fusion.1), channel_id=1, source_target_pairs={{0,2},{1,3},{2,4},{3,5},{4,6},{5,7},{6,8},{7,9},{8,10},{9,11},{10,... | collective-permute-start | bytes 393224 | tf_op jit(solution)/shard_map/ppermute | solution.py:200
  7.7 29.4 %all-to-all-start = ((f32[32,8,128]{2,1,0:T(8,128)}), f32[32,8,128]{2,1,0:T(8,128)S(1)}, u32[]{:S(2)}, u32[]{:S(2)}) async-start(f32[32,8,128]{2,1,0:T(8,128)} %broadcast_in_dim.2), calls=%async_computation | async-start | bytes 262144 | tf_op jit(solution)/shard_map/all_to_all | solution.py:217
  13.2 44.6 %collective-permute-start = (s32[2,8]{1,0:T(2,128)}, s32[2,8]{1,0:T(2,128)S(1)}, u32[]{:S(2)}, u32[]{:S(2)}) collective-permute-start(s32[2,8]{1,0:T(2,128)} %nb_ref.3), channel_id=1, source_target_pairs={{0,1},{1,0},{2,3},{3,2},{4,5},{5,4},{6,7},{7,6},{8,9},{9,8},{10,11... | collective-permute-start | bytes 200 | tf_op jit(solution)/shard_map/ppermute | solution.py:205
  13.6 11.4 %collective-permute-start.4 = (f32[128,256]{1,0:T(8,128)S(1)}, f32[128,256]{1,0:T(8,128)S(1)}, u32[]{:S(2)}, u32[]{:S(2)}) collective-permute-start(f32[128,256]{1,0:T(8,128)S(1)} %maximum_select_fusion.1), channel_id=1, source_target_pairs={{0,4},{1,5},{2,6},{3,7},{4,8},{5,9},{6,10},{7,11},{8,12},{9,13},{1... | collective-permute-start | bytes 393224 | tf_op jit(solution)/shard_map/ppermute | solution.py:200
  16.7 16.1 %collective-permute-start.5 = (f32[128,256]{1,0:T(8,128)S(1)}, f32[128,256]{1,0:T(8,128)S(1)}, u32[]{:S(2)}, u32[]{:S(2)}) collective-permute-start(f32[128,256]{1,0:T(8,128)S(1)} %maximum_select_fusion.1), channel_id=1, source_target_pairs={{0,6},{1,7},{2,8},{3,9},{4,10},{5,11},{6,12},{7,13},{8,14},{9,15},... | collective-permute-start | bytes 393224 | tf_op jit(solution)/shard_map/ppermute | solution.py:200
  20.7 15.0 %collective-permute-start.6 = (f32[128,256]{1,0:T(8,128)S(1)}, f32[128,256]{1,0:T(8,128)S(1)}, u32[]{:S(2)}, u32[]{:S(2)}) collective-permute-start(f32[128,256]{1,0:T(8,128)S(1)} %maximum_select_fusion.1), channel_id=1, source_target_pairs={{0,8},{1,9},{2,10},{3,11},{4,12},{5,13},{6,14},{7,15},{8,16},{9,17... | collective-permute-start | bytes 393224 | tf_op jit(solution)/shard_map/ppermute | solution.py:200
  23.0 14.1 %collective-permute-start.7 = (f32[128,256]{1,0:T(8,128)S(1)}, f32[128,256]{1,0:T(8,128)S(1)}, u32[]{:S(2)}, u32[]{:S(2)}) collective-permute-start(f32[128,256]{1,0:T(8,128)S(1)} %maximum_select_fusion.1), channel_id=1, source_target_pairs={{0,10},{1,11},{2,12},{3,13},{4,14},{5,15},{6,16},{7,17},{8,18},{9,... | collective-permute-start | bytes 393224 | tf_op jit(solution)/shard_map/ppermute | solution.py:200
  25.0 12.1 %collective-permute-start.8 = (f32[128,256]{1,0:T(8,128)S(1)}, f32[128,256]{1,0:T(8,128)S(1)}, u32[]{:S(2)}, u32[]{:S(2)}) collective-permute-start(f32[128,256]{1,0:T(8,128)S(1)} %maximum_select_fusion.1), channel_id=1, source_target_pairs={{0,12},{1,13},{2,14},{3,15},{4,16},{5,17},{6,18},{7,19},{8,20},{9,... | collective-permute-start | bytes 393224 | tf_op jit(solution)/shard_map/ppermute | solution.py:200
  32.8 25.0 %collective-permute-start.9 = (f32[128,256]{1,0:T(8,128)S(1)}, f32[128,256]{1,0:T(8,128)S(1)}, u32[]{:S(2)}, u32[]{:S(2)}) collective-permute-start(f32[128,256]{1,0:T(8,128)S(1)} %maximum_select_fusion.1), channel_id=1, source_target_pairs={{0,14},{1,15},{2,16},{3,17},{4,18},{5,19},{6,20},{7,21},{8,22},{9,... | collective-permute-start | bytes 393224 | tf_op jit(solution)/shard_map/ppermute | solution.py:200
  35.8 22.0 %collective-permute-start.10 = (f32[128,256]{1,0:T(8,128)S(1)}, f32[128,256]{1,0:T(8,128)S(1)}, u32[]{:S(2)}, u32[]{:S(2)}) collective-permute-start(f32[128,256]{1,0:T(8,128)S(1)} %maximum_select_fusion.1), channel_id=1, source_target_pairs={{0,16},{1,17},{2,18},{3,19},{4,20},{5,21},{6,22},{7,23},{8,24},{9,... | collective-permute-start | bytes 393224 | tf_op jit(solution)/shard_map/ppermute | solution.py:200
  54.8 0.6 copy-start.1
  55.4 3.6 %collective-permute-start.1 = (f32[576,128]{1,0:T(8,128)S(1)}, f32[576,128]{1,0:T(8,128)S(1)}, u32[]{:S(2)}, u32[]{:S(2)}) collective-permute-start(f32[576,128]{1,0:T(8,128)S(1)} %get-tuple-element.13.g_ref), channel_id=1, source_target_pairs={{0,1},{1,0},{2,3},{3,2},{4,5},{5,4},{6,7},{7,6},{8,9},{9,8},{10,11... | collective-permute-start | bytes 884744 | tf_op jit(solution)/shard_map/ppermute | solution.py:205
  65.8 17.5 %collective-permute-start.11 = (f32[128,256]{1,0:T(8,128)S(1)}, f32[128,256]{1,0:T(8,128)S(1)}, u32[]{:S(2)}, u32[]{:S(2)}) collective-permute-start(f32[128,256]{1,0:T(8,128)S(1)} %get-tuple-element.15), channel_id=1, source_target_pairs={{2,0},{3,1},{4,2},{5,3},{6,4},{7,5},{8,6},{9,7},{10,8},{11,9},{12,... | collective-permute-start | bytes 393224 | tf_op jit(solution)/shard_map/ppermute | solution.py:200
  75.5 9.7 %collective-permute-start.12 = (f32[128,256]{1,0:T(8,128)S(1)}, f32[128,256]{1,0:T(8,128)S(1)}, u32[]{:S(2)}, u32[]{:S(2)}) collective-permute-start(f32[128,256]{1,0:T(8,128)S(1)} %get-tuple-element.16), channel_id=1, source_target_pairs={{4,0},{5,1},{6,2},{7,3},{8,4},{9,5},{10,6},{11,7},{12,8},{13,9},{1... | collective-permute-start | bytes 393224 | tf_op jit(solution)/shard_map/ppermute | solution.py:200
  77.5 9.7 %collective-permute-start.13 = (f32[128,256]{1,0:T(8,128)S(1)}, f32[128,256]{1,0:T(8,128)S(1)}, u32[]{:S(2)}, u32[]{:S(2)}) collective-permute-start(f32[128,256]{1,0:T(8,128)S(1)} %get-tuple-element.17), channel_id=1, source_target_pairs={{6,0},{7,1},{8,2},{9,3},{10,4},{11,5},{12,6},{13,7},{14,8},{15,9},... | collective-permute-start | bytes 393224 | tf_op jit(solution)/shard_map/ppermute | solution.py:200
  79.4 16.5 %collective-permute-start.14 = (f32[128,256]{1,0:T(8,128)S(1)}, f32[128,256]{1,0:T(8,128)S(1)}, u32[]{:S(2)}, u32[]{:S(2)}) collective-permute-start(f32[128,256]{1,0:T(8,128)S(1)} %get-tuple-element.18), channel_id=1, source_target_pairs={{8,0},{9,1},{10,2},{11,3},{12,4},{13,5},{14,6},{15,7},{16,8},{17,9... | collective-permute-start | bytes 393224 | tf_op jit(solution)/shard_map/ppermute | solution.py:200
  81.3 20.7 %collective-permute-start.15 = (f32[128,256]{1,0:T(8,128)S(1)}, f32[128,256]{1,0:T(8,128)S(1)}, u32[]{:S(2)}, u32[]{:S(2)}) collective-permute-start(f32[128,256]{1,0:T(8,128)S(1)} %get-tuple-element.19), channel_id=1, source_target_pairs={{10,0},{11,1},{12,2},{13,3},{14,4},{15,5},{16,6},{17,7},{18,8},{19... | collective-permute-start | bytes 393224 | tf_op jit(solution)/shard_map/ppermute | solution.py:200
  83.3 18.8 %collective-permute-start.16 = (f32[128,256]{1,0:T(8,128)S(1)}, f32[128,256]{1,0:T(8,128)S(1)}, u32[]{:S(2)}, u32[]{:S(2)}) collective-permute-start(f32[128,256]{1,0:T(8,128)S(1)} %get-tuple-element.20), channel_id=1, source_target_pairs={{12,0},{13,1},{14,2},{15,3},{16,4},{17,5},{18,6},{19,7},{20,8},{21... | collective-permute-start | bytes 393224 | tf_op jit(solution)/shard_map/ppermute | solution.py:200
  85.2 16.9 %collective-permute-start.17 = (f32[128,256]{1,0:T(8,128)S(1)}, f32[128,256]{1,0:T(8,128)S(1)}, u32[]{:S(2)}, u32[]{:S(2)}) collective-permute-start(f32[128,256]{1,0:T(8,128)S(1)} %get-tuple-element.21), channel_id=1, source_target_pairs={{14,0},{15,1},{16,2},{17,3},{18,4},{19,5},{20,6},{21,7},{22,8},{23... | collective-permute-start | bytes 393224 | tf_op jit(solution)/shard_map/ppermute | solution.py:200
  87.1 14.9 %collective-permute-start.18 = (f32[128,256]{1,0:T(8,128)S(1)}, f32[128,256]{1,0:T(8,128)S(1)}, u32[]{:S(2)}, u32[]{:S(2)}) collective-permute-start(f32[128,256]{1,0:T(8,128)S(1)} %get-tuple-element.22), channel_id=1, source_target_pairs={{16,0},{17,1},{18,2},{19,3},{20,4},{21,5},{22,6},{23,7},{24,8},{25... | collective-permute-start | bytes 393224 | tf_op jit(solution)/shard_map/ppermute | solution.py:200
  102.2 12.1 %collective-permute-start.19 = (f32[128,128]{1,0:T(8,128)S(1)}, f32[128,128]{1,0:T(8,128)S(1)}, u32[]{:S(2)}, u32[]{:S(2)}) collective-permute-start(f32[128,128]{1,0:T(8,128)S(1)} %get-tuple-element.25), channel_id=1, source_target_pairs={{0,1},{1,0},{2,3},{3,2},{4,5},{5,4},{6,7},{7,6},{8,9},{9,8},{10,11... | collective-permute-start | bytes 196616 | tf_op jit(solution)/shard_map/ppermute | solution.py:205
where the time goes:
time: 116 us; the launch traced here: 115 us
  starting transfers between devices  53.3 us (46%)
  Pallas kernels  33.1 us (29%)
  waiting for transfers between devices  22.6 us (19%)
  local copies, waits for them, and re-layouts  4.22 us (4%)
    ppermute x16, starting transfers between devices, passed(): lax.ppermute(value, AXES, [(i, i + by) for i in range(size) if 0 <= i + b...  42.1 us
    ppermute x16, waiting for transfers between devices, passed(): lax.ppermute(value, AXES, [(i, i + by) for i in range(size) if 0 <= i + b...  20.5 us
    pallas_call x1, Pallas kernels, shards(): pl.pallas_call(factor_kernel, out_shape=(jax.ShapeDtypeStruct((COND + PTS...  17.6 us
    pallas_call x1, Pallas kernels, shards(): pl.pallas_call(logdet_kernel, out_shape=jax.ShapeDtypeStruct((8, WIDE), F...  8.65 us
    pallas_call x1, Pallas kernels, shards(): pl.pallas_call(apply_kernel, out_shape=(tile,) * (CHIPS_BACK + 1), in_spe...  6.8 us
    ppermute x4, starting transfers between devices, swapped(): return lax.ppermute(value, AXES, [(i, i ^ 1) for i in range(size)])  5.74 us
    all_to_all x1, starting transfers between devices, shards(): lax.all_to_all(jnp.broadcast_to(jnp.pad(coords, ((0, 6), (0, 0)))[None],...  5.44 us
  transfers between devices with their start and end apart: 21, of which 6 were waited for; matrix products, arithmetic and copies ran while one was open for 2% of the time, Pallas kernels for 23%

commit v1 on v0

--- a/solution.py
+++ b/solution.py
@@ -11,13 +11,12 @@
 NEIGH = 8
 SPAN = 16
 BLK = 2
-CORES = 2
 WIDE = 128
 SQRT_THREE = 1.7320508075688772
 NUGGET = 0.25
 AXES = ("group", "shard")
-CHIPS_BACK = SPAN // CORES
-CHIP_PTS = CORES * BLK * PTS
+SLAB = 4
+WINDOW = SPAN // SLAB + 1
 COND = NEIGH * PTS
 STEPS = COND // WIDE
 HIGHEST = lax.Precision.HIGHEST
@@ -131,49 +130,63 @@
                 total = total - dot(panels[b][k, j], solved[b][j])
             solved[b][k] = total
     schur = [m[STEPS, STEPS] for m in mats]
-    schur_inv = inverses(schur)
     for k in range(STEPS):
         g_ref[k * WIDE : (k + 1) * WIDE, :] = -jnp.concatenate([s[k] for s in solved], axis=1)
-    g_ref[COND : COND + PTS, :] = jnp.concatenate(schur_inv, axis=1)
     s_ref[...] = jnp.concatenate(schur, axis=1)
 
 
-def apply_kernel(where_ref, nb_ref, other_ref, g_ref, h_ref, window_ref, *rest):
-    outs, dense = rest[:-1], rest[-1]
+def apply_kernel(where_ref, ids_ref, *rest):
+    windows, w_refs, v_refs, outs = rest[:WINDOW], rest[WINDOW : WINDOW + SLAB], rest[WINDOW + SLAB : WINDOW + 2 * SLAB], rest[WINDOW + 2 * SLAB : -2]
+    held, total = rest[-2], rest[-1]
     me = where_ref[0]
-    chip = lax.div(me, CORES)
-    dense[...] = jnp.zeros_like(dense)
-    for side, (ids, src) in enumerate(((nb_ref, g_ref), (other_ref, h_ref))):
-        core = lax.rem(me, CORES)
-        core = core if side == 0 else 1 - core
+    slab, quarter = lax.div(me, SLAB), lax.rem(me, SLAB)
+    low = iota((PTS, WIDE), 1) < PTS
+    for o in range(WINDOW):
+        held[o * SLAB : (o + 1) * SLAB] = windows[o][...]
+    total[...] = jnp.zeros_like(total)
+
+    for k in range(SLAB):
+        sender = quarter ^ k
+        device = slab * SLAB + sender
+        places = []
         for b in range(BLK):
-            from_lanes = slice(b * PTS, (b + 1) * PTS)
-            lanes = slice((side * BLK + b) * PTS, (side * BLK + b + 1) * PTS)
             for m in range(NEIGH):
-                ident = ids[b, m]
-
-                @pl.when(ident >= 0)
-                def _():
-                    dev = lax.div(ident, BLK)
-                    back = chip - lax.div(dev, CORES)
-                    inside = lax.rem(ident, CORES * BLK)
-                    row = pl.multiple_of(back * CHIP_PTS + inside * PTS, PTS)
-                    dense[pl.ds(row, PTS), lanes] = src[m * PTS : (m + 1) * PTS, from_lanes]
-
-            row = pl.multiple_of((core * BLK + b) * PTS, PTS)
-            dense[pl.ds(row, PTS), lanes] = eye(PTS)
-    total = None
-    for o in range(CHIPS_BACK + 1):
-        part = dot(window_ref[o], dense[o * CHIP_PTS : (o + 1) * CHIP_PTS, :])
-        total = part if total is None else total + part
-    pieces = []
-    for side, src in enumerate((g_ref, h_ref)):
+                ident = ids_ref[sender, b * NEIGH + m]
+                ident = jnp.where(ident >= 0, ident, device * BLK)
+                owner = lax.div(ident, BLK)
+                place = (slab - lax.div(owner, SLAB)) * SLAB + lax.rem(owner, SLAB)
+                turn = (lax.rem(ident, BLK) ^ (m % 2)) * PTS
+                places.append((place, turn))
+        gathered = []
         for b in range(BLK):
-            q = side * BLK + b
-            pieces.append(dot(total[:, q * PTS : (q + 1) * PTS], src[COND : COND + PTS, b * PTS : (b + 1) * PTS]))
-    scaled = jnp.concatenate(pieces, axis=1)
-    for o in range(CHIPS_BACK + 1):
-        outs[o][...] = dot(scaled, dense[o * CHIP_PTS : (o + 1) * CHIP_PTS, :], ((1,), (1,)))
+            pieces = []
+            for m in range(0, NEIGH, 2):
+                (p0, t0), (p1, t1) = places[b * NEIGH + m], places[b * NEIGH + m + 1]
+                first = pltpu.roll(held[p0], t0, 1)
+                second = pltpu.roll(held[p1], t1, 1)
+                pieces.append(jnp.where(low, first, second))
+            gathered.append(jnp.concatenate(pieces, axis=1))
+        w = w_refs[k][...]
+        white = dot(jnp.concatenate(gathered, axis=0), w)
+        white = held[sender] + jnp.where(low, white[:PTS], white[PTS:])
+        v = v_refs[k][...]
+        inv = jnp.concatenate([jnp.where(low, v, 0.0), jnp.where(low, 0.0, v)], axis=0)
+        scaled = dot(white, inv)
+        total[sender] += scaled
+        sides = jnp.concatenate([jnp.where(low, scaled, 0.0), jnp.where(low, 0.0, scaled)], axis=0)
+        back = dot(sides, w, ((1,), (1,)))
+        for b in range(BLK):
+            for m in range(NEIGH):
+                place, turn = places[b * NEIGH + m]
+                tile = back[b * PTS : (b + 1) * PTS, (m // 2) * WIDE : (m // 2 + 1) * WIDE]
+                tile = jnp.where(low, tile, 0.0) if m % 2 == 0 else jnp.where(low, 0.0, tile)
+                total[place] += pltpu.roll(tile, turn, 1)
+    for o in range(WINDOW):
+        outs[o][...] = total[o * SLAB : (o + 1) * SLAB]
+
+
+def invert_kernel(s_ref, v_ref):
+    v_ref[...] = jnp.concatenate(inverses([s_ref[:, b * PTS : (b + 1) * PTS] for b in range(BLK)]), axis=1)
 
 
 def logdet_kernel(s_ref, out_ref, work):
@@ -200,55 +213,66 @@
     return lax.ppermute(value, AXES, [(i, i + by) for i in range(size) if 0 <= i + by < size])
 
 
-def swapped(value):
+def swapped(value, mask):
     size = lax.axis_size(AXES)
-    return lax.ppermute(value, AXES, [(i, i ^ 1) for i in range(size)])
+    return lax.ppermute(value, AXES, [(i, i ^ mask) for i in range(size)])
+
+
+def within_slab(value):
+    groups = [[SLAB * j + i for i in range(SLAB)] for j in range(lax.axis_size(AXES[1]) // SLAB)]
+    return lax.all_to_all(value, AXES[1], 0, 0, axis_index_groups=groups)
 
 
 def shards(coords, probes, neighbours):
     count = lax.axis_size(AXES)
-    half = probes.shape[0] // CORES
+    quarter = probes.shape[0] // SLAB
     device = lax.axis_index(AXES)
-    core = device % CORES
     here = jnp.reshape(device, (1,)).astype(jnp.int32)
     smem = pl.BlockSpec(memory_space=pltpu.SMEM)
     vmem = pl.BlockSpec(memory_space=pltpu.VMEM)
 
-    everywhere = lax.all_to_all(
-        jnp.broadcast_to(jnp.pad(coords, ((0, 6), (0, 0)))[None], (count, 8, WIDE)), AXES, 0, 0
-    )
-    other_neighbours = swapped(neighbours)
-    kept = lax.dynamic_slice_in_dim(probes, core * half, half, 0)
-    given = swapped(lax.dynamic_slice_in_dim(probes, (1 - core) * half, half, 0))
-    chip_probes = jnp.where(
-        core == 0, jnp.concatenate([kept, given], axis=1), jnp.concatenate([given, kept], axis=1)
-    )
-    window = jnp.stack([chip_probes] + [passed(chip_probes, CORES * o) for o in range(1, CHIPS_BACK + 1)])
-
-    g, schur = pl.pallas_call(
+    ids_row = jnp.pad(neighbours.astype(F32).reshape(1, -1), ((0, 0), (0, WIDE - BLK * NEIGH)))
+    told = jnp.pad(jnp.concatenate([coords, ids_row], axis=0), ((0, 5), (0, 0)))
+    everywhere = lax.all_to_all(jnp.broadcast_to(told[None], (count, 8, WIDE)), AXES, 0, 0)
+    ids = lax.dynamic_slice(everywhere, (device // SLAB * SLAB, 2, 0), (SLAB, 1, BLK * NEIGH))
+    ids = ids.reshape(SLAB, BLK * NEIGH).astype(jnp.int32)
+    own = within_slab(probes.reshape(SLAB, quarter, WIDE))
+    window = [own] + [passed(own, SLAB * o) for o in range(1, WINDOW)]
+
+    w, schur = pl.pallas_call(
         factor_kernel,
-        out_shape=(
-            jax.ShapeDtypeStruct((COND + PTS, WIDE), F32),
-            jax.ShapeDtypeStruct((PTS, WIDE), F32),
-        ),
+        out_shape=(jax.ShapeDtypeStruct((COND, WIDE), F32), jax.ShapeDtypeStruct((PTS, WIDE), F32)),
         in_specs=[smem, smem, vmem],
         out_specs=(vmem, vmem),
         compiler_params=pltpu.CompilerParams(vmem_limit_bytes=32 * 2**20),
         cost_estimate=pl.CostEstimate(flops=10**9, bytes_accessed=10**6, transcendentals=10**6),
         name="factor",
     )(here, neighbours, everywhere)
-    h = swapped(g)
-    tile = jax.ShapeDtypeStruct((half, CHIP_PTS), F32)
+    w_y = swapped(w, 2)
+    w_d = swapped(w, 1)
+    v = pl.pallas_call(
+        invert_kernel,
+        out_shape=jax.ShapeDtypeStruct((PTS, WIDE), F32),
+        in_specs=[vmem],
+        out_specs=vmem,
+        cost_estimate=pl.CostEstimate(flops=10**8, bytes_accessed=10**5, transcendentals=0),
+        name="invert",
+    )(schur)
+    v_y = swapped(v, 2)
+    v_d = swapped(v, 1)
+    w_yd = swapped(w_y, 1)
+    v_yd = swapped(v_y, 1)
+    tile = jax.ShapeDtypeStruct((SLAB, quarter, WIDE), F32)
     terms = pl.pallas_call(
         apply_kernel,
-        out_shape=(tile,) * (CHIPS_BACK + 1),
-        in_specs=[smem, smem, smem, vmem, vmem, vmem],
-        out_specs=(vmem,) * (CHIPS_BACK + 1),
-        scratch_shapes=[pltpu.VMEM(((CHIPS_BACK + 1) * CHIP_PTS, CORES * BLK * PTS), F32)],
+        out_shape=(tile,) * WINDOW,
+        in_specs=[smem, smem] + [vmem] * (WINDOW + 2 * SLAB),
+        out_specs=(vmem,) * WINDOW,
+        scratch_shapes=[pltpu.VMEM((WINDOW * SLAB, quarter, WIDE), F32)] * 2,
         compiler_params=pltpu.CompilerParams(vmem_limit_bytes=32 * 2**20),
         cost_estimate=pl.CostEstimate(flops=10**9, bytes_accessed=10**6, transcendentals=0),
         name="apply",
-    )(here, neighbours, other_neighbours, g, h, window)
+    )(here, ids, *window, w, w_d, w_y, w_yd, v, v_d, v_y, v_yd)
     logs = pl.pallas_call(
         logdet_kernel,
         out_shape=jax.ShapeDtypeStruct((8, WIDE), F32),
@@ -258,15 +282,12 @@
         cost_estimate=pl.CostEstimate(flops=10**7, bytes_accessed=10**6, transcendentals=0),
         name="logdet",
     )(schur)
-    total = terms[0]
-    for o in range(1, CHIPS_BACK + 1):
-        total = total + passed(terms[o], -CORES * o)
-    width = BLK * PTS
-    mine = lax.dynamic_slice_in_dim(total, core * width, width, 1)
-    theirs = swapped(lax.dynamic_slice_in_dim(total, (1 - core) * width, width, 1))
-    result = jnp.where(
-        core == 0, jnp.concatenate([mine, theirs], axis=0), jnp.concatenate([theirs, mine], axis=0)
-    )
+    returned = [passed(terms[o], -SLAB * o) for o in range(1, WINDOW)]
+    kept, logs = lax.optimization_barrier((terms[0], logs))
+    total = kept
+    for part in returned:
+        total = total + part
+    result = within_slab(total).reshape(SLAB * quarter, WIDE)
     return result, logs[0, :: PTS]
 
 

time: 116 us -> 94.3 us (0.81)
  starting transfers between devices: 53.3 us -> 30 us
  blocking collectives: 0 us -> 8.82 us
  waiting for transfers between devices: 22.6 us -> 15.9 us
    ppermute x16 -> x8, starting transfers between devices: 42.1 us -> 16.4 us  [passed(): lax.ppermute(value, AXES, [(i, i + by) for i in range(size) if 0 <= i + b...]
    ppermute x16 -> x8, waiting for transfers between devices: 20.5 us -> 6.42 us  [passed(): lax.ppermute(value, AXES, [(i, i + by) for i in range(size) if 0 <= i + b...]
    all_to_all x1 -> x2, waiting for transfers between devices: 0.01 us -> 9.44 us  [the longest x1 7.1 us: shards(): lax.all_to_all(jnp.broadcast_to(told[None], (count, 8, WIDE)), AXES, 0, 0)]
    all_to_all x0 -> x1, blocking collectives: none -> 8.82 us  [within_slab(): return lax.all_to_all(value, AXES[1], 0, 0, axis_index_groups=groups)]
    all_to_all x1 -> x2, starting transfers between devices: 5.44 us -> 11.1 us  [the longest x1 6.44 us: shards(): lax.all_to_all(jnp.broadcast_to(told[None], (count, 8, WIDE)), AXES, 0, 0)]
    ppermute x4 -> x6, starting transfers between devices: 5.74 us -> 2.49 us  [swapped(): return lax.ppermute(value, AXES, [(i, i ^ mask) for i in range(size)])]
    ppermute x4 -> x6, waiting for transfers between devices: 2.06 us -> 0.02 us  [swapped(): return lax.ppermute(value, AXES, [(i, i ^ mask) for i in range(size)])]
    unnamed x11, local copies, waits for them, and re-layouts: 0.7 us -> 1.87 us
  transfers between devices with their start and end apart: 21 -> 16, of which waited for: 6 -> 4; matrix products, arithmetic and copies ran while one was open for 2% -> 1% of each run, Pallas kernels for 23% -> 13%
where the time goes in v1:
time: 94.3 us; the launch traced here: 93 us
  Pallas kernels  32.3 us (34%)
  starting transfers between devices  30 us (32%)
  waiting for transfers between devices  15.9 us (17%)
  blocking collectives  8.82 us (9%)
  local copies, waits for them, and re-layouts  3.89 us (4%)
  other arithmetic  1.39 us (1%)
    ppermute x8, starting transfers between devices, passed(): lax.ppermute(value, AXES, [(i, i + by) for i in range(size) if 0 <= i + b...  16.4 us
    pallas_call x1, Pallas kernels, shards(): pl.pallas_call(factor_kernel, out_shape=(jax.ShapeDtypeStruct((COND, WIDE...  15.9 us
    all_to_all x1, blocking collectives, within_slab(): return lax.all_to_all(value, AXES[1], 0, 0, axis_index_groups=groups)  8.82 us
    pallas_call x1, Pallas kernels, shards(): pl.pallas_call(logdet_kernel, out_shape=jax.ShapeDtypeStruct((8, WIDE), F...  8.66 us
    all_to_all x1, waiting for transfers between devices, shards(): lax.all_to_all(jnp.broadcast_to(told[None], (count, 8, WIDE)), AXES, 0, 0)  7.1 us
    all_to_all x1, starting transfers between devices, shards(): lax.all_to_all(jnp.broadcast_to(told[None], (count, 8, WIDE)), AXES, 0, 0)  6.44 us
    ppermute x8, waiting for transfers between devices, passed(): lax.ppermute(value, AXES, [(i, i + by) for i in range(size) if 0 <= i + b...  6.42 us
    all_to_all x1, starting transfers between devices, within_slab(): return lax.all_to_all(value, AXES[1], 0, 0, axis_index_groups=groups)  4.62 us
  transfers between devices with their start and end apart: 16, of which 4 were waited for; matrix products, arithmetic and copies ran while one was open for 1% of the time, Pallas kernels for 13%

profile of v1, /device:TPU:3, one launch (start us, length us, event | category | flops | bytes accessed | tf_op | source)
XLA Modules:
  0.0 93.0 jit_solution(16156638908261619158)
XLA Ops:
  0.6 0.7 convert_element_type.12
  1.3 0.0 copy-start.4
  1.3 0.1 reshape.20
  1.4 0.6 copy-done.4
  2.0 0.7 broadcast_in_dim.2
  2.7 6.4 %all-to-all-start = ((f32[32,8,128]{2,1,0:T(8,128)}), f32[32,8,128]{2,1,0:T(8,128)S(1)}, u32[]{:S(2)}, u32[]{:S(2)}) async-start(f32[32,8,128]{2,1,0:T(8,128)} %broadcast_in_dim.2), calls=%async_computation | async-start | bytes 262144 | tf_op jit(solution)/shard_map/all_to_all | solution.py:236
  9.1 0.0 copy-start
  9.1 7.1 %all-to-all-done.coords_ref = f32[32,8,128]{2,1,0:T(8,128)S(1)} async-done(((f32[32,8,128]{2,1,0:T(8,128)}), f32[32,8,128]{2,1,0:T(8,128)S(1)}, u32[]{:S(2)}, u32[]{:S(2)}) %all-to-all-start) | async-done | bytes 131104 | tf_op jit(solution)/shard_map/all_to_all | solution.py:236
  16.2 0.0 copy-done
  16.2 0.0 copy-start.3
  16.2 15.9 %factor.1 = (f32[512,128]{1,0:T(8,128)S(1)}, f32[64,128]{1,0:T(8,128)S(1)}) custom-call(s32[1]{0:T(128)} %bitcast.where_ref, s32[2,8]{1,0:T(2,128)S(1)} %copy-done, f32[32,8,128]{2,1,0:T(8,128)S(1)} %all-to-all-done.coords_ref), custom_call_target="tpu_custom_call" | custom-call | flops 1000000000 | bytes 1000000 | tf_op jit(solution)/shard_map/factor/pallas_call | solution.py:242
  32.2 0.0 copy-start.2
  32.2 0.6 copy-done.2
  32.8 0.3 collective-permute-start.5
  33.1 0.0 copy-done.3
  33.1 8.8 %all_to_all.15.rest_0_ = f32[4,64,128]{2,1,0:T(8,128)S(1)} all-to-all(f32[4,64,128]{2,1,0:T(8,128)S(1)} %bitcast.7), channel_id=1, replica_groups={{0,1,2,3},{4,5,6,7},{8,9,10,11},{12,13,14,15},{16,17,18,19},{20,21,22,2..., dimensions={0} | all-to-all | bytes 262144 | tf_op jit(solution)/shard_map/all_to_all | solution.py:223
  41.9 1.3 %collective-permute-start.3 = (f32[4,64,128]{2,1,0:T(8,128)S(1)}, f32[4,64,128]{2,1,0:T(8,128)S(1)}, u32[]{:S(2)}, u32[]{:S(2)}) collective-permute-start(f32[4,64,128]{2,1,0:T(8,128)S(1)} %all_to_all.15.rest_0_), channel_id=1, source_target_pairs={{0,16},{1,17},{2,18},{3,19},{4,20},{5,21},{6,22},{7,23},{8,24},{9,... | collective-permute-start | bytes 393224 | tf_op jit(solution)/shard_map/ppermute | solution.py:213
  43.2 2.8 %collective-permute-start.2 = (f32[4,64,128]{2,1,0:T(8,128)S(1)}, f32[4,64,128]{2,1,0:T(8,128)S(1)}, u32[]{:S(2)}, u32[]{:S(2)}) collective-permute-start(f32[4,64,128]{2,1,0:T(8,128)S(1)} %all_to_all.15.rest_0_), channel_id=1, source_target_pairs={{0,12},{1,13},{2,14},{3,15},{4,16},{5,17},{6,18},{7,19},{8,20},{9,... | collective-permute-start | bytes 393224 | tf_op jit(solution)/shard_map/ppermute | solution.py:213
  46.0 1.4 %collective-permute-start.4 = (f32[512,128]{1,0:T(8,128)S(1)}, f32[512,128]{1,0:T(8,128)S(1)}, u32[]{:S(2)}, u32[]{:S(2)}) collective-permute-start(f32[512,128]{1,0:T(8,128)S(1)} %get-tuple-element.11.rest_5_), channel_id=1, source_target_pairs={{0,1},{1,0},{2,3},{3,2},{4,5},{5,4},{6,7},{7,6},{8,9},{9,8},{10,11... | collective-permute-start | bytes 786440 | tf_op jit(solution)/shard_map/ppermute | solution.py:218
  47.4 0.0 collective-permute-done.5.rest_7_
  47.4 0.1 collective-permute-start.6
  47.5 1.9 %collective-permute-start.1 = (f32[4,64,128]{2,1,0:T(8,128)S(1)}, f32[4,64,128]{2,1,0:T(8,128)S(1)}, u32[]{:S(2)}, u32[]{:S(2)}) collective-permute-start(f32[4,64,128]{2,1,0:T(8,128)S(1)} %all_to_all.15.rest_0_), channel_id=1, source_target_pairs={{0,8},{1,9},{2,10},{3,11},{4,12},{5,13},{6,14},{7,15},{8,16},{9,17... | collective-permute-start | bytes 393224 | tf_op jit(solution)/shard_map/ppermute | solution.py:213
  49.4 3.3 %invert.1.rest_9_ = f32[64,128]{1,0:T(8,128)} custom-call(f32[64,128]{1,0:T(8,128)} %copy-done.2), custom_call_target="tpu_custom_call" | custom-call | flops 100000000 | bytes 100000 | tf_op jit(solution)/shard_map/invert/pallas_call | solution.py:253
  52.7 0.0 copy-start.1
  52.7 0.0 collective-permute-done.3.rest_4_
  52.8 0.2 collective-permute-start.8
  53.0 0.0 collective-permute-done.2.rest_3_
  53.0 1.9 %collective-permute-start = (f32[4,64,128]{2,1,0:T(8,128)S(1)}, f32[4,64,128]{2,1,0:T(8,128)S(1)}, u32[]{:S(2)}, u32[]{:S(2)}) collective-permute-start(f32[4,64,128]{2,1,0:T(8,128)S(1)} %all_to_all.15.rest_0_), channel_id=1, source_target_pairs={{0,4},{1,5},{2,6},{3,7},{4,8},{5,9},{6,10},{7,11},{8,12},{9,13},{1... | collective-permute-start | bytes 393224 | tf_op jit(solution)/shard_map/ppermute | solution.py:213
  54.9 3.1 %collective-permute-done.1.rest_2_ = f32[4,64,128]{2,1,0:T(8,128)S(1)} collective-permute-done((f32[4,64,128]{2,1,0:T(8,128)S(1)}, f32[4,64,128]{2,1,0:T(8,128)S(1)}, u32[]{:S(2)}, u32[]{:S(2)}) %collective-permute-start.1) | collective-permute-done | bytes 131104 | tf_op jit(solution)/shard_map/ppermute | solution.py:213
  58.0 0.0 copy-done.1
  58.0 0.5 collective-permute-start.7
  58.5 0.0 collective-permute-done.8.rest_11_
  58.5 0.1 collective-permute-start.9
  58.5 3.3 %collective-permute-done.rest_1_ = f32[4,64,128]{2,1,0:T(8,128)S(1)} collective-permute-done((f32[4,64,128]{2,1,0:T(8,128)S(1)}, f32[4,64,128]{2,1,0:T(8,128)S(1)}, u32[]{:S(2)}, u32[]{:S(2)}) %collective-permute-start) | collective-permute-done | bytes 131104 | tf_op jit(solution)/shard_map/ppermute | solution.py:213
  61.9 0.0 collective-permute-done.7.rest_10_
  61.9 0.0 collective-permute-done.9.rest_12_
  61.9 0.0 collective-permute-done.4.rest_6_
  61.9 0.0 collective-permute-done.6.rest_8_
  61.9 4.3 %apply.1 = (f32[4,64,128]{2,1,0:T(8,128)S(1)}, f32[4,64,128]{2,1,0:T(8,128)S(1)}, f32[4,64,128]{2,1,0:T(8,128)S(1)}, f32[4,64,128]{2,1,0:T(8,128)S(1)}, f32[4,64,128]{2,1,0:T(8,128)S(1)}) custom-call(s32[1]{0:T(128)} %bitcast.where_ref, s32[4,16]{1,0:T(4,128)S(1)} %bitcast.5, f32[4,64,128]{2,1,0:T(8,128)S(1)} %all_to_all.15.rest_0_, ...), custom_call_target="tpu_custom_call" | custom-call | flops 1000000000 | bytes 1000000 | tf_op jit(solution)/shard_map/apply/pallas_call | solution.py:266
  66.2 3.4 %collective-permute-start.10 = (f32[4,64,128]{2,1,0:T(8,128)S(1)}, f32[4,64,128]{2,1,0:T(8,128)S(1)}, u32[]{:S(2)}, u32[]{:S(2)}) collective-permute-start(f32[4,64,128]{2,1,0:T(8,128)S(1)} %get-tuple-element.15), channel_id=1, source_target_pairs={{4,0},{5,1},{6,2},{7,3},{8,4},{9,5},{10,6},{11,7},{12,8},{13,9},{1... | collective-permute-start | bytes 393224 | tf_op jit(solution)/shard_map/ppermute | solution.py:213
  69.6 1.9 %collective-permute-start.11 = (f32[4,64,128]{2,1,0:T(8,128)S(1)}, f32[4,64,128]{2,1,0:T(8,128)S(1)}, u32[]{:S(2)}, u32[]{:S(2)}) collective-permute-start(f32[4,64,128]{2,1,0:T(8,128)S(1)} %get-tuple-element.16), channel_id=1, source_target_pairs={{8,0},{9,1},{10,2},{11,3},{12,4},{13,5},{14,6},{15,7},{16,8},{17,9... | collective-permute-start | bytes 393224 | tf_op jit(solution)/shard_map/ppermute | solution.py:213
  71.5 1.9 %collective-permute-start.12 = (f32[4,64,128]{2,1,0:T(8,128)S(1)}, f32[4,64,128]{2,1,0:T(8,128)S(1)}, u32[]{:S(2)}, u32[]{:S(2)}) collective-permute-start(f32[4,64,128]{2,1,0:T(8,128)S(1)} %get-tuple-element.17), channel_id=1, source_target_pairs={{12,0},{13,1},{14,2},{15,3},{16,4},{17,5},{18,6},{19,7},{20,8},{21... | collective-permute-start | bytes 393224 | tf_op jit(solution)/shard_map/ppermute | solution.py:213
  73.5 1.3 %collective-permute-start.13 = (f32[4,64,128]{2,1,0:T(8,128)S(1)}, f32[4,64,128]{2,1,0:T(8,128)S(1)}, u32[]{:S(2)}, u32[]{:S(2)}) collective-permute-start(f32[4,64,128]{2,1,0:T(8,128)S(1)} %get-tuple-element.18), channel_id=1, source_target_pairs={{16,0},{17,1},{18,2},{19,3},{20,4},{21,5},{22,6},{23,7},{24,8},{25... | collective-permute-start | bytes 393224 | tf_op jit(solution)/shard_map/ppermute | solution.py:213
  74.8 8.7 %logdet.1 = f32[8,128]{1,0:T(8,128)} custom-call(f32[64,128]{1,0:T(8,128)} %copy-done.2), custom_call_target="tpu_custom_call" | custom-call | flops 10000000 | bytes 1000000 | tf_op jit(solution)/shard_map/logdet/pallas_call | solution.py:276
  83.4 0.0 collective-permute-done.10
  83.4 0.0 collective-permute-done.11
  83.4 0.0 collective-permute-done.12
  83.4 0.0 collective-permute-done.13
  83.4 0.7 add_add_fusion
  84.1 4.6 %all-to-all-start.2 = ((f32[4,64,128]{2,1,0:T(8,128)}), f32[4,64,128]{2,1,0:T(8,128)S(1)}, u32[]{:S(2)}, u32[]{:S(2)}) async-start(f32[4,64,128]{2,1,0:T(8,128)} %add_add_fusion), calls=%async_computation.2 | async-start | bytes 262144 | tf_op jit(solution)/shard_map/all_to_all | solution.py:223
  88.7 1.3 %slice.3 = f32[1,2]{1,0:T(1,128)} slice(f32[8,128]{1,0:T(8,128)} %logdet.1), slice={[0:1:1], [0:128:64]} | slice | bytes 16 | tf_op jit(solution)/shard_map/slice | solution.py:291
  90.0 2.3 %all-to-all-done.2 = f32[4,64,128]{2,1,0:T(8,128)S(1)} async-done(((f32[4,64,128]{2,1,0:T(8,128)}), f32[4,64,128]{2,1,0:T(8,128)S(1)}, u32[]{:S(2)}, u32[]{:S(2)}) %all-to-all-start.2) | async-done | bytes 131104 | tf_op jit(solution)/shard_map/all_to_all | solution.py:223
  92.3 0.7 copy.6
  (3 shorter events, 0.0 us)
Async XLA Ops:
  1.3 0.7 copy-start.4
  2.7 13.6 %all-to-all-start = ((f32[32,8,128]{2,1,0:T(8,128)}), f32[32,8,128]{2,1,0:T(8,128)S(1)}, u32[]{:S(2)}, u32[]{:S(2)}) async-start(f32[32,8,128]{2,1,0:T(8,128)} %broadcast_in_dim.2), calls=%async_computation | async-start | bytes 262144 | tf_op jit(solution)/shard_map/all_to_all | solution.py:236
  9.1 7.1 %copy-start = (s32[2,8]{1,0:T(2,128)S(1)}, s32[2,8]{1,0:T(2,128)}, u32[]{:S(2)}) copy-start(s32[2,8]{1,0:T(2,128)} %nb_ref.1) | copy-start | bytes 196
  16.2 16.8 %copy-start.3 = (f32[256,128]{1,0:T(8,128)S(1)}, f32[256,128]{1,0:T(8,128)}, u32[]{:S(2)}) copy-start(f32[256,128]{1,0:T(8,128)} %param.4) | copy-start | bytes 393220
  32.2 0.6 copy-start.2
  32.8 14.6 %collective-permute-start.5 = (f32[512,128]{1,0:T(8,128)S(1)}, f32[512,128]{1,0:T(8,128)S(1)}, u32[]{:S(2)}, u32[]{:S(2)}) collective-permute-start(f32[512,128]{1,0:T(8,128)S(1)} %get-tuple-element.11.rest_5_), channel_id=1, source_target_pairs={{0,2},{1,3},{2,0},{3,1},{4,6},{5,7},{6,4},{7,5},{8,10},{9,11},{10,... | collective-permute-start | bytes 786440 | tf_op jit(solution)/shard_map/ppermute | solution.py:218
  41.9 10.9 %collective-permute-start.3 = (f32[4,64,128]{2,1,0:T(8,128)S(1)}, f32[4,64,128]{2,1,0:T(8,128)S(1)}, u32[]{:S(2)}, u32[]{:S(2)}) collective-permute-start(f32[4,64,128]{2,1,0:T(8,128)S(1)} %all_to_all.15.rest_0_), channel_id=1, source_target_pairs={{0,16},{1,17},{2,18},{3,19},{4,20},{5,21},{6,22},{7,23},{8,24},{9,... | collective-permute-start | bytes 393224 | tf_op jit(solution)/shard_map/ppermute | solution.py:213
  43.2 9.8 %collective-permute-start.2 = (f32[4,64,128]{2,1,0:T(8,128)S(1)}, f32[4,64,128]{2,1,0:T(8,128)S(1)}, u32[]{:S(2)}, u32[]{:S(2)}) collective-permute-start(f32[4,64,128]{2,1,0:T(8,128)S(1)} %all_to_all.15.rest_0_), channel_id=1, source_target_pairs={{0,12},{1,13},{2,14},{3,15},{4,16},{5,17},{6,18},{7,19},{8,20},{9,... | collective-permute-start | bytes 393224 | tf_op jit(solution)/shard_map/ppermute | solution.py:213
  46.0 15.9 %collective-permute-start.4 = (f32[512,128]{1,0:T(8,128)S(1)}, f32[512,128]{1,0:T(8,128)S(1)}, u32[]{:S(2)}, u32[]{:S(2)}) collective-permute-start(f32[512,128]{1,0:T(8,128)S(1)} %get-tuple-element.11.rest_5_), channel_id=1, source_target_pairs={{0,1},{1,0},{2,3},{3,2},{4,5},{5,4},{6,7},{7,6},{8,9},{9,8},{10,11... | collective-permute-start | bytes 786440 | tf_op jit(solution)/shard_map/ppermute | solution.py:218
  47.4 14.5 %collective-permute-start.6 = (f32[512,128]{1,0:T(8,128)S(1)}, f32[512,128]{1,0:T(8,128)S(1)}, u32[]{:S(2)}, u32[]{:S(2)}) collective-permute-start(f32[512,128]{1,0:T(8,128)S(1)} %collective-permute-done.5.rest_7_), channel_id=1, source_target_pairs={{0,1},{1,0},{2,3},{3,2},{4,5},{5,4},{6,7},{7,6},{8,9},{9,8},{10,11... | collective-permute-start | bytes 786440 | tf_op jit(solution)/shard_map/ppermute | solution.py:218
  47.5 10.5 %collective-permute-start.1 = (f32[4,64,128]{2,1,0:T(8,128)S(1)}, f32[4,64,128]{2,1,0:T(8,128)S(1)}, u32[]{:S(2)}, u32[]{:S(2)}) collective-permute-start(f32[4,64,128]{2,1,0:T(8,128)S(1)} %all_to_all.15.rest_0_), channel_id=1, source_target_pairs={{0,8},{1,9},{2,10},{3,11},{4,12},{5,13},{6,14},{7,15},{8,16},{9,17... | collective-permute-start | bytes 393224 | tf_op jit(solution)/shard_map/ppermute | solution.py:213
  52.7 5.2 %copy-start.1 = (f32[64,128]{1,0:T(8,128)S(1)}, f32[64,128]{1,0:T(8,128)}, u32[]{:S(2)}) copy-start(f32[64,128]{1,0:T(8,128)} %invert.1.rest_9_) | copy-start | bytes 98308
  52.8 5.7 %collective-permute-start.8 = (f32[64,128]{1,0:T(8,128)}, f32[64,128]{1,0:T(8,128)S(1)}, u32[]{:S(2)}, u32[]{:S(2)}) collective-permute-start(f32[64,128]{1,0:T(8,128)} %invert.1.rest_9_), channel_id=1, source_target_pairs={{0,2},{1,3},{2,0},{3,1},{4,6},{5,7},{6,4},{7,5},{8,10},{9,11},{10,... | collective-permute-start | bytes 98312 | tf_op jit(solution)/shard_map/ppermute | solution.py:218
  53.0 8.9 %collective-permute-start = (f32[4,64,128]{2,1,0:T(8,128)S(1)}, f32[4,64,128]{2,1,0:T(8,128)S(1)}, u32[]{:S(2)}, u32[]{:S(2)}) collective-permute-start(f32[4,64,128]{2,1,0:T(8,128)S(1)} %all_to_all.15.rest_0_), channel_id=1, source_target_pairs={{0,4},{1,5},{2,6},{3,7},{4,8},{5,9},{6,10},{7,11},{8,12},{9,13},{1... | collective-permute-start | bytes 393224 | tf_op jit(solution)/shard_map/ppermute | solution.py:213
  58.0 3.9 %collective-permute-start.7 = (f32[64,128]{1,0:T(8,128)S(1)}, f32[64,128]{1,0:T(8,128)S(1)}, u32[]{:S(2)}, u32[]{:S(2)}) collective-permute-start(f32[64,128]{1,0:T(8,128)S(1)} %copy-done.1), channel_id=1, source_target_pairs={{0,1},{1,0},{2,3},{3,2},{4,5},{5,4},{6,7},{7,6},{8,9},{9,8},{10,11... | collective-permute-start | bytes 98312 | tf_op jit(solution)/shard_map/ppermute | solution.py:218
  58.5 3.4 %collective-permute-start.9 = (f32[64,128]{1,0:T(8,128)S(1)}, f32[64,128]{1,0:T(8,128)S(1)}, u32[]{:S(2)}, u32[]{:S(2)}) collective-permute-start(f32[64,128]{1,0:T(8,128)S(1)} %collective-permute-done.8.rest_11_), channel_id=1, source_target_pairs={{0,1},{1,0},{2,3},{3,2},{4,5},{5,4},{6,7},{7,6},{8,9},{9,8},{10,11... | collective-permute-start | bytes 98312 | tf_op jit(solution)/shard_map/ppermute | solution.py:218
  66.2 17.2 %collective-permute-start.10 = (f32[4,64,128]{2,1,0:T(8,128)S(1)}, f32[4,64,128]{2,1,0:T(8,128)S(1)}, u32[]{:S(2)}, u32[]{:S(2)}) collective-permute-start(f32[4,64,128]{2,1,0:T(8,128)S(1)} %get-tuple-element.15), channel_id=1, source_target_pairs={{4,0},{5,1},{6,2},{7,3},{8,4},{9,5},{10,6},{11,7},{12,8},{13,9},{1... | collective-permute-start | bytes 393224 | tf_op jit(solution)/shard_map/ppermute | solution.py:213
  69.6 13.8 %collective-permute-start.11 = (f32[4,64,128]{2,1,0:T(8,128)S(1)}, f32[4,64,128]{2,1,0:T(8,128)S(1)}, u32[]{:S(2)}, u32[]{:S(2)}) collective-permute-start(f32[4,64,128]{2,1,0:T(8,128)S(1)} %get-tuple-element.16), channel_id=1, source_target_pairs={{8,0},{9,1},{10,2},{11,3},{12,4},{13,5},{14,6},{15,7},{16,8},{17,9... | collective-permute-start | bytes 393224 | tf_op jit(solution)/shard_map/ppermute | solution.py:213
  71.5 11.9 %collective-permute-start.12 = (f32[4,64,128]{2,1,0:T(8,128)S(1)}, f32[4,64,128]{2,1,0:T(8,128)S(1)}, u32[]{:S(2)}, u32[]{:S(2)}) collective-permute-start(f32[4,64,128]{2,1,0:T(8,128)S(1)} %get-tuple-element.17), channel_id=1, source_target_pairs={{12,0},{13,1},{14,2},{15,3},{16,4},{17,5},{18,6},{19,7},{20,8},{21... | collective-permute-start | bytes 393224 | tf_op jit(solution)/shard_map/ppermute | solution.py:213
  73.5 10.0 %collective-permute-start.13 = (f32[4,64,128]{2,1,0:T(8,128)S(1)}, f32[4,64,128]{2,1,0:T(8,128)S(1)}, u32[]{:S(2)}, u32[]{:S(2)}) collective-permute-start(f32[4,64,128]{2,1,0:T(8,128)S(1)} %get-tuple-element.18), channel_id=1, source_target_pairs={{16,0},{17,1},{18,2},{19,3},{20,4},{21,5},{22,6},{23,7},{24,8},{25... | collective-permute-start | bytes 393224 | tf_op jit(solution)/shard_map/ppermute | solution.py:213
  84.1 8.2 %all-to-all-start.2 = ((f32[4,64,128]{2,1,0:T(8,128)}), f32[4,64,128]{2,1,0:T(8,128)S(1)}, u32[]{:S(2)}, u32[]{:S(2)}) async-start(f32[4,64,128]{2,1,0:T(8,128)} %add_add_fusion), calls=%async_computation.2 | async-start | bytes 262144 | tf_op jit(solution)/shard_map/all_to_all | solution.py:223

commit v2 on v1

--- a/solution.py
+++ b/solution.py
@@ -20,11 +20,16 @@
 COND = NEIGH * PTS
 STEPS = COND // WIDE
 HIGHEST = lax.Precision.HIGHEST
+HIGH = lax.Precision.HIGH
 F32 = jnp.float32
 
 
-def dot(a, b, dims=((1,), (0,))):
-    return lax.dot_general(a, b, (dims, ((), ())), precision=HIGHEST, preferred_element_type=F32)
+def dot(a, b, dims=((1,), (0,)), precision=HIGHEST):
+    return lax.dot_general(a, b, (dims, ((), ())), precision=precision, preferred_element_type=F32)
+
+
+def quick(a, b, dims=((1,), (0,))):
+    return dot(a, b, dims, HIGH)
 
 
 def iota(shape, dim):
@@ -51,15 +56,15 @@
     rs = [ident - alpha * m for m in mats]
     c = factors[0]
     xs = [(alpha * c) * (ident + r) for r in rs]
-    rs = [(1.0 - c) * ident + c * dot(r, r) for r in rs]
+    rs = [(1.0 - c) * ident + c * quick(r, r) for r in rs]
     for c in factors[1:-1]:
-        nxt = [c * (x + dot(x, r)) for x, r in zip(xs, rs)]
-        rs = [(1.0 - c) * ident + c * dot(r, r) for r in rs]
+        nxt = [c * (x + quick(x, r)) for x, r in zip(xs, rs)]
+        rs = [(1.0 - c) * ident + c * quick(r, r) for r in rs]
         xs = nxt
     c = factors[-1]
-    xs = [c * (x + dot(x, r)) for x, r in zip(xs, rs)]
+    xs = [c * (x + quick(x, r)) for x, r in zip(xs, rs)]
     es = [ident - dot(m, x) for m, x in zip(mats, xs)]
-    return [x + dot(x, e) for x, e in zip(xs, es)]
+    return [x + quick(x, e) for x, e in zip(xs, es)]
 
 
 def kernel_value(dx, dy):
@@ -151,10 +156,10 @@
         places = []
         for b in range(BLK):
             for m in range(NEIGH):
-                ident = ids_ref[sender, b * NEIGH + m]
+                ident = ids_ref[sender, b, m]
                 ident = jnp.where(ident >= 0, ident, device * BLK)
                 owner = lax.div(ident, BLK)
-                place = (slab - lax.div(owner, SLAB)) * SLAB + lax.rem(owner, SLAB)
+                place = (slab - lax.div(owner, SLAB)) * SLAB + (lax.rem(owner, SLAB) ^ quarter)
                 turn = (lax.rem(ident, BLK) ^ (m % 2)) * PTS
                 places.append((place, turn))
         gathered = []
@@ -167,14 +172,14 @@
                 pieces.append(jnp.where(low, first, second))
             gathered.append(jnp.concatenate(pieces, axis=1))
         w = w_refs[k][...]
-        white = dot(jnp.concatenate(gathered, axis=0), w)
-        white = held[sender] + jnp.where(low, white[:PTS], white[PTS:])
+        white = quick(jnp.concatenate(gathered, axis=0), w)
+        white = held[k] + jnp.where(low, white[:PTS], white[PTS:])
         v = v_refs[k][...]
         inv = jnp.concatenate([jnp.where(low, v, 0.0), jnp.where(low, 0.0, v)], axis=0)
         scaled = dot(white, inv)
-        total[sender] += scaled
+        total[k] += scaled
         sides = jnp.concatenate([jnp.where(low, scaled, 0.0), jnp.where(low, 0.0, scaled)], axis=0)
-        back = dot(sides, w, ((1,), (1,)))
+        back = quick(sides, w, ((1,), (1,)))
         for b in range(BLK):
             for m in range(NEIGH):
                 place, turn = places[b * NEIGH + m]
@@ -208,6 +213,35 @@
     out_ref[...] = jnp.broadcast_to(total * (1.0 / PTS), out_ref.shape)
 
 
+def prepare_kernel(where_ref, coords_ref, nb_ref, probes_ref, told_ref, *outs_and_scratch):
+    outs, scratch = outs_and_scratch[:-1], outs_and_scratch[-1]
+    quarter = lax.rem(where_ref[0], SLAB)
+    rows = outs[0].shape[0]
+    scratch[...] = jnp.zeros_like(scratch)
+    scratch[:2, :] = coords_ref[...]
+    scratch[2 : 2 + BLK, :NEIGH] = nb_ref[...].astype(F32)
+    told_ref[...] = jnp.broadcast_to(scratch[...][None], told_ref.shape)
+    for k in range(SLAB):
+        outs[k][...] = probes_ref[pl.ds(pl.multiple_of((quarter ^ k) * rows, rows), rows), :]
+
+
+def sum_kernel(*refs):
+    terms, outs = refs[:WINDOW], refs[WINDOW:]
+    for k in range(SLAB):
+        value = terms[0][k]
+        for o in range(1, WINDOW):
+            value = value + terms[o][k]
+        outs[k][...] = value
+
+
+def place_kernel(where_ref, *refs):
+    tiles, out_ref = refs[:SLAB], refs[SLAB]
+    quarter = lax.rem(where_ref[0], SLAB)
+    rows = tiles[0].shape[0]
+    for k in range(SLAB):
+        out_ref[pl.ds(pl.multiple_of((quarter ^ k) * rows, rows), rows), :] = tiles[k][...]
+
+
 def passed(value, by):
     size = lax.axis_size(AXES)
     return lax.ppermute(value, AXES, [(i, i + by) for i in range(size) if 0 <= i + by < size])
@@ -218,9 +252,18 @@
     return lax.ppermute(value, AXES, [(i, i ^ mask) for i in range(size)])
 
 
-def within_slab(value):
-    groups = [[SLAB * j + i for i in range(SLAB)] for j in range(lax.axis_size(AXES[1]) // SLAB)]
-    return lax.all_to_all(value, AXES[1], 0, 0, axis_index_groups=groups)
+def local(kernel, name, outs, specs, scratch=(), gflops=1):
+    vmem = pl.BlockSpec(memory_space=pltpu.VMEM)
+    return pl.pallas_call(
+        kernel,
+        out_shape=outs,
+        in_specs=specs,
+        out_specs=jax.tree.map(lambda _: vmem, outs),
+        scratch_shapes=list(scratch),
+        compiler_params=pltpu.CompilerParams(vmem_limit_bytes=32 * 2**20),
+        cost_estimate=pl.CostEstimate(flops=gflops * 10**9, bytes_accessed=10**5, transcendentals=0),
+        name=name,
+    )
 
 
 def shards(coords, probes, neighbours):
@@ -230,64 +273,53 @@
     here = jnp.reshape(device, (1,)).astype(jnp.int32)
     smem = pl.BlockSpec(memory_space=pltpu.SMEM)
     vmem = pl.BlockSpec(memory_space=pltpu.VMEM)
-
-    ids_row = jnp.pad(neighbours.astype(F32).reshape(1, -1), ((0, 0), (0, WIDE - BLK * NEIGH)))
-    told = jnp.pad(jnp.concatenate([coords, ids_row], axis=0), ((0, 5), (0, 0)))
-    everywhere = lax.all_to_all(jnp.broadcast_to(told[None], (count, 8, WIDE)), AXES, 0, 0)
-    ids = lax.dynamic_slice(everywhere, (device // SLAB * SLAB, 2, 0), (SLAB, 1, BLK * NEIGH))
-    ids = ids.reshape(SLAB, BLK * NEIGH).astype(jnp.int32)
-    own = within_slab(probes.reshape(SLAB, quarter, WIDE))
+    tile = jax.ShapeDtypeStruct((quarter, WIDE), F32)
+    tiles = jax.ShapeDtypeStruct((SLAB, quarter, WIDE), F32)
+    square = jax.ShapeDtypeStruct((PTS, WIDE), F32)
+
+    told, *pieces = local(
+        prepare_kernel,
+        "prepare",
+        (jax.ShapeDtypeStruct((count, 8, WIDE), F32),) + (tile,) * SLAB,
+        [smem, vmem, vmem, vmem],
+        [pltpu.VMEM((8, WIDE), F32)],
+    )(here, coords, neighbours, probes)
+    everywhere = lax.all_to_all(told, AXES, 0, 0)
+    own = jnp.stack([pieces[0]] + [swapped(pieces[k], k) for k in range(1, SLAB)])
+    ids = lax.dynamic_slice(everywhere, (device // SLAB * SLAB, 2, 0), (SLAB, BLK, NEIGH)).astype(jnp.int32)
     window = [own] + [passed(own, SLAB * o) for o in range(1, WINDOW)]
 
-    w, schur = pl.pallas_call(
+    w, schur = local(
         factor_kernel,
-        out_shape=(jax.ShapeDtypeStruct((COND, WIDE), F32), jax.ShapeDtypeStruct((PTS, WIDE), F32)),
-        in_specs=[smem, smem, vmem],
-        out_specs=(vmem, vmem),
-        compiler_params=pltpu.CompilerParams(vmem_limit_bytes=32 * 2**20),
-        cost_estimate=pl.CostEstimate(flops=10**9, bytes_accessed=10**6, transcendentals=10**6),
-        name="factor",
+        "factor",
+        (jax.ShapeDtypeStruct((COND, WIDE), F32), square),
+        [smem, smem, vmem],
+        gflops=16,
     )(here, neighbours, everywhere)
+    w, schur, *window = lax.optimization_barrier((w, schur, *window))
     w_y = swapped(w, 2)
     w_d = swapped(w, 1)
-    v = pl.pallas_call(
-        invert_kernel,
-        out_shape=jax.ShapeDtypeStruct((PTS, WIDE), F32),
-        in_specs=[vmem],
-        out_specs=vmem,
-        cost_estimate=pl.CostEstimate(flops=10**8, bytes_accessed=10**5, transcendentals=0),
-        name="invert",
-    )(schur)
-    v_y = swapped(v, 2)
-    v_d = swapped(v, 1)
+    v = local(invert_kernel, "invert", square, [vmem], gflops=3)(schur)
+    v_d, v_y, v_yd = (swapped(v, k) for k in range(1, SLAB))
+    w_y, v = lax.optimization_barrier((w_y, v))
     w_yd = swapped(w_y, 1)
-    v_yd = swapped(v_y, 1)
-    tile = jax.ShapeDtypeStruct((SLAB, quarter, WIDE), F32)
-    terms = pl.pallas_call(
+    terms = local(
         apply_kernel,
-        out_shape=(tile,) * WINDOW,
-        in_specs=[smem, smem] + [vmem] * (WINDOW + 2 * SLAB),
-        out_specs=(vmem,) * WINDOW,
-        scratch_shapes=[pltpu.VMEM((WINDOW * SLAB, quarter, WIDE), F32)] * 2,
-        compiler_params=pltpu.CompilerParams(vmem_limit_bytes=32 * 2**20),
-        cost_estimate=pl.CostEstimate(flops=10**9, bytes_accessed=10**6, transcendentals=0),
-        name="apply",
+        "apply",
+        (tiles,) * WINDOW,
+        [smem, smem] + [vmem] * (WINDOW + 2 * SLAB),
+        [pltpu.VMEM((WINDOW * SLAB, quarter, WIDE), F32)] * 2,
+        gflops=4,
     )(here, ids, *window, w, w_d, w_y, w_yd, v, v_d, v_y, v_yd)
-    logs = pl.pallas_call(
-        logdet_kernel,
-        out_shape=jax.ShapeDtypeStruct((8, WIDE), F32),
-        in_specs=[vmem],
-        out_specs=vmem,
-        scratch_shapes=[pltpu.VMEM((PTS, WIDE), F32)],
-        cost_estimate=pl.CostEstimate(flops=10**7, bytes_accessed=10**6, transcendentals=0),
-        name="logdet",
+    logs = local(
+        logdet_kernel, "logdet", jax.ShapeDtypeStruct((8, WIDE), F32), [vmem], [pltpu.VMEM((PTS, WIDE), F32)], gflops=9
     )(schur)
     returned = [passed(terms[o], -SLAB * o) for o in range(1, WINDOW)]
     kept, logs = lax.optimization_barrier((terms[0], logs))
-    total = kept
-    for part in returned:
-        total = total + part
-    result = within_slab(total).reshape(SLAB * quarter, WIDE)
+    sums = local(sum_kernel, "sum", (tile,) * SLAB, [vmem] * WINDOW)(kept, *returned)
+    result = local(place_kernel, "place", jax.ShapeDtypeStruct(probes.shape, F32), [smem] + [vmem] * SLAB)(
+        here, sums[0], *(swapped(sums[k], k) for k in range(1, SLAB))
+    )
     return result, logs[0, :: PTS]
 
 

time: 94.3 us -> 80.1 us (0.85)
  starting transfers between devices: 30 us -> 39.1 us
  blocking collectives: 8.82 us -> 0 us
  Pallas kernels: 32.3 us -> 26.5 us
  waiting for transfers between devices: 15.9 us -> 11 us
  local copies, waits for them, and re-layouts: 3.89 us -> 2.17 us
  other arithmetic: 1.39 us -> 0.02 us
    ppermute x6 -> x12, waiting for transfers between devices: 0.02 us -> 10.9 us  [swapped(): return lax.ppermute(value, AXES, [(i, i ^ mask) for i in range(size)])]
    all_to_all x2 -> x1, waiting for transfers between devices: 9.44 us -> 0.01 us  [shards(): everywhere = lax.all_to_all(told, AXES, 0, 0)]
    all_to_all x1 -> x0, blocking collectives: 8.82 us -> none  [within_slab(): return lax.all_to_all(value, AXES[1], 0, 0, axis_index_groups=groups)]
    ppermute x6 -> x12, starting transfers between devices: 2.49 us -> 11 us  [swapped(): return lax.ppermute(value, AXES, [(i, i ^ mask) for i in range(size)])]
    ppermute x8, waiting for transfers between devices: 6.42 us -> 0.02 us  [passed(): lax.ppermute(value, AXES, [(i, i + by) for i in range(size) if 0 <= i + b...]
    pallas_call x4 -> x7, Pallas kernels: 32.3 us -> 26.5 us  [the longest x1 12.7 us: shards(): local(factor_kernel, 'factor', (jax.ShapeDtypeStruct((COND, WIDE), F32),...]
    ppermute x8, starting transfers between devices: 16.4 us -> 21.7 us  [passed(): lax.ppermute(value, AXES, [(i, i + by) for i in range(size) if 0 <= i + b...]
    all_to_all x2 -> x1, starting transfers between devices: 11.1 us -> 6.44 us  [shards(): everywhere = lax.all_to_all(told, AXES, 0, 0)]
  transfers between devices with their start and end apart: 16 -> 21, of which waited for: 4 -> 6; matrix products, arithmetic and copies ran while one was open for 1% -> 1% of each run, Pallas kernels for 13% -> 27%
where the time goes in v2:
time: 80.1 us; the launch traced here: 79.5 us
  starting transfers between devices  39.1 us (49%)
  Pallas kernels  26.5 us (33%)
  waiting for transfers between devices  11 us (14%)
  local copies, waits for them, and re-layouts  2.17 us (3%)
  between operations  0.85 us (1%)
    ppermute x8, starting transfers between devices, passed(): lax.ppermute(value, AXES, [(i, i + by) for i in range(size) if 0 <= i + b...  21.7 us
    pallas_call x1, Pallas kernels, shards(): local(factor_kernel, 'factor', (jax.ShapeDtypeStruct((COND, WIDE), F32),...  12.7 us
    ppermute x12, starting transfers between devices, swapped(): return lax.ppermute(value, AXES, [(i, i ^ mask) for i in range(size)])  11 us
    ppermute x12, waiting for transfers between devices, swapped(): return lax.ppermute(value, AXES, [(i, i ^ mask) for i in range(size)])  10.9 us
    pallas_call x1, Pallas kernels, shards(): local(logdet_kernel, 'logdet', jax.ShapeDtypeStruct((8, WIDE), F32), [vme...  7.31 us
    all_to_all x1, starting transfers between devices, shards(): everywhere = lax.all_to_all(told, AXES, 0, 0)  6.44 us
    pallas_call x1, Pallas kernels, shards(): local(apply_kernel, 'apply', (tiles,) * WINDOW, [smem, smem] + [vmem] * (...  3.45 us
  transfers between devices with their start and end apart: 21, of which 6 were waited for; matrix products, arithmetic and copies ran while one was open for 1% of the time, Pallas kernels for 27%

profile of v2, /device:TPU:3, one launch (start us, length us, event | category | flops | bytes accessed | tf_op | source)
XLA Modules:
  0.0 79.5 jit_solution(18050396371511033810)
XLA Ops:
  0.6 0.0 copy-start.2
  0.6 0.0 copy-start.1
  0.7 0.7 copy-done.2
  1.3 0.0 copy-done.1
  1.3 0.0 copy-start
  1.3 0.9 %copy-done = f32[256,128]{1,0:T(8,128)S(1)} copy-done((f32[256,128]{1,0:T(8,128)S(1)}, f32[256,128]{1,0:T(8,128)}, u32[]{:S(2)}) %copy-start) | copy-done | bytes 131096
  2.2 0.7 prepare.1
  2.9 6.4 %all-to-all-start = ((f32[32,8,128]{2,1,0:T(8,128)}), f32[32,8,128]{2,1,0:T(8,128)S(1)}, u32[]{:S(2)}, u32[]{:S(2)}) async-start(f32[32,8,128]{2,1,0:T(8,128)} %get-tuple-element.29), calls=%async_computation | async-start | bytes 262144 | tf_op jit(solution)/shard_map/all_to_all | solution.py:287
  9.4 0.4 collective-permute-start
  9.8 1.2 %collective-permute-start.1 = (f32[64,128]{1,0:T(8,128)S(1)}, f32[64,128]{1,0:T(8,128)S(1)}, u32[]{:S(2)}, u32[]{:S(2)}) collective-permute-start(f32[64,128]{1,0:T(8,128)S(1)} %get-tuple-element.34), channel_id=1, source_target_pairs={{0,2},{1,3},{2,0},{3,1},{4,6},{5,7},{6,4},{7,5},{8,10},{9,11},{10,... | collective-permute-start | bytes 98312 | tf_op jit(solution)/shard_map/ppermute | solution.py:252
  11.0 0.6 collective-permute-start.2
  11.6 0.0 collective-permute-done
  11.6 1.5 %collective-permute-done.1 = f32[64,128]{1,0:T(8,128)S(1)} collective-permute-done((f32[64,128]{1,0:T(8,128)S(1)}, f32[64,128]{1,0:T(8,128)S(1)}, u32[]{:S(2)}, u32[]{:S(2)}) %collective-permute-start.1) | collective-permute-done | bytes 32800 | tf_op jit(solution)/shard_map/ppermute | solution.py:252
  13.0 1.9 %collective-permute-done.2 = f32[64,128]{1,0:T(8,128)S(1)} collective-permute-done((f32[64,128]{1,0:T(8,128)S(1)}, f32[64,128]{1,0:T(8,128)S(1)}, u32[]{:S(2)}, u32[]{:S(2)}) %collective-permute-start.2) | collective-permute-done | bytes 32800 | tf_op jit(solution)/shard_map/ppermute | solution.py:252
  14.9 1.3 %collective-permute-start.6 = (f32[4,64,128]{2,1,0:T(8,128)S(1)}, f32[4,64,128]{2,1,0:T(8,128)S(1)}, u32[]{:S(2)}, u32[]{:S(2)}) collective-permute-start(f32[4,64,128]{2,1,0:T(8,128)S(1)} %pad_maximum_fusion.rest_0_), channel_id=1, source_target_pairs={{0,16},{1,17},{2,18},{3,19},{4,20},{5,21},{6,22},{7,23},{8,24},{9,... | collective-permute-start | bytes 393224 | tf_op jit(solution)/shard_map/ppermute | solution.py:247
  16.2 4.8 %collective-permute-start.5 = (f32[4,64,128]{2,1,0:T(8,128)S(1)}, f32[4,64,128]{2,1,0:T(8,128)S(1)}, u32[]{:S(2)}, u32[]{:S(2)}) collective-permute-start(f32[4,64,128]{2,1,0:T(8,128)S(1)} %pad_maximum_fusion.rest_0_), channel_id=1, source_target_pairs={{0,12},{1,13},{2,14},{3,15},{4,16},{5,17},{6,18},{7,19},{8,20},{9,... | collective-permute-start | bytes 393224 | tf_op jit(solution)/shard_map/ppermute | solution.py:247
  21.0 1.9 %collective-permute-start.4 = (f32[4,64,128]{2,1,0:T(8,128)S(1)}, f32[4,64,128]{2,1,0:T(8,128)S(1)}, u32[]{:S(2)}, u32[]{:S(2)}) collective-permute-start(f32[4,64,128]{2,1,0:T(8,128)S(1)} %pad_maximum_fusion.rest_0_), channel_id=1, source_target_pairs={{0,8},{1,9},{2,10},{3,11},{4,12},{5,13},{6,14},{7,15},{8,16},{9,17... | collective-permute-start | bytes 393224 | tf_op jit(solution)/shard_map/ppermute | solution.py:247
  22.9 1.9 %collective-permute-start.3 = (f32[4,64,128]{2,1,0:T(8,128)S(1)}, f32[4,64,128]{2,1,0:T(8,128)S(1)}, u32[]{:S(2)}, u32[]{:S(2)}) collective-permute-start(f32[4,64,128]{2,1,0:T(8,128)S(1)} %pad_maximum_fusion.rest_0_), channel_id=1, source_target_pairs={{0,4},{1,5},{2,6},{3,7},{4,8},{5,9},{6,10},{7,11},{8,12},{9,13},{1... | collective-permute-start | bytes 393224 | tf_op jit(solution)/shard_map/ppermute | solution.py:247
  24.9 0.0 all-to-all-done.coords_ref
  24.9 12.7 %factor.1 = (f32[512,128]{1,0:T(8,128)S(1)}, f32[64,128]{1,0:T(8,128)S(1)}) custom-call(s32[1]{0:T(128)} %bitcast.where_ref, s32[2,8]{1,0:T(2,128)S(1)} %copy-done.2, f32[32,8,128]{2,1,0:T(8,128)S(1)} %all-to-all-done.coords_ref), custom_call_target="tpu_custom_call" | custom-call | flops 16000000000 | bytes 100000 | tf_op jit(solution)/shard_map/factor/pallas_call | solution.py:292
  37.6 0.0 collective-permute-done.6.rest_4_
  37.6 0.0 collective-permute-done.5.rest_3_
  37.6 0.0 collective-permute-done.4.rest_2_
  37.6 0.0 collective-permute-done.3.rest_1_
  37.7 0.5 collective-permute-start.8
  38.2 0.9 %collective-permute-start.7 = (f32[512,128]{1,0:T(8,128)S(1)}, f32[512,128]{1,0:T(8,128)S(1)}, u32[]{:S(2)}, u32[]{:S(2)}) collective-permute-start(f32[512,128]{1,0:T(8,128)S(1)} %get-tuple-element.41.rest_5_), channel_id=1, source_target_pairs={{0,1},{1,0},{2,3},{3,2},{4,5},{5,4},{6,7},{7,6},{8,9},{9,8},{10,11... | collective-permute-start | bytes 786440 | tf_op jit(solution)/shard_map/ppermute | solution.py:252
  39.1 1.6 %invert.1.rest_9_ = f32[64,128]{1,0:T(8,128)S(1)} custom-call(f32[64,128]{1,0:T(8,128)S(1)} %get-tuple-element.42.s_ref), custom_call_target="tpu_custom_call" | custom-call | flops 3000000000 | bytes 100000 | tf_op jit(solution)/shard_map/invert/pallas_call | solution.py:302
  40.7 4.2 %collective-permute-done.8.rest_7_ = f32[512,128]{1,0:T(8,128)S(1)} collective-permute-done((f32[512,128]{1,0:T(8,128)S(1)}, f32[512,128]{1,0:T(8,128)S(1)}, u32[]{:S(2)}, u32[]{:S(2)}) %collective-permute-start.8) | collective-permute-done | bytes 262176 | tf_op jit(solution)/shard_map/ppermute | solution.py:252
  44.9 1.5 %collective-permute-start.9 = (f32[512,128]{1,0:T(8,128)S(1)}, f32[512,128]{1,0:T(8,128)S(1)}, u32[]{:S(2)}, u32[]{:S(2)}) collective-permute-start(f32[512,128]{1,0:T(8,128)S(1)} %collective-permute-done.8.rest_7_), channel_id=1, source_target_pairs={{0,1},{1,0},{2,3},{3,2},{4,5},{5,4},{6,7},{7,6},{8,9},{9,8},{10,11... | collective-permute-start | bytes 786440 | tf_op jit(solution)/shard_map/ppermute | solution.py:252
  46.4 0.4 collective-permute-start.12
  46.8 1.0 %collective-permute-start.11 = (f32[64,128]{1,0:T(8,128)S(1)}, f32[64,128]{1,0:T(8,128)S(1)}, u32[]{:S(2)}, u32[]{:S(2)}) collective-permute-start(f32[64,128]{1,0:T(8,128)S(1)} %invert.1.rest_9_), channel_id=1, source_target_pairs={{0,2},{1,3},{2,0},{3,1},{4,6},{5,7},{6,4},{7,5},{8,10},{9,11},{10,... | collective-permute-start | bytes 98312 | tf_op jit(solution)/shard_map/ppermute | solution.py:252
  47.8 0.8 collective-permute-start.10
  48.6 1.3 %collective-permute-done.12.rest_12_ = f32[64,128]{1,0:T(8,128)S(1)} collective-permute-done((f32[64,128]{1,0:T(8,128)S(1)}, f32[64,128]{1,0:T(8,128)S(1)}, u32[]{:S(2)}, u32[]{:S(2)}) %collective-permute-start.12) | collective-permute-done | bytes 32800 | tf_op jit(solution)/shard_map/ppermute | solution.py:252
  49.9 0.0 collective-permute-done.11.rest_11_
  49.9 0.0 collective-permute-done.10.rest_10_
  49.9 0.0 collective-permute-done.7.rest_6_
  49.9 0.0 collective-permute-done.9.rest_8_
  49.9 3.4 %apply.1 = (f32[4,64,128]{2,1,0:T(8,128)S(1)}, f32[4,64,128]{2,1,0:T(8,128)S(1)}, f32[4,64,128]{2,1,0:T(8,128)S(1)}, f32[4,64,128]{2,1,0:T(8,128)S(1)}, f32[4,64,128]{2,1,0:T(8,128)S(1)}) custom-call(s32[1]{0:T(128)} %bitcast.where_ref, s32[4,2,8]{2,1,0:T(2,128)S(1)} %dynamic-slice_convert_fusion.ids_ref, f32[4,64,128]{2,1,0:T(8,128)S(1)} %pad_maximum_fusion.rest_0_, ...), custom_call_target="tpu_custom_call" | custom-call | flops 4000000000 | bytes 100000 | tf_op jit(solution)/shard_map/apply/pallas_call | solution.py:306
  53.4 6.1 %collective-permute-start.13 = (f32[4,64,128]{2,1,0:T(8,128)S(1)}, f32[4,64,128]{2,1,0:T(8,128)S(1)}, u32[]{:S(2)}, u32[]{:S(2)}) collective-permute-start(f32[4,64,128]{2,1,0:T(8,128)S(1)} %get-tuple-element.47), channel_id=1, source_target_pairs={{4,0},{5,1},{6,2},{7,3},{8,4},{9,5},{10,6},{11,7},{12,8},{13,9},{1... | collective-permute-start | bytes 393224 | tf_op jit(solution)/shard_map/ppermute | solution.py:247
  59.5 2.5 %collective-permute-start.14 = (f32[4,64,128]{2,1,0:T(8,128)S(1)}, f32[4,64,128]{2,1,0:T(8,128)S(1)}, u32[]{:S(2)}, u32[]{:S(2)}) collective-permute-start(f32[4,64,128]{2,1,0:T(8,128)S(1)} %get-tuple-element.48), channel_id=1, source_target_pairs={{8,0},{9,1},{10,2},{11,3},{12,4},{13,5},{14,6},{15,7},{16,8},{17,9... | collective-permute-start | bytes 393224 | tf_op jit(solution)/shard_map/ppermute | solution.py:247
  62.0 1.9 %collective-permute-start.15 = (f32[4,64,128]{2,1,0:T(8,128)S(1)}, f32[4,64,128]{2,1,0:T(8,128)S(1)}, u32[]{:S(2)}, u32[]{:S(2)}) collective-permute-start(f32[4,64,128]{2,1,0:T(8,128)S(1)} %get-tuple-element.49), channel_id=1, source_target_pairs={{12,0},{13,1},{14,2},{15,3},{16,4},{17,5},{18,6},{19,7},{20,8},{21... | collective-permute-start | bytes 393224 | tf_op jit(solution)/shard_map/ppermute | solution.py:247
  63.9 1.3 %collective-permute-start.16 = (f32[4,64,128]{2,1,0:T(8,128)S(1)}, f32[4,64,128]{2,1,0:T(8,128)S(1)}, u32[]{:S(2)}, u32[]{:S(2)}) collective-permute-start(f32[4,64,128]{2,1,0:T(8,128)S(1)} %get-tuple-element.50), channel_id=1, source_target_pairs={{16,0},{17,1},{18,2},{19,3},{20,4},{21,5},{22,6},{23,7},{24,8},{25... | collective-permute-start | bytes 393224 | tf_op jit(solution)/shard_map/ppermute | solution.py:247
  65.2 7.3 %logdet.1 = f32[8,128]{1,0:T(8,128)S(1)} custom-call(f32[64,128]{1,0:T(8,128)S(1)} %get-tuple-element.42.s_ref), custom_call_target="tpu_custom_call" | custom-call | flops 8999999488 | bytes 100000 | tf_op jit(solution)/shard_map/logdet/pallas_call | solution.py:314
  72.5 0.0 collective-permute-done.13.refs_1_
  72.5 0.0 collective-permute-done.14.refs_2_
  72.5 0.0 collective-permute-done.15.refs_3_
  72.5 0.0 collective-permute-done.16.refs_4_
  72.5 0.1 sum.1
  72.6 1.9 %collective-permute-start.17 = (f32[64,128]{1,0:T(8,128)S(1)}, f32[64,128]{1,0:T(8,128)S(1)}, u32[]{:S(2)}, u32[]{:S(2)}) collective-permute-start(f32[64,128]{1,0:T(8,128)S(1)} %get-tuple-element.52), channel_id=1, source_target_pairs={{0,1},{1,0},{2,3},{3,2},{4,5},{5,4},{6,7},{7,6},{8,9},{9,8},{10,11... | collective-permute-start | bytes 98312 | tf_op jit(solution)/shard_map/ppermute | solution.py:252
  74.5 1.0 %collective-permute-start.18 = (f32[64,128]{1,0:T(8,128)S(1)}, f32[64,128]{1,0:T(8,128)S(1)}, u32[]{:S(2)}, u32[]{:S(2)}) collective-permute-start(f32[64,128]{1,0:T(8,128)S(1)} %get-tuple-element.53), channel_id=1, source_target_pairs={{0,2},{1,3},{2,0},{3,1},{4,6},{5,7},{6,4},{7,5},{8,10},{9,11},{10,... | collective-permute-start | bytes 98312 | tf_op jit(solution)/shard_map/ppermute | solution.py:252
  75.5 0.7 collective-permute-start.19
  76.2 0.6 slice.3
  76.8 0.0 collective-permute-done.17.refs_1_
  76.8 0.5 collective-permute-done.18.refs_2_
  77.3 1.6 %collective-permute-done.19.refs_3_ = f32[64,128]{1,0:T(8,128)S(1)} collective-permute-done((f32[64,128]{1,0:T(8,128)S(1)}, f32[64,128]{1,0:T(8,128)S(1)}, u32[]{:S(2)}, u32[]{:S(2)}) %collective-permute-start.19) | collective-permute-done | bytes 32800 | tf_op jit(solution)/shard_map/ppermute | solution.py:252
  78.9 0.7 place.1
  (2 shorter events, 0.0 us)
Async XLA Ops:
  0.6 0.7 copy-start.2
  0.6 0.7 copy-start.1
  1.3 0.9 %copy-start = (f32[256,128]{1,0:T(8,128)S(1)}, f32[256,128]{1,0:T(8,128)}, u32[]{:S(2)}) copy-start(f32[256,128]{1,0:T(8,128)} %probes_ref.1) | copy-start | bytes 393220
  2.9 21.9 %all-to-all-start = ((f32[32,8,128]{2,1,0:T(8,128)}), f32[32,8,128]{2,1,0:T(8,128)S(1)}, u32[]{:S(2)}, u32[]{:S(2)}) async-start(f32[32,8,128]{2,1,0:T(8,128)} %get-tuple-element.29), calls=%async_computation | async-start | bytes 262144 | tf_op jit(solution)/shard_map/all_to_all | solution.py:287
  9.4 2.2 %collective-permute-start = (f32[64,128]{1,0:T(8,128)S(1)}, f32[64,128]{1,0:T(8,128)S(1)}, u32[]{:S(2)}, u32[]{:S(2)}) collective-permute-start(f32[64,128]{1,0:T(8,128)S(1)} %get-tuple-element.33), channel_id=1, source_target_pairs={{0,1},{1,0},{2,3},{3,2},{4,5},{5,4},{6,7},{7,6},{8,9},{9,8},{10,11... | collective-permute-start | bytes 98312 | tf_op jit(solution)/shard_map/ppermute | solution.py:252
  9.8 3.3 %collective-permute-start.1 = (f32[64,128]{1,0:T(8,128)S(1)}, f32[64,128]{1,0:T(8,128)S(1)}, u32[]{:S(2)}, u32[]{:S(2)}) collective-permute-start(f32[64,128]{1,0:T(8,128)S(1)} %get-tuple-element.34), channel_id=1, source_target_pairs={{0,2},{1,3},{2,0},{3,1},{4,6},{5,7},{6,4},{7,5},{8,10},{9,11},{10,... | collective-permute-start | bytes 98312 | tf_op jit(solution)/shard_map/ppermute | solution.py:252
  11.0 3.9 %collective-permute-start.2 = (f32[64,128]{1,0:T(8,128)S(1)}, f32[64,128]{1,0:T(8,128)S(1)}, u32[]{:S(2)}, u32[]{:S(2)}) collective-permute-start(f32[64,128]{1,0:T(8,128)S(1)} %get-tuple-element.35), channel_id=1, source_target_pairs={{0,3},{1,2},{2,1},{3,0},{4,7},{5,6},{6,5},{7,4},{8,11},{9,10},{10,... | collective-permute-start | bytes 98312 | tf_op jit(solution)/shard_map/ppermute | solution.py:252
  14.9 22.7 %collective-permute-start.6 = (f32[4,64,128]{2,1,0:T(8,128)S(1)}, f32[4,64,128]{2,1,0:T(8,128)S(1)}, u32[]{:S(2)}, u32[]{:S(2)}) collective-permute-start(f32[4,64,128]{2,1,0:T(8,128)S(1)} %pad_maximum_fusion.rest_0_), channel_id=1, source_target_pairs={{0,16},{1,17},{2,18},{3,19},{4,20},{5,21},{6,22},{7,23},{8,24},{9,... | collective-permute-start | bytes 393224 | tf_op jit(solution)/shard_map/ppermute | solution.py:247
  16.2 21.4 %collective-permute-start.5 = (f32[4,64,128]{2,1,0:T(8,128)S(1)}, f32[4,64,128]{2,1,0:T(8,128)S(1)}, u32[]{:S(2)}, u32[]{:S(2)}) collective-permute-start(f32[4,64,128]{2,1,0:T(8,128)S(1)} %pad_maximum_fusion.rest_0_), channel_id=1, source_target_pairs={{0,12},{1,13},{2,14},{3,15},{4,16},{5,17},{6,18},{7,19},{8,20},{9,... | collective-permute-start | bytes 393224 | tf_op jit(solution)/shard_map/ppermute | solution.py:247
  21.0 16.6 %collective-permute-start.4 = (f32[4,64,128]{2,1,0:T(8,128)S(1)}, f32[4,64,128]{2,1,0:T(8,128)S(1)}, u32[]{:S(2)}, u32[]{:S(2)}) collective-permute-start(f32[4,64,128]{2,1,0:T(8,128)S(1)} %pad_maximum_fusion.rest_0_), channel_id=1, source_target_pairs={{0,8},{1,9},{2,10},{3,11},{4,12},{5,13},{6,14},{7,15},{8,16},{9,17... | collective-permute-start | bytes 393224 | tf_op jit(solution)/shard_map/ppermute | solution.py:247
  22.9 14.7 %collective-permute-start.3 = (f32[4,64,128]{2,1,0:T(8,128)S(1)}, f32[4,64,128]{2,1,0:T(8,128)S(1)}, u32[]{:S(2)}, u32[]{:S(2)}) collective-permute-start(f32[4,64,128]{2,1,0:T(8,128)S(1)} %pad_maximum_fusion.rest_0_), channel_id=1, source_target_pairs={{0,4},{1,5},{2,6},{3,7},{4,8},{5,9},{6,10},{7,11},{8,12},{9,13},{1... | collective-permute-start | bytes 393224 | tf_op jit(solution)/shard_map/ppermute | solution.py:247
  37.7 7.2 %collective-permute-start.8 = (f32[512,128]{1,0:T(8,128)S(1)}, f32[512,128]{1,0:T(8,128)S(1)}, u32[]{:S(2)}, u32[]{:S(2)}) collective-permute-start(f32[512,128]{1,0:T(8,128)S(1)} %get-tuple-element.41.rest_5_), channel_id=1, source_target_pairs={{0,2},{1,3},{2,0},{3,1},{4,6},{5,7},{6,4},{7,5},{8,10},{9,11},{10,... | collective-permute-start | bytes 786440 | tf_op jit(solution)/shard_map/ppermute | solution.py:252
  38.2 11.7 %collective-permute-start.7 = (f32[512,128]{1,0:T(8,128)S(1)}, f32[512,128]{1,0:T(8,128)S(1)}, u32[]{:S(2)}, u32[]{:S(2)}) collective-permute-start(f32[512,128]{1,0:T(8,128)S(1)} %get-tuple-element.41.rest_5_), channel_id=1, source_target_pairs={{0,1},{1,0},{2,3},{3,2},{4,5},{5,4},{6,7},{7,6},{8,9},{9,8},{10,11... | collective-permute-start | bytes 786440 | tf_op jit(solution)/shard_map/ppermute | solution.py:252
  44.9 5.0 %collective-permute-start.9 = (f32[512,128]{1,0:T(8,128)S(1)}, f32[512,128]{1,0:T(8,128)S(1)}, u32[]{:S(2)}, u32[]{:S(2)}) collective-permute-start(f32[512,128]{1,0:T(8,128)S(1)} %collective-permute-done.8.rest_7_), channel_id=1, source_target_pairs={{0,1},{1,0},{2,3},{3,2},{4,5},{5,4},{6,7},{7,6},{8,9},{9,8},{10,11... | collective-permute-start | bytes 786440 | tf_op jit(solution)/shard_map/ppermute | solution.py:252
  46.4 3.5 %collective-permute-start.12 = (f32[64,128]{1,0:T(8,128)S(1)}, f32[64,128]{1,0:T(8,128)S(1)}, u32[]{:S(2)}, u32[]{:S(2)}) collective-permute-start(f32[64,128]{1,0:T(8,128)S(1)} %invert.1.rest_9_), channel_id=1, source_target_pairs={{0,3},{1,2},{2,1},{3,0},{4,7},{5,6},{6,5},{7,4},{8,11},{9,10},{10,... | collective-permute-start | bytes 98312 | tf_op jit(solution)/shard_map/ppermute | solution.py:252
  46.8 3.1 %collective-permute-start.11 = (f32[64,128]{1,0:T(8,128)S(1)}, f32[64,128]{1,0:T(8,128)S(1)}, u32[]{:S(2)}, u32[]{:S(2)}) collective-permute-start(f32[64,128]{1,0:T(8,128)S(1)} %invert.1.rest_9_), channel_id=1, source_target_pairs={{0,2},{1,3},{2,0},{3,1},{4,6},{5,7},{6,4},{7,5},{8,10},{9,11},{10,... | collective-permute-start | bytes 98312 | tf_op jit(solution)/shard_map/ppermute | solution.py:252
  47.8 2.1 %collective-permute-start.10 = (f32[64,128]{1,0:T(8,128)S(1)}, f32[64,128]{1,0:T(8,128)S(1)}, u32[]{:S(2)}, u32[]{:S(2)}) collective-permute-start(f32[64,128]{1,0:T(8,128)S(1)} %invert.1.rest_9_), channel_id=1, source_target_pairs={{0,1},{1,0},{2,3},{3,2},{4,5},{5,4},{6,7},{7,6},{8,9},{9,8},{10,11... | collective-permute-start | bytes 98312 | tf_op jit(solution)/shard_map/ppermute | solution.py:252
  53.4 19.1 %collective-permute-start.13 = (f32[4,64,128]{2,1,0:T(8,128)S(1)}, f32[4,64,128]{2,1,0:T(8,128)S(1)}, u32[]{:S(2)}, u32[]{:S(2)}) collective-permute-start(f32[4,64,128]{2,1,0:T(8,128)S(1)} %get-tuple-element.47), channel_id=1, source_target_pairs={{4,0},{5,1},{6,2},{7,3},{8,4},{9,5},{10,6},{11,7},{12,8},{13,9},{1... | collective-permute-start | bytes 393224 | tf_op jit(solution)/shard_map/ppermute | solution.py:247
  59.5 13.1 %collective-permute-start.14 = (f32[4,64,128]{2,1,0:T(8,128)S(1)}, f32[4,64,128]{2,1,0:T(8,128)S(1)}, u32[]{:S(2)}, u32[]{:S(2)}) collective-permute-start(f32[4,64,128]{2,1,0:T(8,128)S(1)} %get-tuple-element.48), channel_id=1, source_target_pairs={{8,0},{9,1},{10,2},{11,3},{12,4},{13,5},{14,6},{15,7},{16,8},{17,9... | collective-permute-start | bytes 393224 | tf_op jit(solution)/shard_map/ppermute | solution.py:247
  62.0 10.6 %collective-permute-start.15 = (f32[4,64,128]{2,1,0:T(8,128)S(1)}, f32[4,64,128]{2,1,0:T(8,128)S(1)}, u32[]{:S(2)}, u32[]{:S(2)}) collective-permute-start(f32[4,64,128]{2,1,0:T(8,128)S(1)} %get-tuple-element.49), channel_id=1, source_target_pairs={{12,0},{13,1},{14,2},{15,3},{16,4},{17,5},{18,6},{19,7},{20,8},{21... | collective-permute-start | bytes 393224 | tf_op jit(solution)/shard_map/ppermute | solution.py:247
  63.9 8.7 %collective-permute-start.16 = (f32[4,64,128]{2,1,0:T(8,128)S(1)}, f32[4,64,128]{2,1,0:T(8,128)S(1)}, u32[]{:S(2)}, u32[]{:S(2)}) collective-permute-start(f32[4,64,128]{2,1,0:T(8,128)S(1)} %get-tuple-element.50), channel_id=1, source_target_pairs={{16,0},{17,1},{18,2},{19,3},{20,4},{21,5},{22,6},{23,7},{24,8},{25... | collective-permute-start | bytes 393224 | tf_op jit(solution)/shard_map/ppermute | solution.py:247
  72.6 4.2 %collective-permute-start.17 = (f32[64,128]{1,0:T(8,128)S(1)}, f32[64,128]{1,0:T(8,128)S(1)}, u32[]{:S(2)}, u32[]{:S(2)}) collective-permute-start(f32[64,128]{1,0:T(8,128)S(1)} %get-tuple-element.52), channel_id=1, source_target_pairs={{0,1},{1,0},{2,3},{3,2},{4,5},{5,4},{6,7},{7,6},{8,9},{9,8},{10,11... | collective-permute-start | bytes 98312 | tf_op jit(solution)/shard_map/ppermute | solution.py:252
  74.5 2.8 %collective-permute-start.18 = (f32[64,128]{1,0:T(8,128)S(1)}, f32[64,128]{1,0:T(8,128)S(1)}, u32[]{:S(2)}, u32[]{:S(2)}) collective-permute-start(f32[64,128]{1,0:T(8,128)S(1)} %get-tuple-element.53), channel_id=1, source_target_pairs={{0,2},{1,3},{2,0},{3,1},{4,6},{5,7},{6,4},{7,5},{8,10},{9,11},{10,... | collective-permute-start | bytes 98312 | tf_op jit(solution)/shard_map/ppermute | solution.py:252
  75.5 3.3 %collective-permute-start.19 = (f32[64,128]{1,0:T(8,128)S(1)}, f32[64,128]{1,0:T(8,128)S(1)}, u32[]{:S(2)}, u32[]{:S(2)}) collective-permute-start(f32[64,128]{1,0:T(8,128)S(1)} %get-tuple-element.54), channel_id=1, source_target_pairs={{0,3},{1,2},{2,1},{3,0},{4,7},{5,6},{6,5},{7,4},{8,11},{9,10},{10,... | collective-permute-start | bytes 98312 | tf_op jit(solution)/shard_map/ppermute | solution.py:252

commit v3 on v2

--- a/solution.py
+++ b/solution.py
@@ -70,6 +70,10 @@
 def kernel_value(dx, dy):
     s = SQRT_THREE * jnp.sqrt(dx * dx + dy * dy)
     return (1.0 + s) * jnp.exp(-s)
+
+
+def place_of(me, device):
+    return (lax.div(me, SLAB) - lax.div(device, SLAB)) * SLAB + (lax.rem(device, SLAB) ^ lax.rem(me, SLAB))
 
 
 def factor_kernel(where_ref, nb_ref, coords_ref, g_ref, s_ref):
@@ -135,13 +139,15 @@
                 total = total - dot(panels[b][k, j], solved[b][j])
             solved[b][k] = total
     schur = [m[STEPS, STEPS] for m in mats]
+    schur_inv = inverses(schur)
+    g_ref[COND:, :] = jnp.concatenate(schur_inv, axis=1)
     for k in range(STEPS):
         g_ref[k * WIDE : (k + 1) * WIDE, :] = -jnp.concatenate([s[k] for s in solved], axis=1)
     s_ref[...] = jnp.concatenate(schur, axis=1)
 
 
 def apply_kernel(where_ref, ids_ref, *rest):
-    windows, w_refs, v_refs, outs = rest[:WINDOW], rest[WINDOW : WINDOW + SLAB], rest[WINDOW + SLAB : WINDOW + 2 * SLAB], rest[WINDOW + 2 * SLAB : -2]
+    windows, w_refs, outs = rest[:WINDOW], rest[WINDOW : WINDOW + SLAB], rest[WINDOW + SLAB : -2]
     held, total = rest[-2], rest[-1]
     me = where_ref[0]
     slab, quarter = lax.div(me, SLAB), lax.rem(me, SLAB)
@@ -159,7 +165,7 @@
                 ident = ids_ref[sender, b, m]
                 ident = jnp.where(ident >= 0, ident, device * BLK)
                 owner = lax.div(ident, BLK)
-                place = (slab - lax.div(owner, SLAB)) * SLAB + (lax.rem(owner, SLAB) ^ quarter)
+                place = place_of(me, owner)
                 turn = (lax.rem(ident, BLK) ^ (m % 2)) * PTS
                 places.append((place, turn))
         gathered = []
@@ -171,10 +177,10 @@
                 second = pltpu.roll(held[p1], t1, 1)
                 pieces.append(jnp.where(low, first, second))
             gathered.append(jnp.concatenate(pieces, axis=1))
-        w = w_refs[k][...]
+        w = w_refs[k][:COND, :]
         white = quick(jnp.concatenate(gathered, axis=0), w)
         white = held[k] + jnp.where(low, white[:PTS], white[PTS:])
-        v = v_refs[k][...]
+        v = w_refs[k][COND:, :]
         inv = jnp.concatenate([jnp.where(low, v, 0.0), jnp.where(low, 0.0, v)], axis=0)
         scaled = dot(white, inv)
         total[k] += scaled
@@ -190,10 +196,6 @@
         outs[o][...] = total[o * SLAB : (o + 1) * SLAB]
 
 
-def invert_kernel(s_ref, v_ref):
-    v_ref[...] = jnp.concatenate(inverses([s_ref[:, b * PTS : (b + 1) * PTS] for b in range(BLK)]), axis=1)
-
-
 def logdet_kernel(s_ref, out_ref, work):
     work[...] = s_ref[...]
     rows = iota((PTS, WIDE), 0)
@@ -284,37 +286,36 @@
         [smem, vmem, vmem, vmem],
         [pltpu.VMEM((8, WIDE), F32)],
     )(here, coords, neighbours, probes)
+    own = jnp.stack([pieces[0]] + [swapped(pieces[k], k) for k in range(1, SLAB)])
     everywhere = lax.all_to_all(told, AXES, 0, 0)
-    own = jnp.stack([pieces[0]] + [swapped(pieces[k], k) for k in range(1, SLAB)])
     ids = lax.dynamic_slice(everywhere, (device // SLAB * SLAB, 2, 0), (SLAB, BLK, NEIGH)).astype(jnp.int32)
-    window = [own] + [passed(own, SLAB * o) for o in range(1, WINDOW)]
-
+    early = [passed(own, SLAB * o) for o in (3, 2)]
     w, schur = local(
         factor_kernel,
         "factor",
-        (jax.ShapeDtypeStruct((COND, WIDE), F32), square),
+        (jax.ShapeDtypeStruct((COND + PTS, WIDE), F32), square),
         [smem, smem, vmem],
-        gflops=16,
+        gflops=14,
     )(here, neighbours, everywhere)
-    w, schur, *window = lax.optimization_barrier((w, schur, *window))
+    w, own, *early = lax.optimization_barrier((w, own, *early))
     w_y = swapped(w, 2)
+    late = [passed(own, SLAB), passed(own, SPAN)]
     w_d = swapped(w, 1)
-    v = local(invert_kernel, "invert", square, [vmem], gflops=3)(schur)
-    v_d, v_y, v_yd = (swapped(v, k) for k in range(1, SLAB))
-    w_y, v = lax.optimization_barrier((w_y, v))
+    w_y, *late = lax.optimization_barrier((w_y, *late))
+    window = [own, late[0], early[1], early[0], late[1]]
     w_yd = swapped(w_y, 1)
     terms = local(
         apply_kernel,
         "apply",
         (tiles,) * WINDOW,
-        [smem, smem] + [vmem] * (WINDOW + 2 * SLAB),
+        [smem, smem] + [vmem] * (WINDOW + SLAB),
         [pltpu.VMEM((WINDOW * SLAB, quarter, WIDE), F32)] * 2,
         gflops=4,
-    )(here, ids, *window, w, w_d, w_y, w_yd, v, v_d, v_y, v_yd)
+    )(here, ids, *window, w, w_d, w_y, w_yd)
     logs = local(
         logdet_kernel, "logdet", jax.ShapeDtypeStruct((8, WIDE), F32), [vmem], [pltpu.VMEM((PTS, WIDE), F32)], gflops=9
     )(schur)
-    returned = [passed(terms[o], -SLAB * o) for o in range(1, WINDOW)]
+    returned = [passed(terms[o], -SLAB * o) for o in (3, 2, 4, 1)]
     kept, logs = lax.optimization_barrier((terms[0], logs))
     sums = local(sum_kernel, "sum", (tile,) * SLAB, [vmem] * WINDOW)(kept, *returned)
     result = local(place_kernel, "place", jax.ShapeDtypeStruct(probes.shape, F32), [smem] + [vmem] * SLAB)(

time: 80.1 us -> 75.1 us (0.938)
  starting transfers between devices: 39.1 us -> 34.5 us
    ppermute x8, waiting for transfers between devices: 0.02 us -> 4.8 us  [passed(): lax.ppermute(value, AXES, [(i, i + by) for i in range(size) if 0 <= i + b...]
    ppermute x12 -> x9, waiting for transfers between devices: 10.9 us -> 6.23 us  [swapped(): return lax.ppermute(value, AXES, [(i, i ^ mask) for i in range(size)])]
    ppermute x8, starting transfers between devices: 21.7 us -> 19.2 us  [passed(): lax.ppermute(value, AXES, [(i, i + by) for i in range(size) if 0 <= i + b...]
    ppermute x12 -> x9, starting transfers between devices: 11 us -> 8.8 us  [swapped(): return lax.ppermute(value, AXES, [(i, i ^ mask) for i in range(size)])]
    pallas_call x2 -> x1, Pallas kernels: 14.3 us -> 14.1 us  [shards(): local(factor_kernel, 'factor', (jax.ShapeDtypeStruct((COND + PTS, WIDE),...]
  transfers between devices with their start and end apart: 21 -> 18, of which waited for: 6 -> 7; matrix products, arithmetic and copies ran while one was open for 1% -> 1% of each run, Pallas kernels for 27% -> 29%
where the time goes in v3:
time: 75.1 us; the launch traced here: 74.8 us
  starting transfers between devices  34.5 us (46%)
  Pallas kernels  26.3 us (35%)
  waiting for transfers between devices  11 us (15%)
  local copies, waits for them, and re-layouts  2.17 us (3%)
  between operations  0.81 us (1%)
    ppermute x8, starting transfers between devices, passed(): lax.ppermute(value, AXES, [(i, i + by) for i in range(size) if 0 <= i + b...  19.2 us
    pallas_call x1, Pallas kernels, shards(): local(factor_kernel, 'factor', (jax.ShapeDtypeStruct((COND + PTS, WIDE),...  14.1 us
    ppermute x9, starting transfers between devices, swapped(): return lax.ppermute(value, AXES, [(i, i ^ mask) for i in range(size)])  8.8 us
    pallas_call x1, Pallas kernels, shards(): local(logdet_kernel, 'logdet', jax.ShapeDtypeStruct((8, WIDE), F32), [vme...  7.31 us
    all_to_all x1, starting transfers between devices, shards(): everywhere = lax.all_to_all(told, AXES, 0, 0)  6.44 us
    ppermute x9, waiting for transfers between devices, swapped(): return lax.ppermute(value, AXES, [(i, i ^ mask) for i in range(size)])  6.23 us
    ppermute x8, waiting for transfers between devices, passed(): lax.ppermute(value, AXES, [(i, i + by) for i in range(size) if 0 <= i + b...  4.8 us
    pallas_call x1, Pallas kernels, shards(): local(apply_kernel, 'apply', (tiles,) * WINDOW, [smem, smem] + [vmem] * (...  3.42 us
  transfers between devices with their start and end apart: 18, of which 7 were waited for; matrix products, arithmetic and copies ran while one was open for 1% of the time, Pallas kernels for 29%

profile of v3, /device:TPU:3, one launch (start us, length us, event | category | flops | bytes accessed | tf_op | source)
XLA Modules:
  0.0 74.8 jit_solution(7824487867901993919)
XLA Ops:
  0.6 0.0 copy-start.2
  0.6 0.0 copy-start.1
  0.7 0.7 copy-done.2
  1.3 0.0 copy-done.1
  1.3 0.0 copy-start
  1.3 0.9 %copy-done = f32[256,128]{1,0:T(8,128)S(1)} copy-done((f32[256,128]{1,0:T(8,128)S(1)}, f32[256,128]{1,0:T(8,128)}, u32[]{:S(2)}) %copy-start) | copy-done | bytes 131096
  2.2 0.7 prepare.1
  2.9 6.4 %all-to-all-start = ((f32[32,8,128]{2,1,0:T(8,128)}), f32[32,8,128]{2,1,0:T(8,128)S(1)}, u32[]{:S(2)}, u32[]{:S(2)}) async-start(f32[32,8,128]{2,1,0:T(8,128)} %get-tuple-element.27), calls=%async_computation | async-start | bytes 262144 | tf_op jit(solution)/shard_map/all_to_all | solution.py:290
  9.4 0.4 collective-permute-start
  9.8 1.2 %collective-permute-start.1 = (f32[64,128]{1,0:T(8,128)S(1)}, f32[64,128]{1,0:T(8,128)S(1)}, u32[]{:S(2)}, u32[]{:S(2)}) collective-permute-start(f32[64,128]{1,0:T(8,128)S(1)} %get-tuple-element.31), channel_id=1, source_target_pairs={{0,2},{1,3},{2,0},{3,1},{4,6},{5,7},{6,4},{7,5},{8,10},{9,11},{10,... | collective-permute-start | bytes 98312 | tf_op jit(solution)/shard_map/ppermute | solution.py:254
  11.0 0.6 collective-permute-start.2
  11.6 0.0 collective-permute-done
  11.6 1.5 %collective-permute-done.1 = f32[64,128]{1,0:T(8,128)S(1)} collective-permute-done((f32[64,128]{1,0:T(8,128)S(1)}, f32[64,128]{1,0:T(8,128)S(1)}, u32[]{:S(2)}, u32[]{:S(2)}) %collective-permute-start.1) | collective-permute-done | bytes 32800 | tf_op jit(solution)/shard_map/ppermute | solution.py:254
  13.0 1.9 %collective-permute-done.2 = f32[64,128]{1,0:T(8,128)S(1)} collective-permute-done((f32[64,128]{1,0:T(8,128)S(1)}, f32[64,128]{1,0:T(8,128)S(1)}, u32[]{:S(2)}, u32[]{:S(2)}) %collective-permute-start.2) | collective-permute-done | bytes 32800 | tf_op jit(solution)/shard_map/ppermute | solution.py:254
  14.9 4.0 %collective-permute-start.4 = (f32[4,64,128]{2,1,0:T(8,128)S(1)}, f32[4,64,128]{2,1,0:T(8,128)S(1)}, u32[]{:S(2)}, u32[]{:S(2)}) collective-permute-start(f32[4,64,128]{2,1,0:T(8,128)S(1)} %pad_maximum_fusion.rest_0_), channel_id=1, source_target_pairs={{0,8},{1,9},{2,10},{3,11},{4,12},{5,13},{6,14},{7,15},{8,16},{9,17... | collective-permute-start | bytes 393224 | tf_op jit(solution)/shard_map/ppermute | solution.py:249
  18.9 2.1 %collective-permute-start.3 = (f32[4,64,128]{2,1,0:T(8,128)S(1)}, f32[4,64,128]{2,1,0:T(8,128)S(1)}, u32[]{:S(2)}, u32[]{:S(2)}) collective-permute-start(f32[4,64,128]{2,1,0:T(8,128)S(1)} %pad_maximum_fusion.rest_0_), channel_id=1, source_target_pairs={{0,12},{1,13},{2,14},{3,15},{4,16},{5,17},{6,18},{7,19},{8,20},{9,... | collective-permute-start | bytes 393224 | tf_op jit(solution)/shard_map/ppermute | solution.py:249
  21.0 0.0 all-to-all-done.coords_ref
  21.0 14.1 %factor.1 = (f32[576,128]{1,0:T(8,128)S(1)}, f32[64,128]{1,0:T(8,128)S(1)}) custom-call(s32[1]{0:T(128)} %bitcast.where_ref, s32[2,8]{1,0:T(2,128)S(1)} %copy-done.2, f32[32,8,128]{2,1,0:T(8,128)S(1)} %all-to-all-done.coords_ref), custom_call_target="tpu_custom_call" | custom-call | flops 14000000000 | bytes 100000 | tf_op jit(solution)/shard_map/factor/pallas_call | solution.py:293
  35.1 0.0 collective-permute-done.4.rest_2_
  35.1 0.0 collective-permute-done.3.rest_3_
  35.2 0.5 collective-permute-start.5
  35.7 1.3 %collective-permute-start.7 = (f32[4,64,128]{2,1,0:T(8,128)S(1)}, f32[4,64,128]{2,1,0:T(8,128)S(1)}, u32[]{:S(2)}, u32[]{:S(2)}) collective-permute-start(f32[4,64,128]{2,1,0:T(8,128)S(1)} %pad_maximum_fusion.rest_0_), channel_id=1, source_target_pairs={{0,16},{1,17},{2,18},{3,19},{4,20},{5,21},{6,22},{7,23},{8,24},{9,... | collective-permute-start | bytes 393224 | tf_op jit(solution)/shard_map/ppermute | solution.py:249
  37.0 2.4 %collective-permute-start.6 = (f32[4,64,128]{2,1,0:T(8,128)S(1)}, f32[4,64,128]{2,1,0:T(8,128)S(1)}, u32[]{:S(2)}, u32[]{:S(2)}) collective-permute-start(f32[4,64,128]{2,1,0:T(8,128)S(1)} %pad_maximum_fusion.rest_0_), channel_id=1, source_target_pairs={{0,4},{1,5},{2,6},{3,7},{4,8},{5,9},{6,10},{7,11},{8,12},{9,13},{1... | collective-permute-start | bytes 393224 | tf_op jit(solution)/shard_map/ppermute | solution.py:249
  39.4 1.2 %collective-permute-start.8 = (f32[576,128]{1,0:T(8,128)S(1)}, f32[576,128]{1,0:T(8,128)S(1)}, u32[]{:S(2)}, u32[]{:S(2)}) collective-permute-start(f32[576,128]{1,0:T(8,128)S(1)} %get-tuple-element.34.rest_5_), channel_id=1, source_target_pairs={{0,1},{1,0},{2,3},{3,2},{4,5},{5,4},{6,7},{7,6},{8,9},{9,8},{10,11... | collective-permute-start | bytes 884744 | tf_op jit(solution)/shard_map/ppermute | solution.py:254
  40.6 1.9 %collective-permute-done.7.rest_4_ = f32[4,64,128]{2,1,0:T(8,128)S(1)} collective-permute-done((f32[4,64,128]{2,1,0:T(8,128)S(1)}, f32[4,64,128]{2,1,0:T(8,128)S(1)}, u32[]{:S(2)}, u32[]{:S(2)}) %collective-permute-start.7) | collective-permute-done | bytes 131104 | tf_op jit(solution)/shard_map/ppermute | solution.py:249
  42.5 2.9 %collective-permute-done.6.rest_1_ = f32[4,64,128]{2,1,0:T(8,128)S(1)} collective-permute-done((f32[4,64,128]{2,1,0:T(8,128)S(1)}, f32[4,64,128]{2,1,0:T(8,128)S(1)}, u32[]{:S(2)}, u32[]{:S(2)}) %collective-permute-start.6) | collective-permute-done | bytes 131104 | tf_op jit(solution)/shard_map/ppermute | solution.py:249
  45.4 0.0 collective-permute-done.5.rest_7_
  45.4 2.1 %collective-permute-start.9 = (f32[576,128]{1,0:T(8,128)S(1)}, f32[576,128]{1,0:T(8,128)S(1)}, u32[]{:S(2)}, u32[]{:S(2)}) collective-permute-start(f32[576,128]{1,0:T(8,128)S(1)} %collective-permute-done.5.rest_7_), channel_id=1, source_target_pairs={{0,1},{1,0},{2,3},{3,2},{4,5},{5,4},{6,7},{7,6},{8,9},{9,8},{10,11... | collective-permute-start | bytes 884744 | tf_op jit(solution)/shard_map/ppermute | solution.py:254
  47.5 0.0 collective-permute-done.8.rest_6_
  47.5 1.2 %collective-permute-done.9.rest_8_ = f32[576,128]{1,0:T(8,128)S(1)} collective-permute-done((f32[576,128]{1,0:T(8,128)S(1)}, f32[576,128]{1,0:T(8,128)S(1)}, u32[]{:S(2)}, u32[]{:S(2)}) %collective-permute-start.9) | collective-permute-done | bytes 294944 | tf_op jit(solution)/shard_map/ppermute | solution.py:254
  48.7 3.4 %apply.1 = (f32[4,64,128]{2,1,0:T(8,128)S(1)}, f32[4,64,128]{2,1,0:T(8,128)S(1)}, f32[4,64,128]{2,1,0:T(8,128)S(1)}, f32[4,64,128]{2,1,0:T(8,128)S(1)}, f32[4,64,128]{2,1,0:T(8,128)S(1)}) custom-call(s32[1]{0:T(128)} %bitcast.where_ref, s32[4,2,8]{2,1,0:T(2,128)S(1)} %dynamic-slice_convert_fusion.ids_ref, f32[4,64,128]{2,1,0:T(8,128)S(1)} %pad_maximum_fusion.rest_0_, ...), custom_call_target="tpu_custom_call" | custom-call | flops 4000000000 | bytes 100000 | tf_op jit(solution)/shard_map/apply/pallas_call | solution.py:307
  52.1 1.9 %collective-permute-start.10 = (f32[4,64,128]{2,1,0:T(8,128)S(1)}, f32[4,64,128]{2,1,0:T(8,128)S(1)}, u32[]{:S(2)}, u32[]{:S(2)}) collective-permute-start(f32[4,64,128]{2,1,0:T(8,128)S(1)} %get-tuple-element.43), channel_id=1, source_target_pairs={{12,0},{13,1},{14,2},{15,3},{16,4},{17,5},{18,6},{19,7},{20,8},{21... | collective-permute-start | bytes 393224 | tf_op jit(solution)/shard_map/ppermute | solution.py:249
  54.1 1.9 %collective-permute-start.11 = (f32[4,64,128]{2,1,0:T(8,128)S(1)}, f32[4,64,128]{2,1,0:T(8,128)S(1)}, u32[]{:S(2)}, u32[]{:S(2)}) collective-permute-start(f32[4,64,128]{2,1,0:T(8,128)S(1)} %get-tuple-element.44), channel_id=1, source_target_pairs={{8,0},{9,1},{10,2},{11,3},{12,4},{13,5},{14,6},{15,7},{16,8},{17,9... | collective-permute-start | bytes 393224 | tf_op jit(solution)/shard_map/ppermute | solution.py:249
  56.0 1.3 %collective-permute-start.12 = (f32[4,64,128]{2,1,0:T(8,128)S(1)}, f32[4,64,128]{2,1,0:T(8,128)S(1)}, u32[]{:S(2)}, u32[]{:S(2)}) collective-permute-start(f32[4,64,128]{2,1,0:T(8,128)S(1)} %get-tuple-element.45), channel_id=1, source_target_pairs={{16,0},{17,1},{18,2},{19,3},{20,4},{21,5},{22,6},{23,7},{24,8},{25... | collective-permute-start | bytes 393224 | tf_op jit(solution)/shard_map/ppermute | solution.py:249
  57.3 4.4 %collective-permute-start.13 = (f32[4,64,128]{2,1,0:T(8,128)S(1)}, f32[4,64,128]{2,1,0:T(8,128)S(1)}, u32[]{:S(2)}, u32[]{:S(2)}) collective-permute-start(f32[4,64,128]{2,1,0:T(8,128)S(1)} %get-tuple-element.46), channel_id=1, source_target_pairs={{4,0},{5,1},{6,2},{7,3},{8,4},{9,5},{10,6},{11,7},{12,8},{13,9},{1... | collective-permute-start | bytes 393224 | tf_op jit(solution)/shard_map/ppermute | solution.py:249
  61.7 7.3 %logdet.1 = f32[8,128]{1,0:T(8,128)S(1)} custom-call(f32[64,128]{1,0:T(8,128)S(1)} %get-tuple-element.41.s_ref), custom_call_target="tpu_custom_call" | custom-call | flops 8999999488 | bytes 100000 | tf_op jit(solution)/shard_map/logdet/pallas_call | solution.py:315
  69.0 0.0 collective-permute-done.10.refs_1_
  69.0 0.0 collective-permute-done.11.refs_2_
  69.0 0.0 collective-permute-done.12.refs_3_
  69.0 0.0 collective-permute-done.13.refs_4_
  69.0 0.1 sum.1
  69.1 1.0 %collective-permute-start.14 = (f32[64,128]{1,0:T(8,128)S(1)}, f32[64,128]{1,0:T(8,128)S(1)}, u32[]{:S(2)}, u32[]{:S(2)}) collective-permute-start(f32[64,128]{1,0:T(8,128)S(1)} %get-tuple-element.48), channel_id=1, source_target_pairs={{0,1},{1,0},{2,3},{3,2},{4,5},{5,4},{6,7},{7,6},{8,9},{9,8},{10,11... | collective-permute-start | bytes 98312 | tf_op jit(solution)/shard_map/ppermute | solution.py:254
  70.1 0.7 collective-permute-start.15
  70.8 1.0 %collective-permute-start.16 = (f32[64,128]{1,0:T(8,128)S(1)}, f32[64,128]{1,0:T(8,128)S(1)}, u32[]{:S(2)}, u32[]{:S(2)}) collective-permute-start(f32[64,128]{1,0:T(8,128)S(1)} %get-tuple-element.50), channel_id=1, source_target_pairs={{0,3},{1,2},{2,1},{3,0},{4,7},{5,6},{6,5},{7,4},{8,11},{9,10},{10,... | collective-permute-start | bytes 98312 | tf_op jit(solution)/shard_map/ppermute | solution.py:254
  71.8 0.6 slice.3
  72.4 0.0 collective-permute-done.14.refs_1_
  72.4 0.5 collective-permute-done.15.refs_2_
  72.9 1.2 %collective-permute-done.16.refs_3_ = f32[64,128]{1,0:T(8,128)S(1)} collective-permute-done((f32[64,128]{1,0:T(8,128)S(1)}, f32[64,128]{1,0:T(8,128)S(1)}, u32[]{:S(2)}, u32[]{:S(2)}) %collective-permute-start.16) | collective-permute-done | bytes 32800 | tf_op jit(solution)/shard_map/ppermute | solution.py:254
  74.1 0.7 place.1
  (2 shorter events, 0.0 us)
Async XLA Ops:
  0.6 0.7 copy-start.2
  0.6 0.7 copy-start.1
  1.3 0.9 %copy-start = (f32[256,128]{1,0:T(8,128)S(1)}, f32[256,128]{1,0:T(8,128)}, u32[]{:S(2)}) copy-start(f32[256,128]{1,0:T(8,128)} %probes_ref.1) | copy-start | bytes 393220
  2.9 18.1 %all-to-all-start = ((f32[32,8,128]{2,1,0:T(8,128)}), f32[32,8,128]{2,1,0:T(8,128)S(1)}, u32[]{:S(2)}, u32[]{:S(2)}) async-start(f32[32,8,128]{2,1,0:T(8,128)} %get-tuple-element.27), calls=%async_computation | async-start | bytes 262144 | tf_op jit(solution)/shard_map/all_to_all | solution.py:290
  9.4 2.2 %collective-permute-start = (f32[64,128]{1,0:T(8,128)S(1)}, f32[64,128]{1,0:T(8,128)S(1)}, u32[]{:S(2)}, u32[]{:S(2)}) collective-permute-start(f32[64,128]{1,0:T(8,128)S(1)} %get-tuple-element.30), channel_id=1, source_target_pairs={{0,1},{1,0},{2,3},{3,2},{4,5},{5,4},{6,7},{7,6},{8,9},{9,8},{10,11... | collective-permute-start | bytes 98312 | tf_op jit(solution)/shard_map/ppermute | solution.py:254
  9.8 3.3 %collective-permute-start.1 = (f32[64,128]{1,0:T(8,128)S(1)}, f32[64,128]{1,0:T(8,128)S(1)}, u32[]{:S(2)}, u32[]{:S(2)}) collective-permute-start(f32[64,128]{1,0:T(8,128)S(1)} %get-tuple-element.31), channel_id=1, source_target_pairs={{0,2},{1,3},{2,0},{3,1},{4,6},{5,7},{6,4},{7,5},{8,10},{9,11},{10,... | collective-permute-start | bytes 98312 | tf_op jit(solution)/shard_map/ppermute | solution.py:254
  11.0 3.9 %collective-permute-start.2 = (f32[64,128]{1,0:T(8,128)S(1)}, f32[64,128]{1,0:T(8,128)S(1)}, u32[]{:S(2)}, u32[]{:S(2)}) collective-permute-start(f32[64,128]{1,0:T(8,128)S(1)} %get-tuple-element.32), channel_id=1, source_target_pairs={{0,3},{1,2},{2,1},{3,0},{4,7},{5,6},{6,5},{7,4},{8,11},{9,10},{10,... | collective-permute-start | bytes 98312 | tf_op jit(solution)/shard_map/ppermute | solution.py:254
  14.9 20.2 %collective-permute-start.4 = (f32[4,64,128]{2,1,0:T(8,128)S(1)}, f32[4,64,128]{2,1,0:T(8,128)S(1)}, u32[]{:S(2)}, u32[]{:S(2)}) collective-permute-start(f32[4,64,128]{2,1,0:T(8,128)S(1)} %pad_maximum_fusion.rest_0_), channel_id=1, source_target_pairs={{0,8},{1,9},{2,10},{3,11},{4,12},{5,13},{6,14},{7,15},{8,16},{9,17... | collective-permute-start | bytes 393224 | tf_op jit(solution)/shard_map/ppermute | solution.py:249
  18.9 16.2 %collective-permute-start.3 = (f32[4,64,128]{2,1,0:T(8,128)S(1)}, f32[4,64,128]{2,1,0:T(8,128)S(1)}, u32[]{:S(2)}, u32[]{:S(2)}) collective-permute-start(f32[4,64,128]{2,1,0:T(8,128)S(1)} %pad_maximum_fusion.rest_0_), channel_id=1, source_target_pairs={{0,12},{1,13},{2,14},{3,15},{4,16},{5,17},{6,18},{7,19},{8,20},{9,... | collective-permute-start | bytes 393224 | tf_op jit(solution)/shard_map/ppermute | solution.py:249
  35.2 10.2 %collective-permute-start.5 = (f32[576,128]{1,0:T(8,128)S(1)}, f32[576,128]{1,0:T(8,128)S(1)}, u32[]{:S(2)}, u32[]{:S(2)}) collective-permute-start(f32[576,128]{1,0:T(8,128)S(1)} %get-tuple-element.34.rest_5_), channel_id=1, source_target_pairs={{0,2},{1,3},{2,0},{3,1},{4,6},{5,7},{6,4},{7,5},{8,10},{9,11},{10,... | collective-permute-start | bytes 884744 | tf_op jit(solution)/shard_map/ppermute | solution.py:254
  35.7 6.8 %collective-permute-start.7 = (f32[4,64,128]{2,1,0:T(8,128)S(1)}, f32[4,64,128]{2,1,0:T(8,128)S(1)}, u32[]{:S(2)}, u32[]{:S(2)}) collective-permute-start(f32[4,64,128]{2,1,0:T(8,128)S(1)} %pad_maximum_fusion.rest_0_), channel_id=1, source_target_pairs={{0,16},{1,17},{2,18},{3,19},{4,20},{5,21},{6,22},{7,23},{8,24},{9,... | collective-permute-start | bytes 393224 | tf_op jit(solution)/shard_map/ppermute | solution.py:249
  37.0 8.4 %collective-permute-start.6 = (f32[4,64,128]{2,1,0:T(8,128)S(1)}, f32[4,64,128]{2,1,0:T(8,128)S(1)}, u32[]{:S(2)}, u32[]{:S(2)}) collective-permute-start(f32[4,64,128]{2,1,0:T(8,128)S(1)} %pad_maximum_fusion.rest_0_), channel_id=1, source_target_pairs={{0,4},{1,5},{2,6},{3,7},{4,8},{5,9},{6,10},{7,11},{8,12},{9,13},{1... | collective-permute-start | bytes 393224 | tf_op jit(solution)/shard_map/ppermute | solution.py:249
  39.4 8.1 %collective-permute-start.8 = (f32[576,128]{1,0:T(8,128)S(1)}, f32[576,128]{1,0:T(8,128)S(1)}, u32[]{:S(2)}, u32[]{:S(2)}) collective-permute-start(f32[576,128]{1,0:T(8,128)S(1)} %get-tuple-element.34.rest_5_), channel_id=1, source_target_pairs={{0,1},{1,0},{2,3},{3,2},{4,5},{5,4},{6,7},{7,6},{8,9},{9,8},{10,11... | collective-permute-start | bytes 884744 | tf_op jit(solution)/shard_map/ppermute | solution.py:254
  45.4 3.3 %collective-permute-start.9 = (f32[576,128]{1,0:T(8,128)S(1)}, f32[576,128]{1,0:T(8,128)S(1)}, u32[]{:S(2)}, u32[]{:S(2)}) collective-permute-start(f32[576,128]{1,0:T(8,128)S(1)} %collective-permute-done.5.rest_7_), channel_id=1, source_target_pairs={{0,1},{1,0},{2,3},{3,2},{4,5},{5,4},{6,7},{7,6},{8,9},{9,8},{10,11... | collective-permute-start | bytes 884744 | tf_op jit(solution)/shard_map/ppermute | solution.py:254
  52.1 16.9 %collective-permute-start.10 = (f32[4,64,128]{2,1,0:T(8,128)S(1)}, f32[4,64,128]{2,1,0:T(8,128)S(1)}, u32[]{:S(2)}, u32[]{:S(2)}) collective-permute-start(f32[4,64,128]{2,1,0:T(8,128)S(1)} %get-tuple-element.43), channel_id=1, source_target_pairs={{12,0},{13,1},{14,2},{15,3},{16,4},{17,5},{18,6},{19,7},{20,8},{21... | collective-permute-start | bytes 393224 | tf_op jit(solution)/shard_map/ppermute | solution.py:249
  54.1 15.0 %collective-permute-start.11 = (f32[4,64,128]{2,1,0:T(8,128)S(1)}, f32[4,64,128]{2,1,0:T(8,128)S(1)}, u32[]{:S(2)}, u32[]{:S(2)}) collective-permute-start(f32[4,64,128]{2,1,0:T(8,128)S(1)} %get-tuple-element.44), channel_id=1, source_target_pairs={{8,0},{9,1},{10,2},{11,3},{12,4},{13,5},{14,6},{15,7},{16,8},{17,9... | collective-permute-start | bytes 393224 | tf_op jit(solution)/shard_map/ppermute | solution.py:249
  56.0 13.0 %collective-permute-start.12 = (f32[4,64,128]{2,1,0:T(8,128)S(1)}, f32[4,64,128]{2,1,0:T(8,128)S(1)}, u32[]{:S(2)}, u32[]{:S(2)}) collective-permute-start(f32[4,64,128]{2,1,0:T(8,128)S(1)} %get-tuple-element.45), channel_id=1, source_target_pairs={{16,0},{17,1},{18,2},{19,3},{20,4},{21,5},{22,6},{23,7},{24,8},{25... | collective-permute-start | bytes 393224 | tf_op jit(solution)/shard_map/ppermute | solution.py:249
  57.3 11.7 %collective-permute-start.13 = (f32[4,64,128]{2,1,0:T(8,128)S(1)}, f32[4,64,128]{2,1,0:T(8,128)S(1)}, u32[]{:S(2)}, u32[]{:S(2)}) collective-permute-start(f32[4,64,128]{2,1,0:T(8,128)S(1)} %get-tuple-element.46), channel_id=1, source_target_pairs={{4,0},{5,1},{6,2},{7,3},{8,4},{9,5},{10,6},{11,7},{12,8},{13,9},{1... | collective-permute-start | bytes 393224 | tf_op jit(solution)/shard_map/ppermute | solution.py:249
  69.1 3.3 %collective-permute-start.14 = (f32[64,128]{1,0:T(8,128)S(1)}, f32[64,128]{1,0:T(8,128)S(1)}, u32[]{:S(2)}, u32[]{:S(2)}) collective-permute-start(f32[64,128]{1,0:T(8,128)S(1)} %get-tuple-element.48), channel_id=1, source_target_pairs={{0,1},{1,0},{2,3},{3,2},{4,5},{5,4},{6,7},{7,6},{8,9},{9,8},{10,11... | collective-permute-start | bytes 98312 | tf_op jit(solution)/shard_map/ppermute | solution.py:254
  70.1 2.8 %collective-permute-start.15 = (f32[64,128]{1,0:T(8,128)S(1)}, f32[64,128]{1,0:T(8,128)S(1)}, u32[]{:S(2)}, u32[]{:S(2)}) collective-permute-start(f32[64,128]{1,0:T(8,128)S(1)} %get-tuple-element.49), channel_id=1, source_target_pairs={{0,2},{1,3},{2,0},{3,1},{4,6},{5,7},{6,4},{7,5},{8,10},{9,11},{10,... | collective-permute-start | bytes 98312 | tf_op jit(solution)/shard_map/ppermute | solution.py:254
  70.8 3.3 %collective-permute-start.16 = (f32[64,128]{1,0:T(8,128)S(1)}, f32[64,128]{1,0:T(8,128)S(1)}, u32[]{:S(2)}, u32[]{:S(2)}) collective-permute-start(f32[64,128]{1,0:T(8,128)S(1)} %get-tuple-element.50), channel_id=1, source_target_pairs={{0,3},{1,2},{2,1},{3,0},{4,7},{5,6},{6,5},{7,4},{8,11},{9,10},{10,... | collective-permute-start | bytes 98312 | tf_op jit(solution)/shard_map/ppermute | solution.py:254

commit v4 on v3

--- a/solution.py
+++ b/solution.py
@@ -49,22 +49,49 @@
     return 2.0 / (low + high), factors
 
 
-def inverses(mats):
-    n = mats[0].shape[0]
-    alpha, factors = schedule(0.245, n + 0.26)
-    ident = eye(n)
+def split(a):
+    high = a.astype(jnp.bfloat16)
+    return high, (a - high.astype(F32)).astype(jnp.bfloat16)
+
+
+def products(lefts, right):
+    high, low = split(right)
+    rows = [jnp.concatenate([h, low_part, h], axis=1) for h, low_part in map(split, lefts)]
+    out = lax.dot_general(
+        jnp.concatenate(rows, axis=0),
+        jnp.concatenate([high, high, low], axis=0),
+        (((1,), (0,)), ((), ())),
+        preferred_element_type=F32,
+    )
+    n = right.shape[0]
+    return [out[i * n : (i + 1) * n] for i in range(len(lefts))]
+
+
+def inverses(mats, top, tasks):
+    alpha, factors = schedule(0.245, top + 0.26)
+    stages = len(factors) + 1
+
+    def spread(stage):
+        for task in tasks[stage * len(tasks) // stages : (stage + 1) * len(tasks) // stages]:
+            task()
+
+    ident = eye(WIDE)
     rs = [ident - alpha * m for m in mats]
     c = factors[0]
     xs = [(alpha * c) * (ident + r) for r in rs]
-    rs = [(1.0 - c) * ident + c * quick(r, r) for r in rs]
-    for c in factors[1:-1]:
-        nxt = [c * (x + quick(x, r)) for x, r in zip(xs, rs)]
-        rs = [(1.0 - c) * ident + c * quick(r, r) for r in rs]
-        xs = nxt
+    rs = [(1.0 - c) * ident + c * products([r], r)[0] for r in rs]
+    spread(0)
+    for stage, c in enumerate(factors[1:-1]):
+        pairs = [products([x, r], r) for x, r in zip(xs, rs)]
+        xs = [c * (x + xr) for x, (xr, _) in zip(xs, pairs)]
+        rs = [(1.0 - c) * ident + c * rr for _, rr in pairs]
+        spread(stage + 1)
     c = factors[-1]
-    xs = [c * (x + quick(x, r)) for x, r in zip(xs, rs)]
+    xs = [c * (x + products([x], r)[0]) for x, r in zip(xs, rs)]
+    spread(stages - 2)
     es = [ident - dot(m, x) for m, x in zip(mats, xs)]
-    return [x + quick(x, e) for x, e in zip(xs, es)]
+    spread(stages - 1)
+    return [x + products([x], e)[0] for x, e in zip(xs, es)]
 
 
 def kernel_value(dx, dy):
@@ -90,7 +117,7 @@
     def column(row):
         return jnp.transpose(jnp.broadcast_to(row, (WIDE, WIDE)))
 
-    mats = []
+    points = []
     for b in range(BLK):
         rows, valid = [], []
         for k in range(STEPS):
@@ -108,41 +135,71 @@
         cols = [[column(r) for r in row] for row in rows]
         own_cols = [column(r)[:PTS, :PTS] for r in own]
         valid_cols = [column(v) for v in valid]
-        mat = {}
-        for i in range(STEPS):
-            for j in range(i, STEPS):
-                value = kernel_value(cols[i][0] - rows[j][0], cols[i][1] - rows[j][1])
-                value = valid_cols[i] * valid[j] * value
-                if i == j:
-                    value = value + eye(WIDE) * (NUGGET * valid[j] + (1.0 - valid[j]))
-                mat[i, j] = value
+        points.append((rows, valid, own, cols, own_cols, valid_cols))
+
+    mats = [{} for _ in range(BLK)]
+    panels = [{} for _ in range(BLK)]
+    solved = [{} for _ in range(BLK)]
+
+    def covariance(b, i, j):
+        rows, valid, own, cols, own_cols, valid_cols = points[b]
+        if i == STEPS:
+            value = kernel_value(own_cols[0] - own[0][:, :PTS], own_cols[1] - own[1][:, :PTS])
+            value = value + NUGGET * eye(PTS)
+        elif j == STEPS:
             value = kernel_value(cols[i][0][:, :PTS] - own[0][:, :PTS], cols[i][1][:, :PTS] - own[1][:, :PTS])
-            mat[i, STEPS] = valid_cols[i][:, :PTS] * value
-        value = kernel_value(own_cols[0] - own[0][:, :PTS], own_cols[1] - own[1][:, :PTS])
-        mat[STEPS, STEPS] = value + NUGGET * eye(PTS)
-        mats.append(mat)
-    panels = [{} for _ in range(BLK)]
+            value = valid_cols[i][:, :PTS] * value
+        else:
+            value = kernel_value(cols[i][0] - rows[j][0], cols[i][1] - rows[j][1])
+            value = valid_cols[i] * valid[j] * value
+            if i == j:
+                value = value + eye(WIDE) * (NUGGET * valid[j] + (1.0 - valid[j]))
+        mats[b][i, j] = value
+
+    def panel(b, k, j, inv):
+        panels[b][k, j] = dot(inv, mats[b][k, j])
+
+    def update(b, k, i, j):
+        mats[b][i, j] = mats[b][i, j] - dot(mats[b][k, i], panels[b][k, j], ((0,), (0,)))
+
+    def substitute(b, k):
+        total = panels[b][k, STEPS]
+        for j in range(k + 1, STEPS):
+            total = total - dot(panels[b][k, j], solved[b][j])
+        solved[b][k] = total
+
+    def store(k):
+        g_ref[k * WIDE : (k + 1) * WIDE, :] = -jnp.concatenate([s[k] for s in solved], axis=1)
+
+    blocks = range(BLK)
+    for i in range(STEPS + 1):
+        for j in range(i, STEPS + 1):
+            for b in blocks:
+                covariance(b, i, j)
+    tasks = []
     for k in range(STEPS):
-        invs = inverses([m[k, k] for m in mats])
-        for j in range(k + 1, STEPS + 1):
-            for b in range(BLK):
-                panels[b][k, j] = dot(invs[b], mats[b][k, j])
-        for i in range(k + 1, STEPS + 1):
-            for j in range(i, STEPS + 1):
-                for b in range(BLK):
-                    mats[b][i, j] = mats[b][i, j] - dot(mats[b][k, i], panels[b][k, j], ((0,), (0,)))
-    solved = [{} for _ in range(BLK)]
+        invs = inverses([m[k, k] for m in mats], WIDE, tasks)
+        for b in blocks:
+            panel(b, k, k + 1, invs[b])
+        for b in blocks:
+            update(b, k, k + 1, k + 1)
+        tasks = [functools.partial(panel, b, k, j, invs[b]) for j in range(k + 2, STEPS + 1) for b in blocks]
+        tasks += [
+            functools.partial(update, b, k, i, j)
+            for i in range(k + 1, STEPS + 1)
+            for j in range(i, STEPS + 1)
+            for b in blocks
+            if (i, j) != (k + 1, k + 1)
+        ]
     for k in reversed(range(STEPS)):
-        for b in range(BLK):
-            total = panels[b][k, STEPS]
-            for j in range(k + 1, STEPS):
-                total = total - dot(panels[b][k, j], solved[b][j])
-            solved[b][k] = total
+        tasks += [functools.partial(substitute, b, k) for b in blocks] + [functools.partial(store, k)]
     schur = [m[STEPS, STEPS] for m in mats]
-    schur_inv = inverses(schur)
-    g_ref[COND:, :] = jnp.concatenate(schur_inv, axis=1)
-    for k in range(STEPS):
-        g_ref[k * WIDE : (k + 1) * WIDE, :] = -jnp.concatenate([s[k] for s in solved], axis=1)
+    gap = jnp.zeros((PTS, PTS), F32)
+    both = jnp.concatenate(
+        [jnp.concatenate([schur[0], gap], axis=1), jnp.concatenate([gap, schur[1]], axis=1)], axis=0
+    )
+    both = inverses([both], PTS, tasks)[0]
+    g_ref[COND:, :] = jnp.where(low, both[:PTS], both[PTS:])
     s_ref[...] = jnp.concatenate(schur, axis=1)
 
 

time: 75.1 us -> 73.7 us (0.981)
  Pallas kernels: 26.3 us -> 24.8 us
    pallas_call x1, Pallas kernels: 14.1 us -> 12.7 us  [shards(): local(factor_kernel, 'factor', (jax.ShapeDtypeStruct((COND + PTS, WIDE),...]
  transfers between devices with their start and end apart: 18 -> 18, of which waited for: 7 -> 7; matrix products, arithmetic and copies ran while one was open for 1% -> 1% of each run, Pallas kernels for 29% -> 27%
where the time goes in v4:
time: 73.7 us; the launch traced here: 73.3 us
  starting transfers between devices  34.5 us (47%)
  Pallas kernels  24.8 us (34%)
  waiting for transfers between devices  11 us (15%)
  local copies, waits for them, and re-layouts  2.17 us (3%)
  between operations  0.82 us (1%)
    ppermute x8, starting transfers between devices, passed(): lax.ppermute(value, AXES, [(i, i + by) for i in range(size) if 0 <= i + b...  19.2 us
    pallas_call x1, Pallas kernels, shards(): local(factor_kernel, 'factor', (jax.ShapeDtypeStruct((COND + PTS, WIDE),...  12.7 us
    ppermute x9, starting transfers between devices, swapped(): return lax.ppermute(value, AXES, [(i, i ^ mask) for i in range(size)])  8.81 us
    pallas_call x1, Pallas kernels, shards(): local(logdet_kernel, 'logdet', jax.ShapeDtypeStruct((8, WIDE), F32), [vme...  7.31 us
    all_to_all x1, starting transfers between devices, shards(): everywhere = lax.all_to_all(told, AXES, 0, 0)  6.44 us
    ppermute x9, waiting for transfers between devices, swapped(): return lax.ppermute(value, AXES, [(i, i ^ mask) for i in range(size)])  6.23 us
    ppermute x8, waiting for transfers between devices, passed(): lax.ppermute(value, AXES, [(i, i + by) for i in range(size) if 0 <= i + b...  4.8 us
    pallas_call x1, Pallas kernels, shards(): local(apply_kernel, 'apply', (tiles,) * WINDOW, [smem, smem] + [vmem] * (...  3.42 us
  transfers between devices with their start and end apart: 18, of which 7 were waited for; matrix products, arithmetic and copies ran while one was open for 1% of the time, Pallas kernels for 27%

profile of v4, /device:TPU:3, one launch (start us, length us, event | category | flops | bytes accessed | tf_op | source)
XLA Modules:
  0.0 73.3 jit_solution(763579115911398518)
XLA Ops:
  0.6 0.0 copy-start.2
  0.6 0.0 copy-start.1
  0.7 0.7 copy-done.2
  1.3 0.0 copy-done.1
  1.3 0.0 copy-start
  1.3 0.9 %copy-done = f32[256,128]{1,0:T(8,128)S(1)} copy-done((f32[256,128]{1,0:T(8,128)S(1)}, f32[256,128]{1,0:T(8,128)}, u32[]{:S(2)}) %copy-start) | copy-done | bytes 131096
  2.2 0.7 prepare.1
  2.9 6.4 %all-to-all-start = ((f32[32,8,128]{2,1,0:T(8,128)}), f32[32,8,128]{2,1,0:T(8,128)S(1)}, u32[]{:S(2)}, u32[]{:S(2)}) async-start(f32[32,8,128]{2,1,0:T(8,128)} %get-tuple-element.27), calls=%async_computation | async-start | bytes 262144 | tf_op jit(solution)/shard_map/all_to_all | solution.py:347
  9.4 0.4 collective-permute-start
  9.8 1.2 %collective-permute-start.1 = (f32[64,128]{1,0:T(8,128)S(1)}, f32[64,128]{1,0:T(8,128)S(1)}, u32[]{:S(2)}, u32[]{:S(2)}) collective-permute-start(f32[64,128]{1,0:T(8,128)S(1)} %get-tuple-element.31), channel_id=1, source_target_pairs={{0,2},{1,3},{2,0},{3,1},{4,6},{5,7},{6,4},{7,5},{8,10},{9,11},{10,... | collective-permute-start | bytes 98312 | tf_op jit(solution)/shard_map/ppermute | solution.py:311
  11.0 0.6 collective-permute-start.2
  11.6 0.0 collective-permute-done
  11.6 1.5 %collective-permute-done.1 = f32[64,128]{1,0:T(8,128)S(1)} collective-permute-done((f32[64,128]{1,0:T(8,128)S(1)}, f32[64,128]{1,0:T(8,128)S(1)}, u32[]{:S(2)}, u32[]{:S(2)}) %collective-permute-start.1) | collective-permute-done | bytes 32800 | tf_op jit(solution)/shard_map/ppermute | solution.py:311
  13.0 1.9 %collective-permute-done.2 = f32[64,128]{1,0:T(8,128)S(1)} collective-permute-done((f32[64,128]{1,0:T(8,128)S(1)}, f32[64,128]{1,0:T(8,128)S(1)}, u32[]{:S(2)}, u32[]{:S(2)}) %collective-permute-start.2) | collective-permute-done | bytes 32800 | tf_op jit(solution)/shard_map/ppermute | solution.py:311
  14.9 4.0 %collective-permute-start.4 = (f32[4,64,128]{2,1,0:T(8,128)S(1)}, f32[4,64,128]{2,1,0:T(8,128)S(1)}, u32[]{:S(2)}, u32[]{:S(2)}) collective-permute-start(f32[4,64,128]{2,1,0:T(8,128)S(1)} %pad_maximum_fusion.rest_0_), channel_id=1, source_target_pairs={{0,8},{1,9},{2,10},{3,11},{4,12},{5,13},{6,14},{7,15},{8,16},{9,17... | collective-permute-start | bytes 393224 | tf_op jit(solution)/shard_map/ppermute | solution.py:306
  18.9 2.1 %collective-permute-start.3 = (f32[4,64,128]{2,1,0:T(8,128)S(1)}, f32[4,64,128]{2,1,0:T(8,128)S(1)}, u32[]{:S(2)}, u32[]{:S(2)}) collective-permute-start(f32[4,64,128]{2,1,0:T(8,128)S(1)} %pad_maximum_fusion.rest_0_), channel_id=1, source_target_pairs={{0,12},{1,13},{2,14},{3,15},{4,16},{5,17},{6,18},{7,19},{8,20},{9,... | collective-permute-start | bytes 393224 | tf_op jit(solution)/shard_map/ppermute | solution.py:306
  21.0 0.0 all-to-all-done.coords_ref
  21.0 12.7 %factor.1 = (f32[576,128]{1,0:T(8,128)S(1)}, f32[64,128]{1,0:T(8,128)S(1)}) custom-call(s32[1]{0:T(128)} %bitcast.where_ref, s32[2,8]{1,0:T(2,128)S(1)} %copy-done.2, f32[32,8,128]{2,1,0:T(8,128)S(1)} %all-to-all-done.coords_ref), custom_call_target="tpu_custom_call" | custom-call | flops 14000000000 | bytes 100000 | tf_op jit(solution)/shard_map/factor/pallas_call | solution.py:350
  33.7 0.0 collective-permute-done.4.rest_2_
  33.7 0.0 collective-permute-done.3.rest_3_
  33.7 0.5 collective-permute-start.5
  34.3 1.3 %collective-permute-start.7 = (f32[4,64,128]{2,1,0:T(8,128)S(1)}, f32[4,64,128]{2,1,0:T(8,128)S(1)}, u32[]{:S(2)}, u32[]{:S(2)}) collective-permute-start(f32[4,64,128]{2,1,0:T(8,128)S(1)} %pad_maximum_fusion.rest_0_), channel_id=1, source_target_pairs={{0,16},{1,17},{2,18},{3,19},{4,20},{5,21},{6,22},{7,23},{8,24},{9,... | collective-permute-start | bytes 393224 | tf_op jit(solution)/shard_map/ppermute | solution.py:306
  35.6 2.4 %collective-permute-start.6 = (f32[4,64,128]{2,1,0:T(8,128)S(1)}, f32[4,64,128]{2,1,0:T(8,128)S(1)}, u32[]{:S(2)}, u32[]{:S(2)}) collective-permute-start(f32[4,64,128]{2,1,0:T(8,128)S(1)} %pad_maximum_fusion.rest_0_), channel_id=1, source_target_pairs={{0,4},{1,5},{2,6},{3,7},{4,8},{5,9},{6,10},{7,11},{8,12},{9,13},{1... | collective-permute-start | bytes 393224 | tf_op jit(solution)/shard_map/ppermute | solution.py:306
  37.9 1.2 %collective-permute-start.8 = (f32[576,128]{1,0:T(8,128)S(1)}, f32[576,128]{1,0:T(8,128)S(1)}, u32[]{:S(2)}, u32[]{:S(2)}) collective-permute-start(f32[576,128]{1,0:T(8,128)S(1)} %get-tuple-element.34.rest_5_), channel_id=1, source_target_pairs={{0,1},{1,0},{2,3},{3,2},{4,5},{5,4},{6,7},{7,6},{8,9},{9,8},{10,11... | collective-permute-start | bytes 884744 | tf_op jit(solution)/shard_map/ppermute | solution.py:311
  39.2 1.9 %collective-permute-done.7.rest_4_ = f32[4,64,128]{2,1,0:T(8,128)S(1)} collective-permute-done((f32[4,64,128]{2,1,0:T(8,128)S(1)}, f32[4,64,128]{2,1,0:T(8,128)S(1)}, u32[]{:S(2)}, u32[]{:S(2)}) %collective-permute-start.7) | collective-permute-done | bytes 131104 | tf_op jit(solution)/shard_map/ppermute | solution.py:306
  41.1 2.9 %collective-permute-done.6.rest_1_ = f32[4,64,128]{2,1,0:T(8,128)S(1)} collective-permute-done((f32[4,64,128]{2,1,0:T(8,128)S(1)}, f32[4,64,128]{2,1,0:T(8,128)S(1)}, u32[]{:S(2)}, u32[]{:S(2)}) %collective-permute-start.6) | collective-permute-done | bytes 131104 | tf_op jit(solution)/shard_map/ppermute | solution.py:306
  44.0 0.0 collective-permute-done.5.rest_7_
  44.0 2.1 %collective-permute-start.9 = (f32[576,128]{1,0:T(8,128)S(1)}, f32[576,128]{1,0:T(8,128)S(1)}, u32[]{:S(2)}, u32[]{:S(2)}) collective-permute-start(f32[576,128]{1,0:T(8,128)S(1)} %collective-permute-done.5.rest_7_), channel_id=1, source_target_pairs={{0,1},{1,0},{2,3},{3,2},{4,5},{5,4},{6,7},{7,6},{8,9},{9,8},{10,11... | collective-permute-start | bytes 884744 | tf_op jit(solution)/shard_map/ppermute | solution.py:311
  46.1 0.0 collective-permute-done.8.rest_6_
  46.1 1.2 %collective-permute-done.9.rest_8_ = f32[576,128]{1,0:T(8,128)S(1)} collective-permute-done((f32[576,128]{1,0:T(8,128)S(1)}, f32[576,128]{1,0:T(8,128)S(1)}, u32[]{:S(2)}, u32[]{:S(2)}) %collective-permute-start.9) | collective-permute-done | bytes 294944 | tf_op jit(solution)/shard_map/ppermute | solution.py:311
  47.3 3.4 %apply.1 = (f32[4,64,128]{2,1,0:T(8,128)S(1)}, f32[4,64,128]{2,1,0:T(8,128)S(1)}, f32[4,64,128]{2,1,0:T(8,128)S(1)}, f32[4,64,128]{2,1,0:T(8,128)S(1)}, f32[4,64,128]{2,1,0:T(8,128)S(1)}) custom-call(s32[1]{0:T(128)} %bitcast.where_ref, s32[4,2,8]{2,1,0:T(2,128)S(1)} %dynamic-slice_convert_fusion.ids_ref, f32[4,64,128]{2,1,0:T(8,128)S(1)} %pad_maximum_fusion.rest_0_, ...), custom_call_target="tpu_custom_call" | custom-call | flops 4000000000 | bytes 100000 | tf_op jit(solution)/shard_map/apply/pallas_call | solution.py:364
  50.7 1.9 %collective-permute-start.10 = (f32[4,64,128]{2,1,0:T(8,128)S(1)}, f32[4,64,128]{2,1,0:T(8,128)S(1)}, u32[]{:S(2)}, u32[]{:S(2)}) collective-permute-start(f32[4,64,128]{2,1,0:T(8,128)S(1)} %get-tuple-element.43), channel_id=1, source_target_pairs={{12,0},{13,1},{14,2},{15,3},{16,4},{17,5},{18,6},{19,7},{20,8},{21... | collective-permute-start | bytes 393224 | tf_op jit(solution)/shard_map/ppermute | solution.py:306
  52.6 1.9 %collective-permute-start.11 = (f32[4,64,128]{2,1,0:T(8,128)S(1)}, f32[4,64,128]{2,1,0:T(8,128)S(1)}, u32[]{:S(2)}, u32[]{:S(2)}) collective-permute-start(f32[4,64,128]{2,1,0:T(8,128)S(1)} %get-tuple-element.44), channel_id=1, source_target_pairs={{8,0},{9,1},{10,2},{11,3},{12,4},{13,5},{14,6},{15,7},{16,8},{17,9... | collective-permute-start | bytes 393224 | tf_op jit(solution)/shard_map/ppermute | solution.py:306
  54.6 1.3 %collective-permute-start.12 = (f32[4,64,128]{2,1,0:T(8,128)S(1)}, f32[4,64,128]{2,1,0:T(8,128)S(1)}, u32[]{:S(2)}, u32[]{:S(2)}) collective-permute-start(f32[4,64,128]{2,1,0:T(8,128)S(1)} %get-tuple-element.45), channel_id=1, source_target_pairs={{16,0},{17,1},{18,2},{19,3},{20,4},{21,5},{22,6},{23,7},{24,8},{25... | collective-permute-start | bytes 393224 | tf_op jit(solution)/shard_map/ppermute | solution.py:306
  55.9 4.4 %collective-permute-start.13 = (f32[4,64,128]{2,1,0:T(8,128)S(1)}, f32[4,64,128]{2,1,0:T(8,128)S(1)}, u32[]{:S(2)}, u32[]{:S(2)}) collective-permute-start(f32[4,64,128]{2,1,0:T(8,128)S(1)} %get-tuple-element.46), channel_id=1, source_target_pairs={{4,0},{5,1},{6,2},{7,3},{8,4},{9,5},{10,6},{11,7},{12,8},{13,9},{1... | collective-permute-start | bytes 393224 | tf_op jit(solution)/shard_map/ppermute | solution.py:306
  60.3 7.3 %logdet.1 = f32[8,128]{1,0:T(8,128)S(1)} custom-call(f32[64,128]{1,0:T(8,128)S(1)} %get-tuple-element.41.s_ref), custom_call_target="tpu_custom_call" | custom-call | flops 8999999488 | bytes 100000 | tf_op jit(solution)/shard_map/logdet/pallas_call | solution.py:372
  67.6 0.0 collective-permute-done.10.refs_1_
  67.6 0.0 collective-permute-done.11.refs_2_
  67.6 0.0 collective-permute-done.12.refs_3_
  67.6 0.0 collective-permute-done.13.refs_4_
  67.6 0.1 sum.1
  67.7 1.0 %collective-permute-start.14 = (f32[64,128]{1,0:T(8,128)S(1)}, f32[64,128]{1,0:T(8,128)S(1)}, u32[]{:S(2)}, u32[]{:S(2)}) collective-permute-start(f32[64,128]{1,0:T(8,128)S(1)} %get-tuple-element.48), channel_id=1, source_target_pairs={{0,1},{1,0},{2,3},{3,2},{4,5},{5,4},{6,7},{7,6},{8,9},{9,8},{10,11... | collective-permute-start | bytes 98312 | tf_op jit(solution)/shard_map/ppermute | solution.py:311
  68.7 0.7 collective-permute-start.15
  69.3 1.0 %collective-permute-start.16 = (f32[64,128]{1,0:T(8,128)S(1)}, f32[64,128]{1,0:T(8,128)S(1)}, u32[]{:S(2)}, u32[]{:S(2)}) collective-permute-start(f32[64,128]{1,0:T(8,128)S(1)} %get-tuple-element.50), channel_id=1, source_target_pairs={{0,3},{1,2},{2,1},{3,0},{4,7},{5,6},{6,5},{7,4},{8,11},{9,10},{10,... | collective-permute-start | bytes 98312 | tf_op jit(solution)/shard_map/ppermute | solution.py:311
  70.4 0.6 slice.3
  71.0 0.0 collective-permute-done.14.refs_1_
  71.0 0.5 collective-permute-done.15.refs_2_
  71.4 1.2 %collective-permute-done.16.refs_3_ = f32[64,128]{1,0:T(8,128)S(1)} collective-permute-done((f32[64,128]{1,0:T(8,128)S(1)}, f32[64,128]{1,0:T(8,128)S(1)}, u32[]{:S(2)}, u32[]{:S(2)}) %collective-permute-start.16) | collective-permute-done | bytes 32800 | tf_op jit(solution)/shard_map/ppermute | solution.py:311
  72.7 0.7 place.1
  (2 shorter events, 0.0 us)
Async XLA Ops:
  0.6 0.7 copy-start.2
  0.6 0.7 copy-start.1
  1.3 0.9 %copy-start = (f32[256,128]{1,0:T(8,128)S(1)}, f32[256,128]{1,0:T(8,128)}, u32[]{:S(2)}) copy-start(f32[256,128]{1,0:T(8,128)} %probes_ref.1) | copy-start | bytes 393220
  2.9 18.1 %all-to-all-start = ((f32[32,8,128]{2,1,0:T(8,128)}), f32[32,8,128]{2,1,0:T(8,128)S(1)}, u32[]{:S(2)}, u32[]{:S(2)}) async-start(f32[32,8,128]{2,1,0:T(8,128)} %get-tuple-element.27), calls=%async_computation | async-start | bytes 262144 | tf_op jit(solution)/shard_map/all_to_all | solution.py:347
  9.4 2.2 %collective-permute-start = (f32[64,128]{1,0:T(8,128)S(1)}, f32[64,128]{1,0:T(8,128)S(1)}, u32[]{:S(2)}, u32[]{:S(2)}) collective-permute-start(f32[64,128]{1,0:T(8,128)S(1)} %get-tuple-element.30), channel_id=1, source_target_pairs={{0,1},{1,0},{2,3},{3,2},{4,5},{5,4},{6,7},{7,6},{8,9},{9,8},{10,11... | collective-permute-start | bytes 98312 | tf_op jit(solution)/shard_map/ppermute | solution.py:311
  9.8 3.3 %collective-permute-start.1 = (f32[64,128]{1,0:T(8,128)S(1)}, f32[64,128]{1,0:T(8,128)S(1)}, u32[]{:S(2)}, u32[]{:S(2)}) collective-permute-start(f32[64,128]{1,0:T(8,128)S(1)} %get-tuple-element.31), channel_id=1, source_target_pairs={{0,2},{1,3},{2,0},{3,1},{4,6},{5,7},{6,4},{7,5},{8,10},{9,11},{10,... | collective-permute-start | bytes 98312 | tf_op jit(solution)/shard_map/ppermute | solution.py:311
  11.0 3.9 %collective-permute-start.2 = (f32[64,128]{1,0:T(8,128)S(1)}, f32[64,128]{1,0:T(8,128)S(1)}, u32[]{:S(2)}, u32[]{:S(2)}) collective-permute-start(f32[64,128]{1,0:T(8,128)S(1)} %get-tuple-element.32), channel_id=1, source_target_pairs={{0,3},{1,2},{2,1},{3,0},{4,7},{5,6},{6,5},{7,4},{8,11},{9,10},{10,... | collective-permute-start | bytes 98312 | tf_op jit(solution)/shard_map/ppermute | solution.py:311
  14.9 18.8 %collective-permute-start.4 = (f32[4,64,128]{2,1,0:T(8,128)S(1)}, f32[4,64,128]{2,1,0:T(8,128)S(1)}, u32[]{:S(2)}, u32[]{:S(2)}) collective-permute-start(f32[4,64,128]{2,1,0:T(8,128)S(1)} %pad_maximum_fusion.rest_0_), channel_id=1, source_target_pairs={{0,8},{1,9},{2,10},{3,11},{4,12},{5,13},{6,14},{7,15},{8,16},{9,17... | collective-permute-start | bytes 393224 | tf_op jit(solution)/shard_map/ppermute | solution.py:306
  18.9 14.8 %collective-permute-start.3 = (f32[4,64,128]{2,1,0:T(8,128)S(1)}, f32[4,64,128]{2,1,0:T(8,128)S(1)}, u32[]{:S(2)}, u32[]{:S(2)}) collective-permute-start(f32[4,64,128]{2,1,0:T(8,128)S(1)} %pad_maximum_fusion.rest_0_), channel_id=1, source_target_pairs={{0,12},{1,13},{2,14},{3,15},{4,16},{5,17},{6,18},{7,19},{8,20},{9,... | collective-permute-start | bytes 393224 | tf_op jit(solution)/shard_map/ppermute | solution.py:306
  33.7 10.2 %collective-permute-start.5 = (f32[576,128]{1,0:T(8,128)S(1)}, f32[576,128]{1,0:T(8,128)S(1)}, u32[]{:S(2)}, u32[]{:S(2)}) collective-permute-start(f32[576,128]{1,0:T(8,128)S(1)} %get-tuple-element.34.rest_5_), channel_id=1, source_target_pairs={{0,2},{1,3},{2,0},{3,1},{4,6},{5,7},{6,4},{7,5},{8,10},{9,11},{10,... | collective-permute-start | bytes 884744 | tf_op jit(solution)/shard_map/ppermute | solution.py:311
  34.3 6.8 %collective-permute-start.7 = (f32[4,64,128]{2,1,0:T(8,128)S(1)}, f32[4,64,128]{2,1,0:T(8,128)S(1)}, u32[]{:S(2)}, u32[]{:S(2)}) collective-permute-start(f32[4,64,128]{2,1,0:T(8,128)S(1)} %pad_maximum_fusion.rest_0_), channel_id=1, source_target_pairs={{0,16},{1,17},{2,18},{3,19},{4,20},{5,21},{6,22},{7,23},{8,24},{9,... | collective-permute-start | bytes 393224 | tf_op jit(solution)/shard_map/ppermute | solution.py:306
  35.6 8.4 %collective-permute-start.6 = (f32[4,64,128]{2,1,0:T(8,128)S(1)}, f32[4,64,128]{2,1,0:T(8,128)S(1)}, u32[]{:S(2)}, u32[]{:S(2)}) collective-permute-start(f32[4,64,128]{2,1,0:T(8,128)S(1)} %pad_maximum_fusion.rest_0_), channel_id=1, source_target_pairs={{0,4},{1,5},{2,6},{3,7},{4,8},{5,9},{6,10},{7,11},{8,12},{9,13},{1... | collective-permute-start | bytes 393224 | tf_op jit(solution)/shard_map/ppermute | solution.py:306
  37.9 8.1 %collective-permute-start.8 = (f32[576,128]{1,0:T(8,128)S(1)}, f32[576,128]{1,0:T(8,128)S(1)}, u32[]{:S(2)}, u32[]{:S(2)}) collective-permute-start(f32[576,128]{1,0:T(8,128)S(1)} %get-tuple-element.34.rest_5_), channel_id=1, source_target_pairs={{0,1},{1,0},{2,3},{3,2},{4,5},{5,4},{6,7},{7,6},{8,9},{9,8},{10,11... | collective-permute-start | bytes 884744 | tf_op jit(solution)/shard_map/ppermute | solution.py:311
  44.0 3.3 %collective-permute-start.9 = (f32[576,128]{1,0:T(8,128)S(1)}, f32[576,128]{1,0:T(8,128)S(1)}, u32[]{:S(2)}, u32[]{:S(2)}) collective-permute-start(f32[576,128]{1,0:T(8,128)S(1)} %collective-permute-done.5.rest_7_), channel_id=1, source_target_pairs={{0,1},{1,0},{2,3},{3,2},{4,5},{5,4},{6,7},{7,6},{8,9},{9,8},{10,11... | collective-permute-start | bytes 884744 | tf_op jit(solution)/shard_map/ppermute | solution.py:311
  50.7 16.9 %collective-permute-start.10 = (f32[4,64,128]{2,1,0:T(8,128)S(1)}, f32[4,64,128]{2,1,0:T(8,128)S(1)}, u32[]{:S(2)}, u32[]{:S(2)}) collective-permute-start(f32[4,64,128]{2,1,0:T(8,128)S(1)} %get-tuple-element.43), channel_id=1, source_target_pairs={{12,0},{13,1},{14,2},{15,3},{16,4},{17,5},{18,6},{19,7},{20,8},{21... | collective-permute-start | bytes 393224 | tf_op jit(solution)/shard_map/ppermute | solution.py:306
  52.6 15.0 %collective-permute-start.11 = (f32[4,64,128]{2,1,0:T(8,128)S(1)}, f32[4,64,128]{2,1,0:T(8,128)S(1)}, u32[]{:S(2)}, u32[]{:S(2)}) collective-permute-start(f32[4,64,128]{2,1,0:T(8,128)S(1)} %get-tuple-element.44), channel_id=1, source_target_pairs={{8,0},{9,1},{10,2},{11,3},{12,4},{13,5},{14,6},{15,7},{16,8},{17,9... | collective-permute-start | bytes 393224 | tf_op jit(solution)/shard_map/ppermute | solution.py:306
  54.6 13.0 %collective-permute-start.12 = (f32[4,64,128]{2,1,0:T(8,128)S(1)}, f32[4,64,128]{2,1,0:T(8,128)S(1)}, u32[]{:S(2)}, u32[]{:S(2)}) collective-permute-start(f32[4,64,128]{2,1,0:T(8,128)S(1)} %get-tuple-element.45), channel_id=1, source_target_pairs={{16,0},{17,1},{18,2},{19,3},{20,4},{21,5},{22,6},{23,7},{24,8},{25... | collective-permute-start | bytes 393224 | tf_op jit(solution)/shard_map/ppermute | solution.py:306
  55.9 11.7 %collective-permute-start.13 = (f32[4,64,128]{2,1,0:T(8,128)S(1)}, f32[4,64,128]{2,1,0:T(8,128)S(1)}, u32[]{:S(2)}, u32[]{:S(2)}) collective-permute-start(f32[4,64,128]{2,1,0:T(8,128)S(1)} %get-tuple-element.46), channel_id=1, source_target_pairs={{4,0},{5,1},{6,2},{7,3},{8,4},{9,5},{10,6},{11,7},{12,8},{13,9},{1... | collective-permute-start | bytes 393224 | tf_op jit(solution)/shard_map/ppermute | solution.py:306
  67.7 3.3 %collective-permute-start.14 = (f32[64,128]{1,0:T(8,128)S(1)}, f32[64,128]{1,0:T(8,128)S(1)}, u32[]{:S(2)}, u32[]{:S(2)}) collective-permute-start(f32[64,128]{1,0:T(8,128)S(1)} %get-tuple-element.48), channel_id=1, source_target_pairs={{0,1},{1,0},{2,3},{3,2},{4,5},{5,4},{6,7},{7,6},{8,9},{9,8},{10,11... | collective-permute-start | bytes 98312 | tf_op jit(solution)/shard_map/ppermute | solution.py:311
  68.7 2.8 %collective-permute-start.15 = (f32[64,128]{1,0:T(8,128)S(1)}, f32[64,128]{1,0:T(8,128)S(1)}, u32[]{:S(2)}, u32[]{:S(2)}) collective-permute-start(f32[64,128]{1,0:T(8,128)S(1)} %get-tuple-element.49), channel_id=1, source_target_pairs={{0,2},{1,3},{2,0},{3,1},{4,6},{5,7},{6,4},{7,5},{8,10},{9,11},{10,... | collective-permute-start | bytes 98312 | tf_op jit(solution)/shard_map/ppermute | solution.py:311
  69.3 3.3 %collective-permute-start.16 = (f32[64,128]{1,0:T(8,128)S(1)}, f32[64,128]{1,0:T(8,128)S(1)}, u32[]{:S(2)}, u32[]{:S(2)}) collective-permute-start(f32[64,128]{1,0:T(8,128)S(1)} %get-tuple-element.50), channel_id=1, source_target_pairs={{0,3},{1,2},{2,1},{3,0},{4,7},{5,6},{6,5},{7,4},{8,11},{9,10},{10,... | collective-permute-start | bytes 98312 | tf_op jit(solution)/shard_map/ppermute | solution.py:311

commit v5 on v4

--- a/solution.py
+++ b/solution.py
@@ -209,48 +209,54 @@
     me = where_ref[0]
     slab, quarter = lax.div(me, SLAB), lax.rem(me, SLAB)
     low = iota((PTS, WIDE), 1) < PTS
+    places_held = WINDOW * SLAB
     for o in range(WINDOW):
-        held[o * SLAB : (o + 1) * SLAB] = windows[o][...]
+        for q in range(SLAB):
+            tile = windows[o][q]
+            held[o * SLAB + q] = tile
+            held[places_held + o * SLAB + q] = pltpu.roll(tile, PTS, 1)
     total[...] = jnp.zeros_like(total)
 
-    for k in range(SLAB):
-        sender = quarter ^ k
-        device = slab * SLAB + sender
-        places = []
+    places = []
+    for k in range(SLAB):
+        device = slab * SLAB + (quarter ^ k)
         for b in range(BLK):
             for m in range(NEIGH):
-                ident = ids_ref[sender, b, m]
+                ident = ids_ref[quarter ^ k, b, m]
                 ident = jnp.where(ident >= 0, ident, device * BLK)
-                owner = lax.div(ident, BLK)
-                place = place_of(me, owner)
-                turn = (lax.rem(ident, BLK) ^ (m % 2)) * PTS
-                places.append((place, turn))
-        gathered = []
+                turned = lax.rem(ident, BLK) ^ (m % 2)
+                places.append(place_of(me, lax.div(ident, BLK)) + turned * places_held)
+    gathered = []
+    for k in range(SLAB):
+        sides = []
         for b in range(BLK):
-            pieces = []
-            for m in range(0, NEIGH, 2):
-                (p0, t0), (p1, t1) = places[b * NEIGH + m], places[b * NEIGH + m + 1]
-                first = pltpu.roll(held[p0], t0, 1)
-                second = pltpu.roll(held[p1], t1, 1)
-                pieces.append(jnp.where(low, first, second))
-            gathered.append(jnp.concatenate(pieces, axis=1))
-        w = w_refs[k][:COND, :]
-        white = quick(jnp.concatenate(gathered, axis=0), w)
-        white = held[k] + jnp.where(low, white[:PTS], white[PTS:])
+            at = places[(k * BLK + b) * NEIGH : (k * BLK + b + 1) * NEIGH]
+            pieces = [jnp.where(low, held[at[m]], held[at[m + 1]]) for m in range(0, NEIGH, 2)]
+            sides.append(jnp.concatenate(pieces, axis=1))
+        gathered.append(jnp.concatenate(sides, axis=0))
+    whites = [quick(gathered[k], w_refs[k][:COND, :]) for k in range(SLAB)]
+    scaled = []
+    for k in range(SLAB):
+        white = held[k] + jnp.where(low, whites[k][:PTS], whites[k][PTS:])
         v = w_refs[k][COND:, :]
         inv = jnp.concatenate([jnp.where(low, v, 0.0), jnp.where(low, 0.0, v)], axis=0)
-        scaled = dot(white, inv)
-        total[k] += scaled
-        sides = jnp.concatenate([jnp.where(low, scaled, 0.0), jnp.where(low, 0.0, scaled)], axis=0)
-        back = quick(sides, w, ((1,), (1,)))
+        scaled.append(dot(white, inv))
+    backs = []
+    for k in range(SLAB):
+        sides = jnp.concatenate([jnp.where(low, scaled[k], 0.0), jnp.where(low, 0.0, scaled[k])], axis=0)
+        backs.append(quick(sides, w_refs[k][:COND, :], ((1,), (1,))))
+    for k in range(SLAB):
+        total[k] = scaled[k]
+    for k in range(SLAB):
         for b in range(BLK):
             for m in range(NEIGH):
-                place, turn = places[b * NEIGH + m]
-                tile = back[b * PTS : (b + 1) * PTS, (m // 2) * WIDE : (m // 2 + 1) * WIDE]
+                tile = backs[k][b * PTS : (b + 1) * PTS, (m // 2) * WIDE : (m // 2 + 1) * WIDE]
                 tile = jnp.where(low, tile, 0.0) if m % 2 == 0 else jnp.where(low, 0.0, tile)
-                total[place] += pltpu.roll(tile, turn, 1)
+                total[places[(k * BLK + b) * NEIGH + m]] += tile
     for o in range(WINDOW):
-        outs[o][...] = total[o * SLAB : (o + 1) * SLAB]
+        for q in range(SLAB):
+            place = o * SLAB + q
+            outs[o][q] = total[place] + pltpu.roll(total[places_held + place], PTS, 1)
 
 
 def logdet_kernel(s_ref, out_ref, work):
@@ -366,7 +372,7 @@
         "apply",
         (tiles,) * WINDOW,
         [smem, smem] + [vmem] * (WINDOW + SLAB),
-        [pltpu.VMEM((WINDOW * SLAB, quarter, WIDE), F32)] * 2,
+        [pltpu.VMEM((2 * WINDOW * SLAB, quarter, WIDE), F32)] * 2,
         gflops=4,
     )(here, ids, *window, w, w_d, w_y, w_yd)
     logs = local(

time: 73.7 us -> 72.8 us (0.988)
  Pallas kernels: 24.8 us -> 24 us
    pallas_call x1, Pallas kernels: 3.42 us -> 2.58 us  [shards(): local(apply_kernel, 'apply', (tiles,) * WINDOW, [smem, smem] + [vmem] * (...]
  transfers between devices with their start and end apart: 18 -> 18, of which waited for: 7 -> 7; matrix products, arithmetic and copies ran while one was open for 1% -> 1% of each run, Pallas kernels for 27% -> 28%
where the time goes in v5:
time: 72.8 us; the launch traced here: 72.5 us
  starting transfers between devices  34.4 us (47%)
  Pallas kernels  24 us (33%)
  waiting for transfers between devices  11 us (15%)
  local copies, waits for them, and re-layouts  2.17 us (3%)
  between operations  0.82 us (1%)
    ppermute x8, starting transfers between devices, passed(): lax.ppermute(value, AXES, [(i, i + by) for i in range(size) if 0 <= i + b...  19.2 us
    pallas_call x1, Pallas kernels, shards(): local(factor_kernel, 'factor', (jax.ShapeDtypeStruct((COND + PTS, WIDE),...  12.7 us
    ppermute x9, starting transfers between devices, swapped(): return lax.ppermute(value, AXES, [(i, i ^ mask) for i in range(size)])  8.81 us
    pallas_call x1, Pallas kernels, shards(): local(logdet_kernel, 'logdet', jax.ShapeDtypeStruct((8, WIDE), F32), [vme...  7.31 us
    all_to_all x1, starting transfers between devices, shards(): everywhere = lax.all_to_all(told, AXES, 0, 0)  6.44 us
    ppermute x9, waiting for transfers between devices, swapped(): return lax.ppermute(value, AXES, [(i, i ^ mask) for i in range(size)])  6.23 us
    ppermute x8, waiting for transfers between devices, passed(): lax.ppermute(value, AXES, [(i, i + by) for i in range(size) if 0 <= i + b...  4.8 us
    pallas_call x1, Pallas kernels, shards(): local(apply_kernel, 'apply', (tiles,) * WINDOW, [smem, smem] + [vmem] * (...  2.58 us
  transfers between devices with their start and end apart: 18, of which 7 were waited for; matrix products, arithmetic and copies ran while one was open for 1% of the time, Pallas kernels for 28%

profile of v5, /device:TPU:3, one launch (start us, length us, event | category | flops | bytes accessed | tf_op | source)
XLA Modules:
  0.0 72.5 jit_solution(3400580743719570546)
XLA Ops:
  0.6 0.0 copy-start.2
  0.6 0.0 copy-start.1
  0.7 0.7 copy-done.2
  1.3 0.0 copy-done.1
  1.3 0.0 copy-start
  1.3 0.9 %copy-done = f32[256,128]{1,0:T(8,128)S(1)} copy-done((f32[256,128]{1,0:T(8,128)S(1)}, f32[256,128]{1,0:T(8,128)}, u32[]{:S(2)}) %copy-start) | copy-done | bytes 131096
  2.2 0.7 prepare.1
  2.9 6.4 %all-to-all-start = ((f32[32,8,128]{2,1,0:T(8,128)}), f32[32,8,128]{2,1,0:T(8,128)S(1)}, u32[]{:S(2)}, u32[]{:S(2)}) async-start(f32[32,8,128]{2,1,0:T(8,128)} %get-tuple-element.27), calls=%async_computation | async-start | bytes 262144 | tf_op jit(solution)/shard_map/all_to_all | solution.py:353
  9.4 0.4 collective-permute-start
  9.8 1.2 %collective-permute-start.1 = (f32[64,128]{1,0:T(8,128)S(1)}, f32[64,128]{1,0:T(8,128)S(1)}, u32[]{:S(2)}, u32[]{:S(2)}) collective-permute-start(f32[64,128]{1,0:T(8,128)S(1)} %get-tuple-element.31), channel_id=1, source_target_pairs={{0,2},{1,3},{2,0},{3,1},{4,6},{5,7},{6,4},{7,5},{8,10},{9,11},{10,... | collective-permute-start | bytes 98312 | tf_op jit(solution)/shard_map/ppermute | solution.py:317
  11.0 0.6 collective-permute-start.2
  11.6 0.0 collective-permute-done
  11.6 1.5 %collective-permute-done.1 = f32[64,128]{1,0:T(8,128)S(1)} collective-permute-done((f32[64,128]{1,0:T(8,128)S(1)}, f32[64,128]{1,0:T(8,128)S(1)}, u32[]{:S(2)}, u32[]{:S(2)}) %collective-permute-start.1) | collective-permute-done | bytes 32800 | tf_op jit(solution)/shard_map/ppermute | solution.py:317
  13.0 1.9 %collective-permute-done.2 = f32[64,128]{1,0:T(8,128)S(1)} collective-permute-done((f32[64,128]{1,0:T(8,128)S(1)}, f32[64,128]{1,0:T(8,128)S(1)}, u32[]{:S(2)}, u32[]{:S(2)}) %collective-permute-start.2) | collective-permute-done | bytes 32800 | tf_op jit(solution)/shard_map/ppermute | solution.py:317
  14.9 4.0 %collective-permute-start.4 = (f32[4,64,128]{2,1,0:T(8,128)S(1)}, f32[4,64,128]{2,1,0:T(8,128)S(1)}, u32[]{:S(2)}, u32[]{:S(2)}) collective-permute-start(f32[4,64,128]{2,1,0:T(8,128)S(1)} %pad_maximum_fusion.rest_0_), channel_id=1, source_target_pairs={{0,8},{1,9},{2,10},{3,11},{4,12},{5,13},{6,14},{7,15},{8,16},{9,17... | collective-permute-start | bytes 393224 | tf_op jit(solution)/shard_map/ppermute | solution.py:312
  18.9 2.1 %collective-permute-start.3 = (f32[4,64,128]{2,1,0:T(8,128)S(1)}, f32[4,64,128]{2,1,0:T(8,128)S(1)}, u32[]{:S(2)}, u32[]{:S(2)}) collective-permute-start(f32[4,64,128]{2,1,0:T(8,128)S(1)} %pad_maximum_fusion.rest_0_), channel_id=1, source_target_pairs={{0,12},{1,13},{2,14},{3,15},{4,16},{5,17},{6,18},{7,19},{8,20},{9,... | collective-permute-start | bytes 393224 | tf_op jit(solution)/shard_map/ppermute | solution.py:312
  21.0 0.0 all-to-all-done.coords_ref
  21.0 12.7 %factor.1 = (f32[576,128]{1,0:T(8,128)S(1)}, f32[64,128]{1,0:T(8,128)S(1)}) custom-call(s32[1]{0:T(128)} %bitcast.where_ref, s32[2,8]{1,0:T(2,128)S(1)} %copy-done.2, f32[32,8,128]{2,1,0:T(8,128)S(1)} %all-to-all-done.coords_ref), custom_call_target="tpu_custom_call" | custom-call | flops 14000000000 | bytes 100000 | tf_op jit(solution)/shard_map/factor/pallas_call | solution.py:356
  33.7 0.0 collective-permute-done.4.rest_2_
  33.7 0.0 collective-permute-done.3.rest_3_
  33.7 0.5 collective-permute-start.5
  34.3 1.3 %collective-permute-start.7 = (f32[4,64,128]{2,1,0:T(8,128)S(1)}, f32[4,64,128]{2,1,0:T(8,128)S(1)}, u32[]{:S(2)}, u32[]{:S(2)}) collective-permute-start(f32[4,64,128]{2,1,0:T(8,128)S(1)} %pad_maximum_fusion.rest_0_), channel_id=1, source_target_pairs={{0,16},{1,17},{2,18},{3,19},{4,20},{5,21},{6,22},{7,23},{8,24},{9,... | collective-permute-start | bytes 393224 | tf_op jit(solution)/shard_map/ppermute | solution.py:312
  35.6 2.4 %collective-permute-start.6 = (f32[4,64,128]{2,1,0:T(8,128)S(1)}, f32[4,64,128]{2,1,0:T(8,128)S(1)}, u32[]{:S(2)}, u32[]{:S(2)}) collective-permute-start(f32[4,64,128]{2,1,0:T(8,128)S(1)} %pad_maximum_fusion.rest_0_), channel_id=1, source_target_pairs={{0,4},{1,5},{2,6},{3,7},{4,8},{5,9},{6,10},{7,11},{8,12},{9,13},{1... | collective-permute-start | bytes 393224 | tf_op jit(solution)/shard_map/ppermute | solution.py:312
  37.9 1.2 %collective-permute-start.8 = (f32[576,128]{1,0:T(8,128)S(1)}, f32[576,128]{1,0:T(8,128)S(1)}, u32[]{:S(2)}, u32[]{:S(2)}) collective-permute-start(f32[576,128]{1,0:T(8,128)S(1)} %get-tuple-element.34.rest_5_), channel_id=1, source_target_pairs={{0,1},{1,0},{2,3},{3,2},{4,5},{5,4},{6,7},{7,6},{8,9},{9,8},{10,11... | collective-permute-start | bytes 884744 | tf_op jit(solution)/shard_map/ppermute | solution.py:317
  39.2 1.9 %collective-permute-done.7.rest_4_ = f32[4,64,128]{2,1,0:T(8,128)S(1)} collective-permute-done((f32[4,64,128]{2,1,0:T(8,128)S(1)}, f32[4,64,128]{2,1,0:T(8,128)S(1)}, u32[]{:S(2)}, u32[]{:S(2)}) %collective-permute-start.7) | collective-permute-done | bytes 131104 | tf_op jit(solution)/shard_map/ppermute | solution.py:312
  41.1 2.9 %collective-permute-done.6.rest_1_ = f32[4,64,128]{2,1,0:T(8,128)S(1)} collective-permute-done((f32[4,64,128]{2,1,0:T(8,128)S(1)}, f32[4,64,128]{2,1,0:T(8,128)S(1)}, u32[]{:S(2)}, u32[]{:S(2)}) %collective-permute-start.6) | collective-permute-done | bytes 131104 | tf_op jit(solution)/shard_map/ppermute | solution.py:312
  44.0 0.0 collective-permute-done.5.rest_7_
  44.0 2.1 %collective-permute-start.9 = (f32[576,128]{1,0:T(8,128)S(1)}, f32[576,128]{1,0:T(8,128)S(1)}, u32[]{:S(2)}, u32[]{:S(2)}) collective-permute-start(f32[576,128]{1,0:T(8,128)S(1)} %collective-permute-done.5.rest_7_), channel_id=1, source_target_pairs={{0,1},{1,0},{2,3},{3,2},{4,5},{5,4},{6,7},{7,6},{8,9},{9,8},{10,11... | collective-permute-start | bytes 884744 | tf_op jit(solution)/shard_map/ppermute | solution.py:317
  46.1 0.0 collective-permute-done.8.rest_6_
  46.1 1.2 %collective-permute-done.9.rest_8_ = f32[576,128]{1,0:T(8,128)S(1)} collective-permute-done((f32[576,128]{1,0:T(8,128)S(1)}, f32[576,128]{1,0:T(8,128)S(1)}, u32[]{:S(2)}, u32[]{:S(2)}) %collective-permute-start.9) | collective-permute-done | bytes 294944 | tf_op jit(solution)/shard_map/ppermute | solution.py:317
  47.3 2.6 %apply.1 = (f32[4,64,128]{2,1,0:T(8,128)S(1)}, f32[4,64,128]{2,1,0:T(8,128)S(1)}, f32[4,64,128]{2,1,0:T(8,128)S(1)}, f32[4,64,128]{2,1,0:T(8,128)S(1)}, f32[4,64,128]{2,1,0:T(8,128)S(1)}) custom-call(s32[1]{0:T(128)} %bitcast.where_ref, s32[4,2,8]{2,1,0:T(2,128)S(1)} %dynamic-slice_convert_fusion.ids_ref, f32[4,64,128]{2,1,0:T(8,128)S(1)} %pad_maximum_fusion.rest_0_, ...), custom_call_target="tpu_custom_call" | custom-call | flops 4000000000 | bytes 100000 | tf_op jit(solution)/shard_map/apply/pallas_call | solution.py:370
  49.9 1.9 %collective-permute-start.10 = (f32[4,64,128]{2,1,0:T(8,128)S(1)}, f32[4,64,128]{2,1,0:T(8,128)S(1)}, u32[]{:S(2)}, u32[]{:S(2)}) collective-permute-start(f32[4,64,128]{2,1,0:T(8,128)S(1)} %get-tuple-element.43), channel_id=1, source_target_pairs={{12,0},{13,1},{14,2},{15,3},{16,4},{17,5},{18,6},{19,7},{20,8},{21... | collective-permute-start | bytes 393224 | tf_op jit(solution)/shard_map/ppermute | solution.py:312
  51.8 1.9 %collective-permute-start.11 = (f32[4,64,128]{2,1,0:T(8,128)S(1)}, f32[4,64,128]{2,1,0:T(8,128)S(1)}, u32[]{:S(2)}, u32[]{:S(2)}) collective-permute-start(f32[4,64,128]{2,1,0:T(8,128)S(1)} %get-tuple-element.44), channel_id=1, source_target_pairs={{8,0},{9,1},{10,2},{11,3},{12,4},{13,5},{14,6},{15,7},{16,8},{17,9... | collective-permute-start | bytes 393224 | tf_op jit(solution)/shard_map/ppermute | solution.py:312
  53.7 1.3 %collective-permute-start.12 = (f32[4,64,128]{2,1,0:T(8,128)S(1)}, f32[4,64,128]{2,1,0:T(8,128)S(1)}, u32[]{:S(2)}, u32[]{:S(2)}) collective-permute-start(f32[4,64,128]{2,1,0:T(8,128)S(1)} %get-tuple-element.45), channel_id=1, source_target_pairs={{16,0},{17,1},{18,2},{19,3},{20,4},{21,5},{22,6},{23,7},{24,8},{25... | collective-permute-start | bytes 393224 | tf_op jit(solution)/shard_map/ppermute | solution.py:312
  55.0 4.4 %collective-permute-start.13 = (f32[4,64,128]{2,1,0:T(8,128)S(1)}, f32[4,64,128]{2,1,0:T(8,128)S(1)}, u32[]{:S(2)}, u32[]{:S(2)}) collective-permute-start(f32[4,64,128]{2,1,0:T(8,128)S(1)} %get-tuple-element.46), channel_id=1, source_target_pairs={{4,0},{5,1},{6,2},{7,3},{8,4},{9,5},{10,6},{11,7},{12,8},{13,9},{1... | collective-permute-start | bytes 393224 | tf_op jit(solution)/shard_map/ppermute | solution.py:312
  59.4 7.3 %logdet.1 = f32[8,128]{1,0:T(8,128)S(1)} custom-call(f32[64,128]{1,0:T(8,128)S(1)} %get-tuple-element.41.s_ref), custom_call_target="tpu_custom_call" | custom-call | flops 8999999488 | bytes 100000 | tf_op jit(solution)/shard_map/logdet/pallas_call | solution.py:378
  66.7 0.0 collective-permute-done.10.refs_1_
  66.7 0.0 collective-permute-done.11.refs_2_
  66.7 0.0 collective-permute-done.12.refs_3_
  66.7 0.0 collective-permute-done.13.refs_4_
  66.7 0.1 sum.1
  66.8 1.0 %collective-permute-start.14 = (f32[64,128]{1,0:T(8,128)S(1)}, f32[64,128]{1,0:T(8,128)S(1)}, u32[]{:S(2)}, u32[]{:S(2)}) collective-permute-start(f32[64,128]{1,0:T(8,128)S(1)} %get-tuple-element.48), channel_id=1, source_target_pairs={{0,1},{1,0},{2,3},{3,2},{4,5},{5,4},{6,7},{7,6},{8,9},{9,8},{10,11... | collective-permute-start | bytes 98312 | tf_op jit(solution)/shard_map/ppermute | solution.py:317
  67.8 0.7 collective-permute-start.15
  68.5 1.0 %collective-permute-start.16 = (f32[64,128]{1,0:T(8,128)S(1)}, f32[64,128]{1,0:T(8,128)S(1)}, u32[]{:S(2)}, u32[]{:S(2)}) collective-permute-start(f32[64,128]{1,0:T(8,128)S(1)} %get-tuple-element.50), channel_id=1, source_target_pairs={{0,3},{1,2},{2,1},{3,0},{4,7},{5,6},{6,5},{7,4},{8,11},{9,10},{10,... | collective-permute-start | bytes 98312 | tf_op jit(solution)/shard_map/ppermute | solution.py:317
  69.5 0.6 slice.3
  70.1 0.0 collective-permute-done.14.refs_1_
  70.1 0.5 collective-permute-done.15.refs_2_
  70.6 1.2 %collective-permute-done.16.refs_3_ = f32[64,128]{1,0:T(8,128)S(1)} collective-permute-done((f32[64,128]{1,0:T(8,128)S(1)}, f32[64,128]{1,0:T(8,128)S(1)}, u32[]{:S(2)}, u32[]{:S(2)}) %collective-permute-start.16) | collective-permute-done | bytes 32800 | tf_op jit(solution)/shard_map/ppermute | solution.py:317
  71.8 0.7 place.1
  (2 shorter events, 0.0 us)
Async XLA Ops:
  0.6 0.7 copy-start.2
  0.6 0.7 copy-start.1
  1.3 0.9 %copy-start = (f32[256,128]{1,0:T(8,128)S(1)}, f32[256,128]{1,0:T(8,128)}, u32[]{:S(2)}) copy-start(f32[256,128]{1,0:T(8,128)} %probes_ref.1) | copy-start | bytes 393220
  2.9 18.1 %all-to-all-start = ((f32[32,8,128]{2,1,0:T(8,128)}), f32[32,8,128]{2,1,0:T(8,128)S(1)}, u32[]{:S(2)}, u32[]{:S(2)}) async-start(f32[32,8,128]{2,1,0:T(8,128)} %get-tuple-element.27), calls=%async_computation | async-start | bytes 262144 | tf_op jit(solution)/shard_map/all_to_all | solution.py:353
  9.4 2.2 %collective-permute-start = (f32[64,128]{1,0:T(8,128)S(1)}, f32[64,128]{1,0:T(8,128)S(1)}, u32[]{:S(2)}, u32[]{:S(2)}) collective-permute-start(f32[64,128]{1,0:T(8,128)S(1)} %get-tuple-element.30), channel_id=1, source_target_pairs={{0,1},{1,0},{2,3},{3,2},{4,5},{5,4},{6,7},{7,6},{8,9},{9,8},{10,11... | collective-permute-start | bytes 98312 | tf_op jit(solution)/shard_map/ppermute | solution.py:317
  9.8 3.3 %collective-permute-start.1 = (f32[64,128]{1,0:T(8,128)S(1)}, f32[64,128]{1,0:T(8,128)S(1)}, u32[]{:S(2)}, u32[]{:S(2)}) collective-permute-start(f32[64,128]{1,0:T(8,128)S(1)} %get-tuple-element.31), channel_id=1, source_target_pairs={{0,2},{1,3},{2,0},{3,1},{4,6},{5,7},{6,4},{7,5},{8,10},{9,11},{10,... | collective-permute-start | bytes 98312 | tf_op jit(solution)/shard_map/ppermute | solution.py:317
  11.0 3.9 %collective-permute-start.2 = (f32[64,128]{1,0:T(8,128)S(1)}, f32[64,128]{1,0:T(8,128)S(1)}, u32[]{:S(2)}, u32[]{:S(2)}) collective-permute-start(f32[64,128]{1,0:T(8,128)S(1)} %get-tuple-element.32), channel_id=1, source_target_pairs={{0,3},{1,2},{2,1},{3,0},{4,7},{5,6},{6,5},{7,4},{8,11},{9,10},{10,... | collective-permute-start | bytes 98312 | tf_op jit(solution)/shard_map/ppermute | solution.py:317
  14.9 18.8 %collective-permute-start.4 = (f32[4,64,128]{2,1,0:T(8,128)S(1)}, f32[4,64,128]{2,1,0:T(8,128)S(1)}, u32[]{:S(2)}, u32[]{:S(2)}) collective-permute-start(f32[4,64,128]{2,1,0:T(8,128)S(1)} %pad_maximum_fusion.rest_0_), channel_id=1, source_target_pairs={{0,8},{1,9},{2,10},{3,11},{4,12},{5,13},{6,14},{7,15},{8,16},{9,17... | collective-permute-start | bytes 393224 | tf_op jit(solution)/shard_map/ppermute | solution.py:312
  18.9 14.8 %collective-permute-start.3 = (f32[4,64,128]{2,1,0:T(8,128)S(1)}, f32[4,64,128]{2,1,0:T(8,128)S(1)}, u32[]{:S(2)}, u32[]{:S(2)}) collective-permute-start(f32[4,64,128]{2,1,0:T(8,128)S(1)} %pad_maximum_fusion.rest_0_), channel_id=1, source_target_pairs={{0,12},{1,13},{2,14},{3,15},{4,16},{5,17},{6,18},{7,19},{8,20},{9,... | collective-permute-start | bytes 393224 | tf_op jit(solution)/shard_map/ppermute | solution.py:312
  33.7 10.2 %collective-permute-start.5 = (f32[576,128]{1,0:T(8,128)S(1)}, f32[576,128]{1,0:T(8,128)S(1)}, u32[]{:S(2)}, u32[]{:S(2)}) collective-permute-start(f32[576,128]{1,0:T(8,128)S(1)} %get-tuple-element.34.rest_5_), channel_id=1, source_target_pairs={{0,2},{1,3},{2,0},{3,1},{4,6},{5,7},{6,4},{7,5},{8,10},{9,11},{10,... | collective-permute-start | bytes 884744 | tf_op jit(solution)/shard_map/ppermute | solution.py:317
  34.3 6.8 %collective-permute-start.7 = (f32[4,64,128]{2,1,0:T(8,128)S(1)}, f32[4,64,128]{2,1,0:T(8,128)S(1)}, u32[]{:S(2)}, u32[]{:S(2)}) collective-permute-start(f32[4,64,128]{2,1,0:T(8,128)S(1)} %pad_maximum_fusion.rest_0_), channel_id=1, source_target_pairs={{0,16},{1,17},{2,18},{3,19},{4,20},{5,21},{6,22},{7,23},{8,24},{9,... | collective-permute-start | bytes 393224 | tf_op jit(solution)/shard_map/ppermute | solution.py:312
  35.6 8.4 %collective-permute-start.6 = (f32[4,64,128]{2,1,0:T(8,128)S(1)}, f32[4,64,128]{2,1,0:T(8,128)S(1)}, u32[]{:S(2)}, u32[]{:S(2)}) collective-permute-start(f32[4,64,128]{2,1,0:T(8,128)S(1)} %pad_maximum_fusion.rest_0_), channel_id=1, source_target_pairs={{0,4},{1,5},{2,6},{3,7},{4,8},{5,9},{6,10},{7,11},{8,12},{9,13},{1... | collective-permute-start | bytes 393224 | tf_op jit(solution)/shard_map/ppermute | solution.py:312
  37.9 8.1 %collective-permute-start.8 = (f32[576,128]{1,0:T(8,128)S(1)}, f32[576,128]{1,0:T(8,128)S(1)}, u32[]{:S(2)}, u32[]{:S(2)}) collective-permute-start(f32[576,128]{1,0:T(8,128)S(1)} %get-tuple-element.34.rest_5_), channel_id=1, source_target_pairs={{0,1},{1,0},{2,3},{3,2},{4,5},{5,4},{6,7},{7,6},{8,9},{9,8},{10,11... | collective-permute-start | bytes 884744 | tf_op jit(solution)/shard_map/ppermute | solution.py:317
  44.0 3.3 %collective-permute-start.9 = (f32[576,128]{1,0:T(8,128)S(1)}, f32[576,128]{1,0:T(8,128)S(1)}, u32[]{:S(2)}, u32[]{:S(2)}) collective-permute-start(f32[576,128]{1,0:T(8,128)S(1)} %collective-permute-done.5.rest_7_), channel_id=1, source_target_pairs={{0,1},{1,0},{2,3},{3,2},{4,5},{5,4},{6,7},{7,6},{8,9},{9,8},{10,11... | collective-permute-start | bytes 884744 | tf_op jit(solution)/shard_map/ppermute | solution.py:317
  49.9 16.8 %collective-permute-start.10 = (f32[4,64,128]{2,1,0:T(8,128)S(1)}, f32[4,64,128]{2,1,0:T(8,128)S(1)}, u32[]{:S(2)}, u32[]{:S(2)}) collective-permute-start(f32[4,64,128]{2,1,0:T(8,128)S(1)} %get-tuple-element.43), channel_id=1, source_target_pairs={{12,0},{13,1},{14,2},{15,3},{16,4},{17,5},{18,6},{19,7},{20,8},{21... | collective-permute-start | bytes 393224 | tf_op jit(solution)/shard_map/ppermute | solution.py:312
  51.8 14.9 %collective-permute-start.11 = (f32[4,64,128]{2,1,0:T(8,128)S(1)}, f32[4,64,128]{2,1,0:T(8,128)S(1)}, u32[]{:S(2)}, u32[]{:S(2)}) collective-permute-start(f32[4,64,128]{2,1,0:T(8,128)S(1)} %get-tuple-element.44), channel_id=1, source_target_pairs={{8,0},{9,1},{10,2},{11,3},{12,4},{13,5},{14,6},{15,7},{16,8},{17,9... | collective-permute-start | bytes 393224 | tf_op jit(solution)/shard_map/ppermute | solution.py:312
  53.7 13.0 %collective-permute-start.12 = (f32[4,64,128]{2,1,0:T(8,128)S(1)}, f32[4,64,128]{2,1,0:T(8,128)S(1)}, u32[]{:S(2)}, u32[]{:S(2)}) collective-permute-start(f32[4,64,128]{2,1,0:T(8,128)S(1)} %get-tuple-element.45), channel_id=1, source_target_pairs={{16,0},{17,1},{18,2},{19,3},{20,4},{21,5},{22,6},{23,7},{24,8},{25... | collective-permute-start | bytes 393224 | tf_op jit(solution)/shard_map/ppermute | solution.py:312
  55.0 11.7 %collective-permute-start.13 = (f32[4,64,128]{2,1,0:T(8,128)S(1)}, f32[4,64,128]{2,1,0:T(8,128)S(1)}, u32[]{:S(2)}, u32[]{:S(2)}) collective-permute-start(f32[4,64,128]{2,1,0:T(8,128)S(1)} %get-tuple-element.46), channel_id=1, source_target_pairs={{4,0},{5,1},{6,2},{7,3},{8,4},{9,5},{10,6},{11,7},{12,8},{13,9},{1... | collective-permute-start | bytes 393224 | tf_op jit(solution)/shard_map/ppermute | solution.py:312
  66.8 3.3 %collective-permute-start.14 = (f32[64,128]{1,0:T(8,128)S(1)}, f32[64,128]{1,0:T(8,128)S(1)}, u32[]{:S(2)}, u32[]{:S(2)}) collective-permute-start(f32[64,128]{1,0:T(8,128)S(1)} %get-tuple-element.48), channel_id=1, source_target_pairs={{0,1},{1,0},{2,3},{3,2},{4,5},{5,4},{6,7},{7,6},{8,9},{9,8},{10,11... | collective-permute-start | bytes 98312 | tf_op jit(solution)/shard_map/ppermute | solution.py:317
  67.8 2.8 %collective-permute-start.15 = (f32[64,128]{1,0:T(8,128)S(1)}, f32[64,128]{1,0:T(8,128)S(1)}, u32[]{:S(2)}, u32[]{:S(2)}) collective-permute-start(f32[64,128]{1,0:T(8,128)S(1)} %get-tuple-element.49), channel_id=1, source_target_pairs={{0,2},{1,3},{2,0},{3,1},{4,6},{5,7},{6,4},{7,5},{8,10},{9,11},{10,... | collective-permute-start | bytes 98312 | tf_op jit(solution)/shard_map/ppermute | solution.py:317
  68.5 3.3 %collective-permute-start.16 = (f32[64,128]{1,0:T(8,128)S(1)}, f32[64,128]{1,0:T(8,128)S(1)}, u32[]{:S(2)}, u32[]{:S(2)}) collective-permute-start(f32[64,128]{1,0:T(8,128)S(1)} %get-tuple-element.50), channel_id=1, source_target_pairs={{0,3},{1,2},{2,1},{3,0},{4,7},{5,6},{6,5},{7,4},{8,11},{9,10},{10,... | collective-permute-start | bytes 98312 | tf_op jit(solution)/shard_map/ppermute | solution.py:317

commit v6 on v5

--- a/solution.py
+++ b/solution.py
@@ -278,14 +278,9 @@
     out_ref[...] = jnp.broadcast_to(total * (1.0 / PTS), out_ref.shape)
 
 
-def prepare_kernel(where_ref, coords_ref, nb_ref, probes_ref, told_ref, *outs_and_scratch):
-    outs, scratch = outs_and_scratch[:-1], outs_and_scratch[-1]
+def prepare_kernel(where_ref, probes_ref, *outs):
     quarter = lax.rem(where_ref[0], SLAB)
     rows = outs[0].shape[0]
-    scratch[...] = jnp.zeros_like(scratch)
-    scratch[:2, :] = coords_ref[...]
-    scratch[2 : 2 + BLK, :NEIGH] = nb_ref[...].astype(F32)
-    told_ref[...] = jnp.broadcast_to(scratch[...][None], told_ref.shape)
     for k in range(SLAB):
         outs[k][...] = probes_ref[pl.ds(pl.multiple_of((quarter ^ k) * rows, rows), rows), :]
 
@@ -342,13 +337,11 @@
     tiles = jax.ShapeDtypeStruct((SLAB, quarter, WIDE), F32)
     square = jax.ShapeDtypeStruct((PTS, WIDE), F32)
 
-    told, *pieces = local(
-        prepare_kernel,
-        "prepare",
-        (jax.ShapeDtypeStruct((count, 8, WIDE), F32),) + (tile,) * SLAB,
-        [smem, vmem, vmem, vmem],
-        [pltpu.VMEM((8, WIDE), F32)],
-    )(here, coords, neighbours, probes)
+    told = jnp.pad(coords, ((0, 6), (0, 0))) + jnp.pad(
+        neighbours.astype(F32), ((2, 6 - BLK), (0, WIDE - NEIGH))
+    )
+    told = jnp.broadcast_to(told[None], (count, 8, WIDE))
+    pieces = local(prepare_kernel, "prepare", (tile,) * SLAB, [smem, vmem])(here, probes)
     own = jnp.stack([pieces[0]] + [swapped(pieces[k], k) for k in range(1, SLAB)])
     everywhere = lax.all_to_all(told, AXES, 0, 0)
     ids = lax.dynamic_slice(everywhere, (device // SLAB * SLAB, 2, 0), (SLAB, BLK, NEIGH)).astype(jnp.int32)

time: 72.8 us -> 72 us (0.989)
  local copies, waits for them, and re-layouts: 2.17 us -> 1.27 us
    unnamed x6, local copies, waits for them, and re-layouts: 1.58 us -> 0.01 us
where the time goes in v6:
time: 72 us; the launch traced here: 71.6 us
  starting transfers between devices  34.4 us (48%)
  Pallas kernels  23.3 us (32%)
  waiting for transfers between devices  11 us (15%)
  local copies, waits for them, and re-layouts  1.27 us (2%)
  between operations  0.83 us (1%)
    ppermute x8, starting transfers between devices, passed(): lax.ppermute(value, AXES, [(i, i + by) for i in range(size) if 0 <= i + b...  19.2 us
    pallas_call x1, Pallas kernels, shards(): local(factor_kernel, 'factor', (jax.ShapeDtypeStruct((COND + PTS, WIDE),...  12.7 us
    ppermute x9, starting transfers between devices, swapped(): return lax.ppermute(value, AXES, [(i, i ^ mask) for i in range(size)])  8.83 us
    pallas_call x1, Pallas kernels, shards(): local(logdet_kernel, 'logdet', jax.ShapeDtypeStruct((8, WIDE), F32), [vme...  7.31 us
    all_to_all x1, starting transfers between devices, shards(): everywhere = lax.all_to_all(told, AXES, 0, 0)  6.44 us
    ppermute x9, waiting for transfers between devices, swapped(): return lax.ppermute(value, AXES, [(i, i ^ mask) for i in range(size)])  6.24 us
    ppermute x8, waiting for transfers between devices, passed(): lax.ppermute(value, AXES, [(i, i + by) for i in range(size) if 0 <= i + b...  4.8 us
    pallas_call x1, Pallas kernels, shards(): local(apply_kernel, 'apply', (tiles,) * WINDOW, [smem, smem] + [vmem] * (...  2.6 us
  transfers between devices with their start and end apart: 18, of which 7 were waited for; matrix products, arithmetic and copies ran while one was open for 1% of the time, Pallas kernels for 28%

profile of v6, /device:TPU:3, one launch (start us, length us, event | category | flops | bytes accessed | tf_op | source)
XLA Modules:
  0.0 71.6 jit_solution(8971048703601693513)
XLA Ops:
  0.6 0.0 copy-start.2
  0.6 0.7 convert_element_type.10
  1.3 0.0 copy-done.2
  1.3 0.7 broadcast_in_dim.2
  2.0 0.0 copy-start.1
  2.0 6.4 %all-to-all-start = ((f32[32,8,128]{2,1,0:T(8,128)}), f32[32,8,128]{2,1,0:T(8,128)S(1)}, u32[]{:S(2)}, u32[]{:S(2)}) async-start(f32[32,8,128]{2,1,0:T(8,128)} %broadcast_in_dim.2), calls=%async_computation | async-start | bytes 262144 | tf_op jit(solution)/shard_map/all_to_all | solution.py:346
  8.5 0.0 copy-done.1
  8.5 0.4 collective-permute-start
  8.9 1.2 %collective-permute-start.1 = (f32[64,128]{1,0:T(8,128)S(1)}, f32[64,128]{1,0:T(8,128)S(1)}, u32[]{:S(2)}, u32[]{:S(2)}) collective-permute-start(f32[64,128]{1,0:T(8,128)S(1)} %get-tuple-element.29), channel_id=1, source_target_pairs={{0,2},{1,3},{2,0},{3,1},{4,6},{5,7},{6,4},{7,5},{8,10},{9,11},{10,... | collective-permute-start | bytes 98312 | tf_op jit(solution)/shard_map/ppermute | solution.py:312
  10.1 0.6 collective-permute-start.2
  10.7 0.0 collective-permute-done
  10.7 1.4 %collective-permute-done.1 = f32[64,128]{1,0:T(8,128)S(1)} collective-permute-done((f32[64,128]{1,0:T(8,128)S(1)}, f32[64,128]{1,0:T(8,128)S(1)}, u32[]{:S(2)}, u32[]{:S(2)}) %collective-permute-start.1) | collective-permute-done | bytes 32800 | tf_op jit(solution)/shard_map/ppermute | solution.py:312
  12.1 1.9 %collective-permute-done.2 = f32[64,128]{1,0:T(8,128)S(1)} collective-permute-done((f32[64,128]{1,0:T(8,128)S(1)}, f32[64,128]{1,0:T(8,128)S(1)}, u32[]{:S(2)}, u32[]{:S(2)}) %collective-permute-start.2) | collective-permute-done | bytes 32800 | tf_op jit(solution)/shard_map/ppermute | solution.py:312
  14.0 0.0 copy-start
  14.1 4.0 %collective-permute-start.4 = (f32[4,64,128]{2,1,0:T(8,128)S(1)}, f32[4,64,128]{2,1,0:T(8,128)S(1)}, u32[]{:S(2)}, u32[]{:S(2)}) collective-permute-start(f32[4,64,128]{2,1,0:T(8,128)S(1)} %pad_maximum_fusion.rest_0_), channel_id=1, source_target_pairs={{0,8},{1,9},{2,10},{3,11},{4,12},{5,13},{6,14},{7,15},{8,16},{9,17... | collective-permute-start | bytes 393224 | tf_op jit(solution)/shard_map/ppermute | solution.py:307
  18.1 2.0 %collective-permute-start.3 = (f32[4,64,128]{2,1,0:T(8,128)S(1)}, f32[4,64,128]{2,1,0:T(8,128)S(1)}, u32[]{:S(2)}, u32[]{:S(2)}) collective-permute-start(f32[4,64,128]{2,1,0:T(8,128)S(1)} %pad_maximum_fusion.rest_0_), channel_id=1, source_target_pairs={{0,12},{1,13},{2,14},{3,15},{4,16},{5,17},{6,18},{7,19},{8,20},{9,... | collective-permute-start | bytes 393224 | tf_op jit(solution)/shard_map/ppermute | solution.py:307
  20.1 0.0 all-to-all-done.coords_ref
  20.1 0.0 copy-done
  20.1 12.7 %factor.1 = (f32[576,128]{1,0:T(8,128)S(1)}, f32[64,128]{1,0:T(8,128)S(1)}) custom-call(s32[1]{0:T(128)} %bitcast.where_ref, s32[2,8]{1,0:T(2,128)S(1)} %copy-done, f32[32,8,128]{2,1,0:T(8,128)S(1)} %all-to-all-done.coords_ref), custom_call_target="tpu_custom_call" | custom-call | flops 14000000000 | bytes 100000 | tf_op jit(solution)/shard_map/factor/pallas_call | solution.py:349
  32.8 0.0 collective-permute-done.4.rest_2_
  32.8 0.0 collective-permute-done.3.rest_3_
  32.8 0.6 collective-permute-start.5
  33.4 1.3 %collective-permute-start.7 = (f32[4,64,128]{2,1,0:T(8,128)S(1)}, f32[4,64,128]{2,1,0:T(8,128)S(1)}, u32[]{:S(2)}, u32[]{:S(2)}) collective-permute-start(f32[4,64,128]{2,1,0:T(8,128)S(1)} %pad_maximum_fusion.rest_0_), channel_id=1, source_target_pairs={{0,16},{1,17},{2,18},{3,19},{4,20},{5,21},{6,22},{7,23},{8,24},{9,... | collective-permute-start | bytes 393224 | tf_op jit(solution)/shard_map/ppermute | solution.py:307
  34.7 2.4 %collective-permute-start.6 = (f32[4,64,128]{2,1,0:T(8,128)S(1)}, f32[4,64,128]{2,1,0:T(8,128)S(1)}, u32[]{:S(2)}, u32[]{:S(2)}) collective-permute-start(f32[4,64,128]{2,1,0:T(8,128)S(1)} %pad_maximum_fusion.rest_0_), channel_id=1, source_target_pairs={{0,4},{1,5},{2,6},{3,7},{4,8},{5,9},{6,10},{7,11},{8,12},{9,13},{1... | collective-permute-start | bytes 393224 | tf_op jit(solution)/shard_map/ppermute | solution.py:307
  37.1 1.2 %collective-permute-start.8 = (f32[576,128]{1,0:T(8,128)S(1)}, f32[576,128]{1,0:T(8,128)S(1)}, u32[]{:S(2)}, u32[]{:S(2)}) collective-permute-start(f32[576,128]{1,0:T(8,128)S(1)} %get-tuple-element.32.rest_5_), channel_id=1, source_target_pairs={{0,1},{1,0},{2,3},{3,2},{4,5},{5,4},{6,7},{7,6},{8,9},{9,8},{10,11... | collective-permute-start | bytes 884744 | tf_op jit(solution)/shard_map/ppermute | solution.py:312
  38.3 1.9 %collective-permute-done.7.rest_4_ = f32[4,64,128]{2,1,0:T(8,128)S(1)} collective-permute-done((f32[4,64,128]{2,1,0:T(8,128)S(1)}, f32[4,64,128]{2,1,0:T(8,128)S(1)}, u32[]{:S(2)}, u32[]{:S(2)}) %collective-permute-start.7) | collective-permute-done | bytes 131104 | tf_op jit(solution)/shard_map/ppermute | solution.py:307
  40.2 2.9 %collective-permute-done.6.rest_1_ = f32[4,64,128]{2,1,0:T(8,128)S(1)} collective-permute-done((f32[4,64,128]{2,1,0:T(8,128)S(1)}, f32[4,64,128]{2,1,0:T(8,128)S(1)}, u32[]{:S(2)}, u32[]{:S(2)}) %collective-permute-start.6) | collective-permute-done | bytes 131104 | tf_op jit(solution)/shard_map/ppermute | solution.py:307
  43.1 0.0 collective-permute-done.5.rest_7_
  43.1 2.1 %collective-permute-start.9 = (f32[576,128]{1,0:T(8,128)S(1)}, f32[576,128]{1,0:T(8,128)S(1)}, u32[]{:S(2)}, u32[]{:S(2)}) collective-permute-start(f32[576,128]{1,0:T(8,128)S(1)} %collective-permute-done.5.rest_7_), channel_id=1, source_target_pairs={{0,1},{1,0},{2,3},{3,2},{4,5},{5,4},{6,7},{7,6},{8,9},{9,8},{10,11... | collective-permute-start | bytes 884744 | tf_op jit(solution)/shard_map/ppermute | solution.py:312
  45.2 0.0 collective-permute-done.8.rest_6_
  45.2 1.2 %collective-permute-done.9.rest_8_ = f32[576,128]{1,0:T(8,128)S(1)} collective-permute-done((f32[576,128]{1,0:T(8,128)S(1)}, f32[576,128]{1,0:T(8,128)S(1)}, u32[]{:S(2)}, u32[]{:S(2)}) %collective-permute-start.9) | collective-permute-done | bytes 294944 | tf_op jit(solution)/shard_map/ppermute | solution.py:312
  46.4 2.6 %apply.1 = (f32[4,64,128]{2,1,0:T(8,128)S(1)}, f32[4,64,128]{2,1,0:T(8,128)S(1)}, f32[4,64,128]{2,1,0:T(8,128)S(1)}, f32[4,64,128]{2,1,0:T(8,128)S(1)}, f32[4,64,128]{2,1,0:T(8,128)S(1)}) custom-call(s32[1]{0:T(128)} %bitcast.where_ref, s32[4,2,8]{2,1,0:T(2,128)S(1)} %dynamic-slice_convert_fusion.ids_ref, f32[4,64,128]{2,1,0:T(8,128)S(1)} %pad_maximum_fusion.rest_0_, ...), custom_call_target="tpu_custom_call" | custom-call | flops 4000000000 | bytes 100000 | tf_op jit(solution)/shard_map/apply/pallas_call | solution.py:363
  49.0 1.9 %collective-permute-start.10 = (f32[4,64,128]{2,1,0:T(8,128)S(1)}, f32[4,64,128]{2,1,0:T(8,128)S(1)}, u32[]{:S(2)}, u32[]{:S(2)}) collective-permute-start(f32[4,64,128]{2,1,0:T(8,128)S(1)} %get-tuple-element.41), channel_id=1, source_target_pairs={{12,0},{13,1},{14,2},{15,3},{16,4},{17,5},{18,6},{19,7},{20,8},{21... | collective-permute-start | bytes 393224 | tf_op jit(solution)/shard_map/ppermute | solution.py:307
  50.9 1.9 %collective-permute-start.11 = (f32[4,64,128]{2,1,0:T(8,128)S(1)}, f32[4,64,128]{2,1,0:T(8,128)S(1)}, u32[]{:S(2)}, u32[]{:S(2)}) collective-permute-start(f32[4,64,128]{2,1,0:T(8,128)S(1)} %get-tuple-element.42), channel_id=1, source_target_pairs={{8,0},{9,1},{10,2},{11,3},{12,4},{13,5},{14,6},{15,7},{16,8},{17,9... | collective-permute-start | bytes 393224 | tf_op jit(solution)/shard_map/ppermute | solution.py:307
  52.9 1.3 %collective-permute-start.12 = (f32[4,64,128]{2,1,0:T(8,128)S(1)}, f32[4,64,128]{2,1,0:T(8,128)S(1)}, u32[]{:S(2)}, u32[]{:S(2)}) collective-permute-start(f32[4,64,128]{2,1,0:T(8,128)S(1)} %get-tuple-element.43), channel_id=1, source_target_pairs={{16,0},{17,1},{18,2},{19,3},{20,4},{21,5},{22,6},{23,7},{24,8},{25... | collective-permute-start | bytes 393224 | tf_op jit(solution)/shard_map/ppermute | solution.py:307
  54.2 4.4 %collective-permute-start.13 = (f32[4,64,128]{2,1,0:T(8,128)S(1)}, f32[4,64,128]{2,1,0:T(8,128)S(1)}, u32[]{:S(2)}, u32[]{:S(2)}) collective-permute-start(f32[4,64,128]{2,1,0:T(8,128)S(1)} %get-tuple-element.44), channel_id=1, source_target_pairs={{4,0},{5,1},{6,2},{7,3},{8,4},{9,5},{10,6},{11,7},{12,8},{13,9},{1... | collective-permute-start | bytes 393224 | tf_op jit(solution)/shard_map/ppermute | solution.py:307
  58.5 7.3 %logdet.1 = f32[8,128]{1,0:T(8,128)S(1)} custom-call(f32[64,128]{1,0:T(8,128)S(1)} %get-tuple-element.39.s_ref), custom_call_target="tpu_custom_call" | custom-call | flops 8999999488 | bytes 100000 | tf_op jit(solution)/shard_map/logdet/pallas_call | solution.py:371
  65.8 0.0 collective-permute-done.10.refs_1_
  65.8 0.0 collective-permute-done.11.refs_2_
  65.9 0.0 collective-permute-done.12.refs_3_
  65.9 0.0 collective-permute-done.13.refs_4_
  65.9 0.1 sum.1
  65.9 1.0 %collective-permute-start.14 = (f32[64,128]{1,0:T(8,128)S(1)}, f32[64,128]{1,0:T(8,128)S(1)}, u32[]{:S(2)}, u32[]{:S(2)}) collective-permute-start(f32[64,128]{1,0:T(8,128)S(1)} %get-tuple-element.46), channel_id=1, source_target_pairs={{0,1},{1,0},{2,3},{3,2},{4,5},{5,4},{6,7},{7,6},{8,9},{9,8},{10,11... | collective-permute-start | bytes 98312 | tf_op jit(solution)/shard_map/ppermute | solution.py:312
  66.9 0.7 collective-permute-start.15
  67.6 1.0 %collective-permute-start.16 = (f32[64,128]{1,0:T(8,128)S(1)}, f32[64,128]{1,0:T(8,128)S(1)}, u32[]{:S(2)}, u32[]{:S(2)}) collective-permute-start(f32[64,128]{1,0:T(8,128)S(1)} %get-tuple-element.48), channel_id=1, source_target_pairs={{0,3},{1,2},{2,1},{3,0},{4,7},{5,6},{6,5},{7,4},{8,11},{9,10},{10,... | collective-permute-start | bytes 98312 | tf_op jit(solution)/shard_map/ppermute | solution.py:312
  68.6 0.6 slice.3
  69.2 0.0 collective-permute-done.14.refs_1_
  69.2 0.5 collective-permute-done.15.refs_2_
  69.7 1.2 %collective-permute-done.16.refs_3_ = f32[64,128]{1,0:T(8,128)S(1)} collective-permute-done((f32[64,128]{1,0:T(8,128)S(1)}, f32[64,128]{1,0:T(8,128)S(1)}, u32[]{:S(2)}, u32[]{:S(2)}) %collective-permute-start.16) | collective-permute-done | bytes 32800 | tf_op jit(solution)/shard_map/ppermute | solution.py:312
  71.0 0.7 place.1
  (4 shorter events, 0.0 us)
Async XLA Ops:
  0.6 0.7 copy-start.2
  2.0 6.5 %copy-start.1 = (f32[256,128]{1,0:T(8,128)S(1)}, f32[256,128]{1,0:T(8,128)}, u32[]{:S(2)}) copy-start(f32[256,128]{1,0:T(8,128)} %probes_ref.1) | copy-start | bytes 393220
  2.0 18.1 %all-to-all-start = ((f32[32,8,128]{2,1,0:T(8,128)}), f32[32,8,128]{2,1,0:T(8,128)S(1)}, u32[]{:S(2)}, u32[]{:S(2)}) async-start(f32[32,8,128]{2,1,0:T(8,128)} %broadcast_in_dim.2), calls=%async_computation | async-start | bytes 262144 | tf_op jit(solution)/shard_map/all_to_all | solution.py:346
  8.5 2.2 %collective-permute-start = (f32[64,128]{1,0:T(8,128)S(1)}, f32[64,128]{1,0:T(8,128)S(1)}, u32[]{:S(2)}, u32[]{:S(2)}) collective-permute-start(f32[64,128]{1,0:T(8,128)S(1)} %get-tuple-element.28), channel_id=1, source_target_pairs={{0,1},{1,0},{2,3},{3,2},{4,5},{5,4},{6,7},{7,6},{8,9},{9,8},{10,11... | collective-permute-start | bytes 98312 | tf_op jit(solution)/shard_map/ppermute | solution.py:312
  8.9 3.2 %collective-permute-start.1 = (f32[64,128]{1,0:T(8,128)S(1)}, f32[64,128]{1,0:T(8,128)S(1)}, u32[]{:S(2)}, u32[]{:S(2)}) collective-permute-start(f32[64,128]{1,0:T(8,128)S(1)} %get-tuple-element.29), channel_id=1, source_target_pairs={{0,2},{1,3},{2,0},{3,1},{4,6},{5,7},{6,4},{7,5},{8,10},{9,11},{10,... | collective-permute-start | bytes 98312 | tf_op jit(solution)/shard_map/ppermute | solution.py:312
  10.1 3.9 %collective-permute-start.2 = (f32[64,128]{1,0:T(8,128)S(1)}, f32[64,128]{1,0:T(8,128)S(1)}, u32[]{:S(2)}, u32[]{:S(2)}) collective-permute-start(f32[64,128]{1,0:T(8,128)S(1)} %get-tuple-element.30), channel_id=1, source_target_pairs={{0,3},{1,2},{2,1},{3,0},{4,7},{5,6},{6,5},{7,4},{8,11},{9,10},{10,... | collective-permute-start | bytes 98312 | tf_op jit(solution)/shard_map/ppermute | solution.py:312
  14.0 6.1 %copy-start = (s32[2,8]{1,0:T(2,128)S(1)}, s32[2,8]{1,0:T(2,128)}, u32[]{:S(2)}) copy-start(s32[2,8]{1,0:T(2,128)} %nb_ref.1) | copy-start | bytes 196
  14.1 18.8 %collective-permute-start.4 = (f32[4,64,128]{2,1,0:T(8,128)S(1)}, f32[4,64,128]{2,1,0:T(8,128)S(1)}, u32[]{:S(2)}, u32[]{:S(2)}) collective-permute-start(f32[4,64,128]{2,1,0:T(8,128)S(1)} %pad_maximum_fusion.rest_0_), channel_id=1, source_target_pairs={{0,8},{1,9},{2,10},{3,11},{4,12},{5,13},{6,14},{7,15},{8,16},{9,17... | collective-permute-start | bytes 393224 | tf_op jit(solution)/shard_map/ppermute | solution.py:307
  18.1 14.7 %collective-permute-start.3 = (f32[4,64,128]{2,1,0:T(8,128)S(1)}, f32[4,64,128]{2,1,0:T(8,128)S(1)}, u32[]{:S(2)}, u32[]{:S(2)}) collective-permute-start(f32[4,64,128]{2,1,0:T(8,128)S(1)} %pad_maximum_fusion.rest_0_), channel_id=1, source_target_pairs={{0,12},{1,13},{2,14},{3,15},{4,16},{5,17},{6,18},{7,19},{8,20},{9,... | collective-permute-start | bytes 393224 | tf_op jit(solution)/shard_map/ppermute | solution.py:307
  32.8 10.3 %collective-permute-start.5 = (f32[576,128]{1,0:T(8,128)S(1)}, f32[576,128]{1,0:T(8,128)S(1)}, u32[]{:S(2)}, u32[]{:S(2)}) collective-permute-start(f32[576,128]{1,0:T(8,128)S(1)} %get-tuple-element.32.rest_5_), channel_id=1, source_target_pairs={{0,2},{1,3},{2,0},{3,1},{4,6},{5,7},{6,4},{7,5},{8,10},{9,11},{10,... | collective-permute-start | bytes 884744 | tf_op jit(solution)/shard_map/ppermute | solution.py:312
  33.4 6.8 %collective-permute-start.7 = (f32[4,64,128]{2,1,0:T(8,128)S(1)}, f32[4,64,128]{2,1,0:T(8,128)S(1)}, u32[]{:S(2)}, u32[]{:S(2)}) collective-permute-start(f32[4,64,128]{2,1,0:T(8,128)S(1)} %pad_maximum_fusion.rest_0_), channel_id=1, source_target_pairs={{0,16},{1,17},{2,18},{3,19},{4,20},{5,21},{6,22},{7,23},{8,24},{9,... | collective-permute-start | bytes 393224 | tf_op jit(solution)/shard_map/ppermute | solution.py:307
  34.7 8.4 %collective-permute-start.6 = (f32[4,64,128]{2,1,0:T(8,128)S(1)}, f32[4,64,128]{2,1,0:T(8,128)S(1)}, u32[]{:S(2)}, u32[]{:S(2)}) collective-permute-start(f32[4,64,128]{2,1,0:T(8,128)S(1)} %pad_maximum_fusion.rest_0_), channel_id=1, source_target_pairs={{0,4},{1,5},{2,6},{3,7},{4,8},{5,9},{6,10},{7,11},{8,12},{9,13},{1... | collective-permute-start | bytes 393224 | tf_op jit(solution)/shard_map/ppermute | solution.py:307
  37.1 8.1 %collective-permute-start.8 = (f32[576,128]{1,0:T(8,128)S(1)}, f32[576,128]{1,0:T(8,128)S(1)}, u32[]{:S(2)}, u32[]{:S(2)}) collective-permute-start(f32[576,128]{1,0:T(8,128)S(1)} %get-tuple-element.32.rest_5_), channel_id=1, source_target_pairs={{0,1},{1,0},{2,3},{3,2},{4,5},{5,4},{6,7},{7,6},{8,9},{9,8},{10,11... | collective-permute-start | bytes 884744 | tf_op jit(solution)/shard_map/ppermute | solution.py:312
  43.1 3.3 %collective-permute-start.9 = (f32[576,128]{1,0:T(8,128)S(1)}, f32[576,128]{1,0:T(8,128)S(1)}, u32[]{:S(2)}, u32[]{:S(2)}) collective-permute-start(f32[576,128]{1,0:T(8,128)S(1)} %collective-permute-done.5.rest_7_), channel_id=1, source_target_pairs={{0,1},{1,0},{2,3},{3,2},{4,5},{5,4},{6,7},{7,6},{8,9},{9,8},{10,11... | collective-permute-start | bytes 884744 | tf_op jit(solution)/shard_map/ppermute | solution.py:312
  49.0 16.8 %collective-permute-start.10 = (f32[4,64,128]{2,1,0:T(8,128)S(1)}, f32[4,64,128]{2,1,0:T(8,128)S(1)}, u32[]{:S(2)}, u32[]{:S(2)}) collective-permute-start(f32[4,64,128]{2,1,0:T(8,128)S(1)} %get-tuple-element.41), channel_id=1, source_target_pairs={{12,0},{13,1},{14,2},{15,3},{16,4},{17,5},{18,6},{19,7},{20,8},{21... | collective-permute-start | bytes 393224 | tf_op jit(solution)/shard_map/ppermute | solution.py:307
  50.9 14.9 %collective-permute-start.11 = (f32[4,64,128]{2,1,0:T(8,128)S(1)}, f32[4,64,128]{2,1,0:T(8,128)S(1)}, u32[]{:S(2)}, u32[]{:S(2)}) collective-permute-start(f32[4,64,128]{2,1,0:T(8,128)S(1)} %get-tuple-element.42), channel_id=1, source_target_pairs={{8,0},{9,1},{10,2},{11,3},{12,4},{13,5},{14,6},{15,7},{16,8},{17,9... | collective-permute-start | bytes 393224 | tf_op jit(solution)/shard_map/ppermute | solution.py:307
  52.9 13.0 %collective-permute-start.12 = (f32[4,64,128]{2,1,0:T(8,128)S(1)}, f32[4,64,128]{2,1,0:T(8,128)S(1)}, u32[]{:S(2)}, u32[]{:S(2)}) collective-permute-start(f32[4,64,128]{2,1,0:T(8,128)S(1)} %get-tuple-element.43), channel_id=1, source_target_pairs={{16,0},{17,1},{18,2},{19,3},{20,4},{21,5},{22,6},{23,7},{24,8},{25... | collective-permute-start | bytes 393224 | tf_op jit(solution)/shard_map/ppermute | solution.py:307
  54.2 11.7 %collective-permute-start.13 = (f32[4,64,128]{2,1,0:T(8,128)S(1)}, f32[4,64,128]{2,1,0:T(8,128)S(1)}, u32[]{:S(2)}, u32[]{:S(2)}) collective-permute-start(f32[4,64,128]{2,1,0:T(8,128)S(1)} %get-tuple-element.44), channel_id=1, source_target_pairs={{4,0},{5,1},{6,2},{7,3},{8,4},{9,5},{10,6},{11,7},{12,8},{13,9},{1... | collective-permute-start | bytes 393224 | tf_op jit(solution)/shard_map/ppermute | solution.py:307
  65.9 3.3 %collective-permute-start.14 = (f32[64,128]{1,0:T(8,128)S(1)}, f32[64,128]{1,0:T(8,128)S(1)}, u32[]{:S(2)}, u32[]{:S(2)}) collective-permute-start(f32[64,128]{1,0:T(8,128)S(1)} %get-tuple-element.46), channel_id=1, source_target_pairs={{0,1},{1,0},{2,3},{3,2},{4,5},{5,4},{6,7},{7,6},{8,9},{9,8},{10,11... | collective-permute-start | bytes 98312 | tf_op jit(solution)/shard_map/ppermute | solution.py:312
  66.9 2.8 %collective-permute-start.15 = (f32[64,128]{1,0:T(8,128)S(1)}, f32[64,128]{1,0:T(8,128)S(1)}, u32[]{:S(2)}, u32[]{:S(2)}) collective-permute-start(f32[64,128]{1,0:T(8,128)S(1)} %get-tuple-element.47), channel_id=1, source_target_pairs={{0,2},{1,3},{2,0},{3,1},{4,6},{5,7},{6,4},{7,5},{8,10},{9,11},{10,... | collective-permute-start | bytes 98312 | tf_op jit(solution)/shard_map/ppermute | solution.py:312
  67.6 3.3 %collective-permute-start.16 = (f32[64,128]{1,0:T(8,128)S(1)}, f32[64,128]{1,0:T(8,128)S(1)}, u32[]{:S(2)}, u32[]{:S(2)}) collective-permute-start(f32[64,128]{1,0:T(8,128)S(1)} %get-tuple-element.48), channel_id=1, source_target_pairs={{0,3},{1,2},{2,1},{3,0},{4,7},{5,6},{6,5},{7,4},{8,11},{9,10},{10,... | collective-permute-start | bytes 98312 | tf_op jit(solution)/shard_map/ppermute | solution.py:312

commit v7 on v6

--- a/solution.py
+++ b/solution.py
@@ -337,10 +337,10 @@
     tiles = jax.ShapeDtypeStruct((SLAB, quarter, WIDE), F32)
     square = jax.ShapeDtypeStruct((PTS, WIDE), F32)
 
-    told = jnp.pad(coords, ((0, 6), (0, 0))) + jnp.pad(
-        neighbours.astype(F32), ((2, 6 - BLK), (0, WIDE - NEIGH))
-    )
-    told = jnp.broadcast_to(told[None], (count, 8, WIDE))
+    told = jnp.pad(coords, ((0, BLK), (0, 0))) + jnp.pad(
+        neighbours.astype(F32), ((2, 0), (0, WIDE - NEIGH))
+    )
+    told = jnp.broadcast_to(told[None], (count, 2 + BLK, WIDE))
     pieces = local(prepare_kernel, "prepare", (tile,) * SLAB, [smem, vmem])(here, probes)
     own = jnp.stack([pieces[0]] + [swapped(pieces[k], k) for k in range(1, SLAB)])
     everywhere = lax.all_to_all(told, AXES, 0, 0)

time: 72 us -> 69 us (0.958)
  waiting for transfers between devices: 11 us -> 8.24 us
  local copies, waits for them, and re-layouts: 1.27 us -> 2.34 us
    ppermute x9, waiting for transfers between devices: 6.24 us -> 3.46 us  [swapped(): return lax.ppermute(value, AXES, [(i, i ^ mask) for i in range(size)])]
    unnamed x6, local copies, waits for them, and re-layouts: 0.01 us -> 1.11 us
    ppermute x9, starting transfers between devices: 8.83 us -> 9.82 us  [swapped(): return lax.ppermute(value, AXES, [(i, i ^ mask) for i in range(size)])]
    ppermute x8, starting transfers between devices: 19.2 us -> 18.3 us  [passed(): lax.ppermute(value, AXES, [(i, i + by) for i in range(size) if 0 <= i + b...]
    all_to_all x1, starting transfers between devices: 6.44 us -> 5.72 us  [shards(): everywhere = lax.all_to_all(told, AXES, 0, 0)]
  transfers between devices with their start and end apart: 18 -> 18, of which waited for: 7 -> 5; matrix products, arithmetic and copies ran while one was open for 1% -> 2% of each run, Pallas kernels for 28% -> 29%
where the time goes in v7:
time: 69 us; the launch traced here: 68.6 us
  starting transfers between devices  33.9 us (49%)
  Pallas kernels  23.3 us (34%)
  waiting for transfers between devices  8.24 us (12%)
  local copies, waits for them, and re-layouts  2.34 us (3%)
  between operations  0.84 us (1%)
    ppermute x8, starting transfers between devices, passed(): lax.ppermute(value, AXES, [(i, i + by) for i in range(size) if 0 <= i + b...  18.3 us
    pallas_call x1, Pallas kernels, shards(): local(factor_kernel, 'factor', (jax.ShapeDtypeStruct((COND + PTS, WIDE),...  12.7 us
    ppermute x9, starting transfers between devices, swapped(): return lax.ppermute(value, AXES, [(i, i ^ mask) for i in range(size)])  9.82 us
    pallas_call x1, Pallas kernels, shards(): local(logdet_kernel, 'logdet', jax.ShapeDtypeStruct((8, WIDE), F32), [vme...  7.31 us
    all_to_all x1, starting transfers between devices, shards(): everywhere = lax.all_to_all(told, AXES, 0, 0)  5.72 us
    ppermute x8, waiting for transfers between devices, passed(): lax.ppermute(value, AXES, [(i, i + by) for i in range(size) if 0 <= i + b...  4.78 us
    ppermute x9, waiting for transfers between devices, swapped(): return lax.ppermute(value, AXES, [(i, i ^ mask) for i in range(size)])  3.46 us
    pallas_call x1, Pallas kernels, shards(): local(apply_kernel, 'apply', (tiles,) * WINDOW, [smem, smem] + [vmem] * (...  2.6 us
  transfers between devices with their start and end apart: 18, of which 5 were waited for; matrix products, arithmetic and copies ran while one was open for 2% of the time, Pallas kernels for 29%

profile of v7, /device:TPU:3, one launch (start us, length us, event | category | flops | bytes accessed | tf_op | source)
XLA Modules:
  0.0 68.6 jit_solution(8190276307760876452)
XLA Ops:
  0.6 0.0 copy-start.1
  0.6 0.9 %copy-done.1 = f32[256,128]{1,0:T(8,128)S(1)} copy-done((f32[256,128]{1,0:T(8,128)S(1)}, f32[256,128]{1,0:T(8,128)}, u32[]{:S(2)}) %copy-start.1) | copy-done | bytes 131096
  1.6 0.7 %collective-permute-start = (f32[64,128]{1,0:T(8,128)S(1)}, f32[64,128]{1,0:T(8,128)S(1)}, u32[]{:S(2)}, u32[]{:S(2)}) collective-permute-start(f32[64,128]{1,0:T(8,128)S(1)} %get-tuple-element.28), channel_id=1, source_target_pairs={{0,1},{1,0},{2,3},{3,2},{4,5},{5,4},{6,7},{7,6},{8,9},{9,8},{10,11... | collective-permute-start | bytes 98312 | tf_op jit(solution)/shard_map/ppermute | solution.py:312
  2.3 0.0 copy-start
  2.3 1.3 %collective-permute-start.1 = (f32[64,128]{1,0:T(8,128)S(1)}, f32[64,128]{1,0:T(8,128)S(1)}, u32[]{:S(2)}, u32[]{:S(2)}) collective-permute-start(f32[64,128]{1,0:T(8,128)S(1)} %get-tuple-element.29), channel_id=1, source_target_pairs={{0,2},{1,3},{2,0},{3,1},{4,6},{5,7},{6,4},{7,5},{8,10},{9,11},{10,... | collective-permute-start | bytes 98312 | tf_op jit(solution)/shard_map/ppermute | solution.py:312
  3.6 0.0 copy-start.2
  3.6 0.5 collective-permute-start.2
  4.0 0.0 copy-done
  4.0 0.2 copy-done.2
  4.2 0.6 broadcast_in_dim.2
  4.9 5.7 %all-to-all-start = ((f32[32,4,128]{2,1,0:T(4,128)}), f32[32,4,128]{2,1,0:T(4,128)S(1)}, u32[]{:S(2)}, u32[]{:S(2)}) async-start(f32[32,4,128]{2,1,0:T(4,128)} %broadcast_in_dim.2), calls=%async_computation | async-start | bytes 131072 | tf_op jit(solution)/shard_map/all_to_all | solution.py:346
  10.6 0.0 collective-permute-done
  10.6 0.0 collective-permute-done.1
  10.6 0.0 collective-permute-done.2
  10.7 4.0 %collective-permute-start.4 = (f32[4,64,128]{2,1,0:T(8,128)S(1)}, f32[4,64,128]{2,1,0:T(8,128)S(1)}, u32[]{:S(2)}, u32[]{:S(2)}) collective-permute-start(f32[4,64,128]{2,1,0:T(8,128)S(1)} %pad_maximum_fusion.rest_0_), channel_id=1, source_target_pairs={{0,8},{1,9},{2,10},{3,11},{4,12},{5,13},{6,14},{7,15},{8,16},{9,17... | collective-permute-start | bytes 393224 | tf_op jit(solution)/shard_map/ppermute | solution.py:307
  14.7 2.3 %collective-permute-start.3 = (f32[4,64,128]{2,1,0:T(8,128)S(1)}, f32[4,64,128]{2,1,0:T(8,128)S(1)}, u32[]{:S(2)}, u32[]{:S(2)}) collective-permute-start(f32[4,64,128]{2,1,0:T(8,128)S(1)} %pad_maximum_fusion.rest_0_), channel_id=1, source_target_pairs={{0,12},{1,13},{2,14},{3,15},{4,16},{5,17},{6,18},{7,19},{8,20},{9,... | collective-permute-start | bytes 393224 | tf_op jit(solution)/shard_map/ppermute | solution.py:307
  16.9 0.0 all-to-all-done.coords_ref
  16.9 12.7 %factor.1 = (f32[576,128]{1,0:T(8,128)S(1)}, f32[64,128]{1,0:T(8,128)S(1)}) custom-call(s32[1]{0:T(128)} %bitcast.where_ref, s32[2,8]{1,0:T(2,128)S(1)} %copy-done, f32[32,4,128]{2,1,0:T(4,128)S(1)} %all-to-all-done.coords_ref), custom_call_target="tpu_custom_call" | custom-call | flops 14000000000 | bytes 100000 | tf_op jit(solution)/shard_map/factor/pallas_call | solution.py:349
  29.6 0.0 collective-permute-done.4.rest_2_
  29.7 0.0 collective-permute-done.3.rest_3_
  29.7 1.3 %collective-permute-start.5 = (f32[576,128]{1,0:T(8,128)S(1)}, f32[576,128]{1,0:T(8,128)S(1)}, u32[]{:S(2)}, u32[]{:S(2)}) collective-permute-start(f32[576,128]{1,0:T(8,128)S(1)} %get-tuple-element.32.rest_5_), channel_id=1, source_target_pairs={{0,2},{1,3},{2,0},{3,1},{4,6},{5,7},{6,4},{7,5},{8,10},{9,11},{10,... | collective-permute-start | bytes 884744 | tf_op jit(solution)/shard_map/ppermute | solution.py:312
  30.9 1.3 %collective-permute-start.7 = (f32[4,64,128]{2,1,0:T(8,128)S(1)}, f32[4,64,128]{2,1,0:T(8,128)S(1)}, u32[]{:S(2)}, u32[]{:S(2)}) collective-permute-start(f32[4,64,128]{2,1,0:T(8,128)S(1)} %pad_maximum_fusion.rest_0_), channel_id=1, source_target_pairs={{0,16},{1,17},{2,18},{3,19},{4,20},{5,21},{6,22},{7,23},{8,24},{9,... | collective-permute-start | bytes 393224 | tf_op jit(solution)/shard_map/ppermute | solution.py:307
  32.2 2.4 %collective-permute-start.6 = (f32[4,64,128]{2,1,0:T(8,128)S(1)}, f32[4,64,128]{2,1,0:T(8,128)S(1)}, u32[]{:S(2)}, u32[]{:S(2)}) collective-permute-start(f32[4,64,128]{2,1,0:T(8,128)S(1)} %pad_maximum_fusion.rest_0_), channel_id=1, source_target_pairs={{0,4},{1,5},{2,6},{3,7},{4,8},{5,9},{6,10},{7,11},{8,12},{9,13},{1... | collective-permute-start | bytes 393224 | tf_op jit(solution)/shard_map/ppermute | solution.py:307
  34.6 1.3 %collective-permute-start.8 = (f32[576,128]{1,0:T(8,128)S(1)}, f32[576,128]{1,0:T(8,128)S(1)}, u32[]{:S(2)}, u32[]{:S(2)}) collective-permute-start(f32[576,128]{1,0:T(8,128)S(1)} %get-tuple-element.32.rest_5_), channel_id=1, source_target_pairs={{0,1},{1,0},{2,3},{3,2},{4,5},{5,4},{6,7},{7,6},{8,9},{9,8},{10,11... | collective-permute-start | bytes 884744 | tf_op jit(solution)/shard_map/ppermute | solution.py:312
  35.9 1.1 %collective-permute-done.7.rest_4_ = f32[4,64,128]{2,1,0:T(8,128)S(1)} collective-permute-done((f32[4,64,128]{2,1,0:T(8,128)S(1)}, f32[4,64,128]{2,1,0:T(8,128)S(1)}, u32[]{:S(2)}, u32[]{:S(2)}) %collective-permute-start.7) | collective-permute-done | bytes 131104 | tf_op jit(solution)/shard_map/ppermute | solution.py:307
  36.9 3.7 %collective-permute-done.6.rest_1_ = f32[4,64,128]{2,1,0:T(8,128)S(1)} collective-permute-done((f32[4,64,128]{2,1,0:T(8,128)S(1)}, f32[4,64,128]{2,1,0:T(8,128)S(1)}, u32[]{:S(2)}, u32[]{:S(2)}) %collective-permute-start.6) | collective-permute-done | bytes 131104 | tf_op jit(solution)/shard_map/ppermute | solution.py:307
  40.6 0.0 collective-permute-done.5.rest_7_
  40.6 2.1 %collective-permute-start.9 = (f32[576,128]{1,0:T(8,128)S(1)}, f32[576,128]{1,0:T(8,128)S(1)}, u32[]{:S(2)}, u32[]{:S(2)}) collective-permute-start(f32[576,128]{1,0:T(8,128)S(1)} %collective-permute-done.5.rest_7_), channel_id=1, source_target_pairs={{0,1},{1,0},{2,3},{3,2},{4,5},{5,4},{6,7},{7,6},{8,9},{9,8},{10,11... | collective-permute-start | bytes 884744 | tf_op jit(solution)/shard_map/ppermute | solution.py:312
  42.8 0.0 collective-permute-done.8.rest_6_
  42.8 1.2 %collective-permute-done.9.rest_8_ = f32[576,128]{1,0:T(8,128)S(1)} collective-permute-done((f32[576,128]{1,0:T(8,128)S(1)}, f32[576,128]{1,0:T(8,128)S(1)}, u32[]{:S(2)}, u32[]{:S(2)}) %collective-permute-start.9) | collective-permute-done | bytes 294944 | tf_op jit(solution)/shard_map/ppermute | solution.py:312
  44.0 2.6 %apply.1 = (f32[4,64,128]{2,1,0:T(8,128)S(1)}, f32[4,64,128]{2,1,0:T(8,128)S(1)}, f32[4,64,128]{2,1,0:T(8,128)S(1)}, f32[4,64,128]{2,1,0:T(8,128)S(1)}, f32[4,64,128]{2,1,0:T(8,128)S(1)}) custom-call(s32[1]{0:T(128)} %bitcast.where_ref, s32[4,2,8]{2,1,0:T(2,128)S(1)} %dynamic-slice_convert_fusion.ids_ref, f32[4,64,128]{2,1,0:T(8,128)S(1)} %pad_maximum_fusion.rest_0_, ...), custom_call_target="tpu_custom_call" | custom-call | flops 4000000000 | bytes 100000 | tf_op jit(solution)/shard_map/apply/pallas_call | solution.py:363
  46.6 1.9 %collective-permute-start.10 = (f32[4,64,128]{2,1,0:T(8,128)S(1)}, f32[4,64,128]{2,1,0:T(8,128)S(1)}, u32[]{:S(2)}, u32[]{:S(2)}) collective-permute-start(f32[4,64,128]{2,1,0:T(8,128)S(1)} %get-tuple-element.41), channel_id=1, source_target_pairs={{12,0},{13,1},{14,2},{15,3},{16,4},{17,5},{18,6},{19,7},{20,8},{21... | collective-permute-start | bytes 393224 | tf_op jit(solution)/shard_map/ppermute | solution.py:307
  48.5 1.9 %collective-permute-start.11 = (f32[4,64,128]{2,1,0:T(8,128)S(1)}, f32[4,64,128]{2,1,0:T(8,128)S(1)}, u32[]{:S(2)}, u32[]{:S(2)}) collective-permute-start(f32[4,64,128]{2,1,0:T(8,128)S(1)} %get-tuple-element.42), channel_id=1, source_target_pairs={{8,0},{9,1},{10,2},{11,3},{12,4},{13,5},{14,6},{15,7},{16,8},{17,9... | collective-permute-start | bytes 393224 | tf_op jit(solution)/shard_map/ppermute | solution.py:307
  50.4 1.3 %collective-permute-start.12 = (f32[4,64,128]{2,1,0:T(8,128)S(1)}, f32[4,64,128]{2,1,0:T(8,128)S(1)}, u32[]{:S(2)}, u32[]{:S(2)}) collective-permute-start(f32[4,64,128]{2,1,0:T(8,128)S(1)} %get-tuple-element.43), channel_id=1, source_target_pairs={{16,0},{17,1},{18,2},{19,3},{20,4},{21,5},{22,6},{23,7},{24,8},{25... | collective-permute-start | bytes 393224 | tf_op jit(solution)/shard_map/ppermute | solution.py:307
  51.7 3.3 %collective-permute-start.13 = (f32[4,64,128]{2,1,0:T(8,128)S(1)}, f32[4,64,128]{2,1,0:T(8,128)S(1)}, u32[]{:S(2)}, u32[]{:S(2)}) collective-permute-start(f32[4,64,128]{2,1,0:T(8,128)S(1)} %get-tuple-element.44), channel_id=1, source_target_pairs={{4,0},{5,1},{6,2},{7,3},{8,4},{9,5},{10,6},{11,7},{12,8},{13,9},{1... | collective-permute-start | bytes 393224 | tf_op jit(solution)/shard_map/ppermute | solution.py:307
  55.0 7.3 %logdet.1 = f32[8,128]{1,0:T(8,128)S(1)} custom-call(f32[64,128]{1,0:T(8,128)S(1)} %get-tuple-element.39.s_ref), custom_call_target="tpu_custom_call" | custom-call | flops 8999999488 | bytes 100000 | tf_op jit(solution)/shard_map/logdet/pallas_call | solution.py:371
  62.3 0.0 collective-permute-done.10.refs_1_
  62.3 0.0 collective-permute-done.11.refs_2_
  62.4 0.0 collective-permute-done.12.refs_3_
  62.4 0.0 collective-permute-done.13.refs_4_
  62.4 0.1 sum.1
  62.4 1.0 %collective-permute-start.14 = (f32[64,128]{1,0:T(8,128)S(1)}, f32[64,128]{1,0:T(8,128)S(1)}, u32[]{:S(2)}, u32[]{:S(2)}) collective-permute-start(f32[64,128]{1,0:T(8,128)S(1)} %get-tuple-element.46), channel_id=1, source_target_pairs={{0,1},{1,0},{2,3},{3,2},{4,5},{5,4},{6,7},{7,6},{8,9},{9,8},{10,11... | collective-permute-start | bytes 98312 | tf_op jit(solution)/shard_map/ppermute | solution.py:312
  63.4 1.2 %collective-permute-start.15 = (f32[64,128]{1,0:T(8,128)S(1)}, f32[64,128]{1,0:T(8,128)S(1)}, u32[]{:S(2)}, u32[]{:S(2)}) collective-permute-start(f32[64,128]{1,0:T(8,128)S(1)} %get-tuple-element.47), channel_id=1, source_target_pairs={{0,2},{1,3},{2,0},{3,1},{4,6},{5,7},{6,4},{7,5},{8,10},{9,11},{10,... | collective-permute-start | bytes 98312 | tf_op jit(solution)/shard_map/ppermute | solution.py:312
  64.6 0.5 collective-permute-start.16
  65.1 0.6 slice.3
  65.7 0.0 collective-permute-done.14.refs_1_
  65.7 0.5 collective-permute-done.15.refs_2_
  66.2 1.8 %collective-permute-done.16.refs_3_ = f32[64,128]{1,0:T(8,128)S(1)} collective-permute-done((f32[64,128]{1,0:T(8,128)S(1)}, f32[64,128]{1,0:T(8,128)S(1)}, u32[]{:S(2)}, u32[]{:S(2)}) %collective-permute-start.16) | collective-permute-done | bytes 32800 | tf_op jit(solution)/shard_map/ppermute | solution.py:312
  68.0 0.7 place.1
  (5 shorter events, 0.0 us)
Async XLA Ops:
  0.6 0.9 %copy-start.1 = (f32[256,128]{1,0:T(8,128)S(1)}, f32[256,128]{1,0:T(8,128)}, u32[]{:S(2)}) copy-start(f32[256,128]{1,0:T(8,128)} %probes_ref.1) | copy-start | bytes 393220
  1.6 9.1 %collective-permute-start = (f32[64,128]{1,0:T(8,128)S(1)}, f32[64,128]{1,0:T(8,128)S(1)}, u32[]{:S(2)}, u32[]{:S(2)}) collective-permute-start(f32[64,128]{1,0:T(8,128)S(1)} %get-tuple-element.28), channel_id=1, source_target_pairs={{0,1},{1,0},{2,3},{3,2},{4,5},{5,4},{6,7},{7,6},{8,9},{9,8},{10,11... | collective-permute-start | bytes 98312 | tf_op jit(solution)/shard_map/ppermute | solution.py:312
  2.3 1.7 %copy-start = (s32[2,8]{1,0:T(2,128)S(1)}, s32[2,8]{1,0:T(2,128)}, u32[]{:S(2)}) copy-start(s32[2,8]{1,0:T(2,128)} %nb_ref.1) | copy-start | bytes 196
  2.3 8.3 %collective-permute-start.1 = (f32[64,128]{1,0:T(8,128)S(1)}, f32[64,128]{1,0:T(8,128)S(1)}, u32[]{:S(2)}, u32[]{:S(2)}) collective-permute-start(f32[64,128]{1,0:T(8,128)S(1)} %get-tuple-element.29), channel_id=1, source_target_pairs={{0,2},{1,3},{2,0},{3,1},{4,6},{5,7},{6,4},{7,5},{8,10},{9,11},{10,... | collective-permute-start | bytes 98312 | tf_op jit(solution)/shard_map/ppermute | solution.py:312
  3.6 0.7 copy-start.2
  3.6 7.1 %collective-permute-start.2 = (f32[64,128]{1,0:T(8,128)S(1)}, f32[64,128]{1,0:T(8,128)S(1)}, u32[]{:S(2)}, u32[]{:S(2)}) collective-permute-start(f32[64,128]{1,0:T(8,128)S(1)} %get-tuple-element.30), channel_id=1, source_target_pairs={{0,3},{1,2},{2,1},{3,0},{4,7},{5,6},{6,5},{7,4},{8,11},{9,10},{10,... | collective-permute-start | bytes 98312 | tf_op jit(solution)/shard_map/ppermute | solution.py:312
  4.9 12.0 %all-to-all-start = ((f32[32,4,128]{2,1,0:T(4,128)}), f32[32,4,128]{2,1,0:T(4,128)S(1)}, u32[]{:S(2)}, u32[]{:S(2)}) async-start(f32[32,4,128]{2,1,0:T(4,128)} %broadcast_in_dim.2), calls=%async_computation | async-start | bytes 131072 | tf_op jit(solution)/shard_map/all_to_all | solution.py:346
  10.7 19.0 %collective-permute-start.4 = (f32[4,64,128]{2,1,0:T(8,128)S(1)}, f32[4,64,128]{2,1,0:T(8,128)S(1)}, u32[]{:S(2)}, u32[]{:S(2)}) collective-permute-start(f32[4,64,128]{2,1,0:T(8,128)S(1)} %pad_maximum_fusion.rest_0_), channel_id=1, source_target_pairs={{0,8},{1,9},{2,10},{3,11},{4,12},{5,13},{6,14},{7,15},{8,16},{9,17... | collective-permute-start | bytes 393224 | tf_op jit(solution)/shard_map/ppermute | solution.py:307
  14.7 15.0 %collective-permute-start.3 = (f32[4,64,128]{2,1,0:T(8,128)S(1)}, f32[4,64,128]{2,1,0:T(8,128)S(1)}, u32[]{:S(2)}, u32[]{:S(2)}) collective-permute-start(f32[4,64,128]{2,1,0:T(8,128)S(1)} %pad_maximum_fusion.rest_0_), channel_id=1, source_target_pairs={{0,12},{1,13},{2,14},{3,15},{4,16},{5,17},{6,18},{7,19},{8,20},{9,... | collective-permute-start | bytes 393224 | tf_op jit(solution)/shard_map/ppermute | solution.py:307
  29.7 11.0 %collective-permute-start.5 = (f32[576,128]{1,0:T(8,128)S(1)}, f32[576,128]{1,0:T(8,128)S(1)}, u32[]{:S(2)}, u32[]{:S(2)}) collective-permute-start(f32[576,128]{1,0:T(8,128)S(1)} %get-tuple-element.32.rest_5_), channel_id=1, source_target_pairs={{0,2},{1,3},{2,0},{3,1},{4,6},{5,7},{6,4},{7,5},{8,10},{9,11},{10,... | collective-permute-start | bytes 884744 | tf_op jit(solution)/shard_map/ppermute | solution.py:312
  30.9 6.0 %collective-permute-start.7 = (f32[4,64,128]{2,1,0:T(8,128)S(1)}, f32[4,64,128]{2,1,0:T(8,128)S(1)}, u32[]{:S(2)}, u32[]{:S(2)}) collective-permute-start(f32[4,64,128]{2,1,0:T(8,128)S(1)} %pad_maximum_fusion.rest_0_), channel_id=1, source_target_pairs={{0,16},{1,17},{2,18},{3,19},{4,20},{5,21},{6,22},{7,23},{8,24},{9,... | collective-permute-start | bytes 393224 | tf_op jit(solution)/shard_map/ppermute | solution.py:307
  32.2 8.4 %collective-permute-start.6 = (f32[4,64,128]{2,1,0:T(8,128)S(1)}, f32[4,64,128]{2,1,0:T(8,128)S(1)}, u32[]{:S(2)}, u32[]{:S(2)}) collective-permute-start(f32[4,64,128]{2,1,0:T(8,128)S(1)} %pad_maximum_fusion.rest_0_), channel_id=1, source_target_pairs={{0,4},{1,5},{2,6},{3,7},{4,8},{5,9},{6,10},{7,11},{8,12},{9,13},{1... | collective-permute-start | bytes 393224 | tf_op jit(solution)/shard_map/ppermute | solution.py:307
  34.6 8.1 %collective-permute-start.8 = (f32[576,128]{1,0:T(8,128)S(1)}, f32[576,128]{1,0:T(8,128)S(1)}, u32[]{:S(2)}, u32[]{:S(2)}) collective-permute-start(f32[576,128]{1,0:T(8,128)S(1)} %get-tuple-element.32.rest_5_), channel_id=1, source_target_pairs={{0,1},{1,0},{2,3},{3,2},{4,5},{5,4},{6,7},{7,6},{8,9},{9,8},{10,11... | collective-permute-start | bytes 884744 | tf_op jit(solution)/shard_map/ppermute | solution.py:312
  40.6 3.3 %collective-permute-start.9 = (f32[576,128]{1,0:T(8,128)S(1)}, f32[576,128]{1,0:T(8,128)S(1)}, u32[]{:S(2)}, u32[]{:S(2)}) collective-permute-start(f32[576,128]{1,0:T(8,128)S(1)} %collective-permute-done.5.rest_7_), channel_id=1, source_target_pairs={{0,1},{1,0},{2,3},{3,2},{4,5},{5,4},{6,7},{7,6},{8,9},{9,8},{10,11... | collective-permute-start | bytes 884744 | tf_op jit(solution)/shard_map/ppermute | solution.py:312
  46.6 15.8 %collective-permute-start.10 = (f32[4,64,128]{2,1,0:T(8,128)S(1)}, f32[4,64,128]{2,1,0:T(8,128)S(1)}, u32[]{:S(2)}, u32[]{:S(2)}) collective-permute-start(f32[4,64,128]{2,1,0:T(8,128)S(1)} %get-tuple-element.41), channel_id=1, source_target_pairs={{12,0},{13,1},{14,2},{15,3},{16,4},{17,5},{18,6},{19,7},{20,8},{21... | collective-permute-start | bytes 393224 | tf_op jit(solution)/shard_map/ppermute | solution.py:307
  48.5 13.9 %collective-permute-start.11 = (f32[4,64,128]{2,1,0:T(8,128)S(1)}, f32[4,64,128]{2,1,0:T(8,128)S(1)}, u32[]{:S(2)}, u32[]{:S(2)}) collective-permute-start(f32[4,64,128]{2,1,0:T(8,128)S(1)} %get-tuple-element.42), channel_id=1, source_target_pairs={{8,0},{9,1},{10,2},{11,3},{12,4},{13,5},{14,6},{15,7},{16,8},{17,9... | collective-permute-start | bytes 393224 | tf_op jit(solution)/shard_map/ppermute | solution.py:307
  50.4 11.9 %collective-permute-start.12 = (f32[4,64,128]{2,1,0:T(8,128)S(1)}, f32[4,64,128]{2,1,0:T(8,128)S(1)}, u32[]{:S(2)}, u32[]{:S(2)}) collective-permute-start(f32[4,64,128]{2,1,0:T(8,128)S(1)} %get-tuple-element.43), channel_id=1, source_target_pairs={{16,0},{17,1},{18,2},{19,3},{20,4},{21,5},{22,6},{23,7},{24,8},{25... | collective-permute-start | bytes 393224 | tf_op jit(solution)/shard_map/ppermute | solution.py:307
  51.7 10.7 %collective-permute-start.13 = (f32[4,64,128]{2,1,0:T(8,128)S(1)}, f32[4,64,128]{2,1,0:T(8,128)S(1)}, u32[]{:S(2)}, u32[]{:S(2)}) collective-permute-start(f32[4,64,128]{2,1,0:T(8,128)S(1)} %get-tuple-element.44), channel_id=1, source_target_pairs={{4,0},{5,1},{6,2},{7,3},{8,4},{9,5},{10,6},{11,7},{12,8},{13,9},{1... | collective-permute-start | bytes 393224 | tf_op jit(solution)/shard_map/ppermute | solution.py:307
  62.4 3.3 %collective-permute-start.14 = (f32[64,128]{1,0:T(8,128)S(1)}, f32[64,128]{1,0:T(8,128)S(1)}, u32[]{:S(2)}, u32[]{:S(2)}) collective-permute-start(f32[64,128]{1,0:T(8,128)S(1)} %get-tuple-element.46), channel_id=1, source_target_pairs={{0,1},{1,0},{2,3},{3,2},{4,5},{5,4},{6,7},{7,6},{8,9},{9,8},{10,11... | collective-permute-start | bytes 98312 | tf_op jit(solution)/shard_map/ppermute | solution.py:312
  63.4 2.8 %collective-permute-start.15 = (f32[64,128]{1,0:T(8,128)S(1)}, f32[64,128]{1,0:T(8,128)S(1)}, u32[]{:S(2)}, u32[]{:S(2)}) collective-permute-start(f32[64,128]{1,0:T(8,128)S(1)} %get-tuple-element.47), channel_id=1, source_target_pairs={{0,2},{1,3},{2,0},{3,1},{4,6},{5,7},{6,4},{7,5},{8,10},{9,11},{10,... | collective-permute-start | bytes 98312 | tf_op jit(solution)/shard_map/ppermute | solution.py:312
  64.6 3.3 %collective-permute-start.16 = (f32[64,128]{1,0:T(8,128)S(1)}, f32[64,128]{1,0:T(8,128)S(1)}, u32[]{:S(2)}, u32[]{:S(2)}) collective-permute-start(f32[64,128]{1,0:T(8,128)S(1)} %get-tuple-element.48), channel_id=1, source_target_pairs={{0,3},{1,2},{2,1},{3,0},{4,7},{5,6},{6,5},{7,4},{8,11},{9,10},{10,... | collective-permute-start | bytes 98312 | tf_op jit(solution)/shard_map/ppermute | solution.py:312
